TPU v7x, 256 devices: a whole 4x4x8 slice. The times are simulated.
256 devices in a mesh: ty: 8 (over x, core), tx: 8 (over z), scan: 4 (over y).
Axes of the slice: x: 4, y: 4, z: 8, core: 2. Of those that a mesh axis runs over, the one named last changes fastest.
Arguments:
- specimen: float32 [2, 2, 2048, 2048], P(None, None, 'ty', 'tx'), may hold values from -1 to 1
- probe_modes: float32 [4, 2, 128, 128], replicated, may hold values from -3 to 3
- kernel_phase: float32 [128, 128], replicated, may hold values from -3.140625 to 3.140625
- offsets: int32 [8, 8, 8, 2], P('ty', 'tx', 'scan'), may hold values from -64 to 191, as said below
- live_counts: int32 [8, 8, 4], P('ty', 'tx', 'scan'), may hold values from 1 to 2, as said below
- measured: float32 [8, 8, 8, 128, 128], P('ty', 'tx', 'scan'), may hold values from 0 to 2
Outputs:
- object_grad: float32 [2, 2, 2048, 2048], P(None, None, 'ty', 'tx')
- probe_grad: float32 [4, 2, 128, 128], replicated
Inputs may be any that keep to these rules, and one draw needn't show every extreme that they name: `offsets`: every patch lies inside the object; a patch's top-left lies between -64 and 191 relative to its tile, so it reaches at most 64 pixels into neighbouring tiles. Slots at or beyond a device's live count carry positions too but add nothing. `live_counts`: number of live slots of each device; the live slots are the first ones.
All inputs are finite; a program needn't handle non-finite values.
Results may differ from a plain program's by a relative error of at most 0.00022.
Values sent between devices are 32-bit elements; how exact they have to be, the bound alone decides.
No kernel may reach another device: no remote copies, remote signals or barrier semaphores. Data moves between devices by JAX's collectives and lax.ppermute only.
A program may use at most 64 MiB of HBM per device.

v0:
```python
import jax
import jax.numpy as jnp
from jax import lax
from jax.sharding import PartitionSpec as P


def from_behind(value, axis, steps):
    count = lax.axis_size(axis)
    initial, last = (max(0, -steps), min(count, count - steps))
    return lax.ppermute(value, axis, [(source, source + steps) for source in range(initial, last)])


def extended(x, sides, width):
    for axis, dim in sides:
        devices, length = (lax.axis_size(axis), x.shape[dim])
        up = [(i, (i + 1) % devices) for i in range(devices - 1)]
        down = [(j, i) for i, j in up]
        last = lax.slice_in_dim(x, length - width, length, axis=dim)
        initial = lax.slice_in_dim(x, 0, width, axis=dim)
        before = lax.ppermute(last, axis, up)
        after = lax.ppermute(initial, axis, down)
        x = jnp.concatenate([before, x, after], axis=dim)
    return x


def apply_left(table, field):
    return jnp.einsum("jk,mkl->mjl", table, field, precision=lax.Precision.HIGHEST)


def apply_right(field, table):
    return jnp.einsum("mjl,lk->mjk", field, table, precision=lax.Precision.HIGHEST)


def transform(real_part, imag_part, cos_table, sin_table):
    left_real = apply_left(cos_table, real_part) - apply_left(sin_table, imag_part)
    left_imag = apply_left(cos_table, imag_part) + apply_left(sin_table, real_part)
    out_real = apply_right(left_real, cos_table) - apply_right(left_imag, sin_table)
    out_imag = apply_right(left_real, sin_table) + apply_right(left_imag, cos_table)
    return (out_real, out_imag)


def slot_loss(
    object_patch, probe_modes, recorded, weight_live, cos_table, sin_table, kernel_real, kernel_imag
):
    real_part = probe_modes[:, 0]
    imag_part = probe_modes[:, 1]
    layer_count = object_patch.shape[0]
    for layer in range(layer_count):
        layer_real = object_patch[layer, 0]
        layer_imag = object_patch[layer, 1]
        real_part, imag_part = (
            real_part * layer_real - imag_part * layer_imag,
            real_part * layer_imag + imag_part * layer_real,
        )
        if layer + 1 < layer_count:
            spec_real, spec_imag = transform(real_part, imag_part, cos_table, sin_table)
            spec_real, spec_imag = (
                spec_real * kernel_real - spec_imag * kernel_imag,
                spec_real * kernel_imag + spec_imag * kernel_real,
            )
            real_part, imag_part = transform(spec_real, spec_imag, cos_table, -sin_table)
    far_real, far_imag = transform(real_part, imag_part, cos_table, sin_table)
    intensity = jnp.sum(far_real * far_real + far_imag * far_imag, axis=0)
    return 0.5 * weight_live * jnp.sum((intensity - recorded) ** 2)


def pass_cols(rim_strip, direction):
    return from_behind(rim_strip, "tx", direction)


def pass_rows(rim_strip, direction):
    return from_behind(rim_strip, "ty", direction)


def fold_cols(grid, tile_size, margin):
    from_right = pass_cols(grid[..., :margin], -1)
    from_left = pass_cols(grid[..., tile_size + margin :], 1)
    grid = grid.at[..., tile_size : tile_size + margin].add(from_right)
    grid = grid.at[..., margin : 2 * margin].add(from_left)
    return grid[..., margin : margin + tile_size]


def fold_rows(grid, tile_size, margin):
    from_below = pass_rows(grid[..., :margin, :], -1)
    from_above = pass_rows(grid[..., tile_size + margin :, :], 1)
    grid = grid.at[..., tile_size : tile_size + margin, :].add(from_below)
    grid = grid.at[..., margin : 2 * margin, :].add(from_above)
    return grid[..., margin : margin + tile_size, :]


def per_device(specimen, probe_modes, kernel_phase, offsets, live_counts, measured):
    slice_count = specimen.shape[0]
    tile_size = specimen.shape[2]
    patch_size = probe_modes.shape[2]
    margin = patch_size // 2
    slot_count = offsets.shape[2]
    indices = jnp.arange(patch_size, dtype=jnp.int32)
    product = indices[:, None] * indices[None, :] % patch_size
    angles = product.astype(jnp.float32) * (2.0 * jnp.pi / patch_size)
    scale = 1.0 / jnp.sqrt(jnp.float32(patch_size))
    cos_table = jnp.cos(angles) * scale
    sin_table = -jnp.sin(angles) * scale
    kernel_real = jnp.cos(kernel_phase)
    kernel_imag = jnp.sin(kernel_phase)
    patterns = measured[0, 0]
    live_limit = live_counts[0, 0, 0]
    anchor = jnp.zeros((), jnp.int32)
    numbers = jnp.arange(slot_count, dtype=jnp.int32)

    def slot_gradient(object_patch, recorded, number):
        weight_live = (number < live_limit).astype(jnp.float32)

        def local_loss(patch_value, probe_value):
            return slot_loss(
                patch_value,
                probe_value,
                recorded,
                weight_live,
                cos_table,
                sin_table,
                kernel_real,
                kernel_imag,
            )

        _, pullback = jax.vjp(local_loss, object_patch, probe_modes)
        return pullback(jnp.float32(1.0))

    widened = extended(specimen, (("ty", 2), ("tx", 3)), margin)
    starts = offsets[0, 0] + margin

    def visit(carried, inputs):
        grad_wide, probe_total = carried
        corner, recorded, number = inputs
        object_patch = lax.dynamic_slice(
            widened,
            (anchor, anchor, corner[0], corner[1]),
            (slice_count, 2, patch_size, patch_size),
        )
        patch_grad, probe_part = slot_gradient(object_patch, recorded, number)
        current = lax.dynamic_slice(
            grad_wide,
            (anchor, anchor, corner[0], corner[1]),
            (slice_count, 2, patch_size, patch_size),
        )
        grad_wide = lax.dynamic_update_slice(
            grad_wide, current + patch_grad, (anchor, anchor, corner[0], corner[1])
        )
        return ((grad_wide, probe_total + probe_part), None)

    start = (jnp.zeros(widened.shape, jnp.float32), jnp.zeros(probe_modes.shape, jnp.float32))
    (grad_wide, probe_total), _ = lax.scan(visit, start, (starts, patterns, numbers))
    folded = fold_rows(fold_cols(grad_wide, tile_size, margin), tile_size, margin)
    object_grad = lax.psum(folded, "scan")
    probe_sum, live_total = lax.psum(
        (probe_total, live_limit.astype(jnp.float32)), ("ty", "tx", "scan")
    )
    return (object_grad, probe_sum / live_total)


def solution(mesh):
    placed = (
        P(None, None, "ty", "tx"),
        P(),
        P(),
        P("ty", "tx", "scan", None),
        P("ty", "tx", "scan"),
        P("ty", "tx", "scan", None, None),
    )
    return jax.shard_map(
        per_device,
        mesh=mesh,
        in_specs=placed,
        out_specs=(P(None, None, "ty", "tx"), P()),
        check_vma=False,
    )
```

profile of v0, /device:TPU:1, one launch (start us, length us, event | category | flops | bytes accessed | tf_op | source)
XLA Modules:
  0.0 508.9 jit_solution(17675557315514401191)
XLA Ops:
  7.2 1.6 copy.147
  9.9 4.6 collective-permute-start
  14.5 2.0 collective-permute-start.1
  17.8 3.2 collective-permute-done
  21.0 4.3 collective-permute-done.1
  25.6 3.9 collective-permute-start.2
  29.5 1.3 collective-permute-start.3
  31.0 3.1 collective-permute-done.2
  34.1 4.0 collective-permute-done.3
  38.1 2.0 pad_maximum_fusion
  40.2 1.6 broadcast_in_dim.13.clone
  41.7 121.1 %while.19 = (s32[]{:T(128)}, f32[2,2,384,384]{2,3,1,0:T(8,128)}, f32[4,2,128,128]{2,3,0,1:T(8,128)S(1)}, s32[2,2]{1,0:T(2,128)S(1)}, f32[4,2,128,128]{2,3,0,1:T(...) while((s32[]{:T(128)}, f32[2,2,384,384]{2,3,1,0:T(8,128)}, ...), condition=%wide.region_10.11_spmd.clone.clone, body=%wide.region_0.10_spmd.clone.clone.sunk | while | flops 4853284864 | bytes 49152364 | solution.py:151
  107.7 4.2 dynamic_update_slice.7
  155.2 4.4 dynamic_update_slice.7
  164.0 1.3 collective-permute-start.4
  165.3 4.3 collective-permute-start.5
  169.6 3.2 collective-permute-done.4
  172.8 1.8 add_dynamic-update-slice_fusion
  174.6 1.8 fusion.371
  176.4 2.5 fusion.373
  178.9 1.9 collective-permute-start.6
  183.1 11.3 %collective-permute-start.7 = (f32[2,2,64,256]{2,3,1,0:T(8,128)}, f32[2,2,64,256]{2,3,1,0:T(8,128)}, u32[]{:S(2)}, u32[]{:S(2)}) collective-permute-start(f32[2,2,64,256]{2,3,1,0:T(8,128)} %get-tuple-element.522), channel_id=1, source_target_pairs={{0,32},{32,64},{64,96},{96,128},{128,160},{160,192},{192,224},{1,3... | collective-permute-start | bytes 786440 | tf_op jit(solution)/shard_map/ppermute | solution.py:10
  194.4 2.8 collective-permute-done.6
  197.2 2.9 scatter-add.16
  200.8 1.4 slice_add_fusion
  202.2 4.1 scatter-add.19
  206.3 2.7 slice.225
  209.7 81.7 %psum.23 = f32[]{:T(128)} all-reduce(f32[]{:T(128)S(6)} %convert_element_type.102), channel_id=1, replica_groups=mesh['ty'=8,'tx'=8,'scan'=4] {'ty','tx','scan'}, use_global_device_ids=true, to_apply=%region_13.14 | all-reduce | flops 1 | bytes 8 | tf_op jit(solution)/shard_map/psum | solution.py:154
  291.4 155.3 %all-reduce.11.cloned.1.call-done = f32[4,2,128,128]{3,2,1,0:T(8,128)} async-done(((f32[4,2,128,128]{3,2,1,0:T(8,128)}), f32[4,2,128,128]{3,2,1,0:T(8,128)}) %all-reduce.11.cloned.1.call-update) | async-done | bytes 524304 | tf_op jit(solution)/shard_map/psum | solution.py:154
  446.7 2.6 broadcast_divide_fusion
  449.3 50.1 %all-reduce.9.cloned.1.call-done = f32[2,2,256,256]{2,3,1,0:T(8,128)} async-done(((f32[2,2,256,256]{2,3,1,0:T(8,128)}), f32[2,2,256,256]{2,3,1,0:T(8,128)}) %all-reduce.9.cloned.1.call-update) | async-done | bytes 1048592 | tf_op jit(solution)/shard_map/psum | solution.py:153
  499.4 2.5 copy.157
  (157 shorter events, 82.6 us)
Async XLA Ops:
  7.2 439.5 %all-reduce.11.cloned.1.call-start = ((), (), s32[]{:S(2)}) async-start(), calls=%async_computation.1 | async-start | bytes 1048576 | tf_op jit(solution)/shard_map/psum | solution.py:154
  9.9 20.9 %copy-start.3 = (s32[1,1,2,2]{3,2,1,0:T(2,128)S(1)}, s32[1,1,2,2]{3,2,1,0:T(2,128)}, u32[]{:S(2)}) copy-start(s32[1,1,2,2]{3,2,1,0:T(2,128)} %param.19) | copy-start | bytes 52
  9.9 20.9 %copy-start.2 = (f32[128,128]{1,0:T(8,128)S(1)}, f32[128,128]{1,0:T(8,128)}, u32[]{:S(2)}) copy-start(f32[128,128]{1,0:T(8,128)} %param.18) | copy-start | bytes 196612
  9.9 11.1 %collective-permute-start = (f32[2,2,64,256]{2,3,1,0:T(8,128)}, f32[2,2,64,256]{2,3,1,0:T(8,128)S(1)}, u32[]{:S(2)}, u32[]{:S(2)}) collective-permute-start(f32[2,2,64,256]{2,3,1,0:T(8,128)} %get-tuple-element.528), channel_id=1, source_target_pairs={{0,32},{32,64},{64,96},{96,128},{128,160},{160,192},{192,224},{1,3... | collective-permute-start | bytes 786440 | tf_op jit(solution)/shard_map/ppermute | solution.py:20
  14.5 10.7 %collective-permute-start.1 = (f32[2,2,64,256]{2,3,1,0:T(8,128)}, f32[2,2,64,256]{2,3,1,0:T(8,128)S(1)}, u32[]{:S(2)}, u32[]{:S(2)}) collective-permute-start(f32[2,2,64,256]{2,3,1,0:T(8,128)} %get-tuple-element.529), channel_id=1, source_target_pairs={{32,0},{64,32},{96,64},{128,96},{160,128},{192,160},{224,192},{33,... | collective-permute-start | bytes 786440 | tf_op jit(solution)/shard_map/ppermute | solution.py:21
  25.6 8.5 %collective-permute-start.2 = (f32[2,2,384,64]{2,3,1,0:T(8,128)S(1)}, f32[2,2,384,64]{2,3,1,0:T(8,128)S(1)}, u32[]{:S(2)}, u32[]{:S(2)}) collective-permute-start(f32[2,2,384,64]{2,3,1,0:T(8,128)S(1)} %get-tuple-element.526), channel_id=1, source_target_pairs={{0,4},{4,8},{8,12},{12,16},{16,20},{20,24},{24,28},{1,5},{5,9},{9,... | collective-permute-start | bytes 1179656 | tf_op jit(solution)/shard_map/ppermute | solution.py:20
  29.5 8.7 %collective-permute-start.3 = (f32[2,2,384,64]{2,3,1,0:T(8,128)S(1)}, f32[2,2,384,64]{2,3,1,0:T(8,128)S(1)}, u32[]{:S(2)}, u32[]{:S(2)}) collective-permute-start(f32[2,2,384,64]{2,3,1,0:T(8,128)S(1)} %get-tuple-element.527), channel_id=1, source_target_pairs={{4,0},{8,4},{12,8},{16,12},{20,16},{24,20},{28,24},{5,1},{9,5},{13... | collective-permute-start | bytes 1179656 | tf_op jit(solution)/shard_map/ppermute | solution.py:21
  40.2 1.6 copy-start.1
  164.0 8.8 %collective-permute-start.4 = (f32[2,2,384,64]{2,3,1,0:T(8,128)S(1)}, f32[2,2,384,64]{2,3,1,0:T(8,128)S(1)}, u32[]{:S(2)}, u32[]{:S(2)}) collective-permute-start(f32[2,2,384,64]{2,3,1,0:T(8,128)S(1)} %get-tuple-element.525), channel_id=1, source_target_pairs={{4,0},{8,4},{12,8},{16,12},{20,16},{24,20},{28,24},{5,1},{9,5},{13... | collective-permute-start | bytes 1179656 | tf_op jit(solution)/shard_map/ppermute | solution.py:10
  165.3 9.3 %collective-permute-start.5 = (f32[2,2,384,64]{2,3,1,0:T(8,128)S(1)}, f32[2,2,384,64]{2,3,1,0:T(8,128)S(1)}, u32[]{:S(2)}, u32[]{:S(2)}) collective-permute-start(f32[2,2,384,64]{2,3,1,0:T(8,128)S(1)} %get-tuple-element.524), channel_id=1, source_target_pairs={{0,4},{4,8},{8,12},{12,16},{16,20},{20,24},{24,28},{1,5},{5,9},{9,... | collective-permute-start | bytes 1179656 | tf_op jit(solution)/shard_map/ppermute | solution.py:10
  176.4 5.5 %copy-start = (f32[2,2,384,384]{2,3,1,0:T(8,128)S(1)}, f32[2,2,384,384]{2,3,1,0:T(8,128)}, u32[]{:S(2)}) copy-start(f32[2,2,384,384]{2,3,1,0:T(8,128)} %fusion.371) | copy-start | bytes 7077892
  178.9 18.3 %collective-permute-start.6 = (f32[2,2,64,256]{2,3,1,0:T(8,128)}, f32[2,2,64,256]{2,3,1,0:T(8,128)S(1)}, u32[]{:S(2)}, u32[]{:S(2)}) collective-permute-start(f32[2,2,64,256]{2,3,1,0:T(8,128)} %get-tuple-element.523), channel_id=1, source_target_pairs={{32,0},{64,32},{96,64},{128,96},{160,128},{192,160},{224,192},{33,... | collective-permute-start | bytes 786440 | tf_op jit(solution)/shard_map/ppermute | solution.py:10
  181.8 317.6 %all-reduce.9.cloned.1.call-start = ((), (), s32[]{:S(2)}) async-start(), calls=%async_computation | async-start | bytes 2097152 | tf_op jit(solution)/shard_map/psum | solution.py:153
  183.1 17.7 %collective-permute-start.7 = (f32[2,2,64,256]{2,3,1,0:T(8,128)}, f32[2,2,64,256]{2,3,1,0:T(8,128)}, u32[]{:S(2)}, u32[]{:S(2)}) collective-permute-start(f32[2,2,64,256]{2,3,1,0:T(8,128)} %get-tuple-element.522), channel_id=1, source_target_pairs={{0,32},{32,64},{64,96},{96,128},{128,160},{160,192},{192,224},{1,3... | collective-permute-start | bytes 786440 | tf_op jit(solution)/shard_map/ppermute | solution.py:10
Sparse Core Ops, SparseCore 0:
  181.9 264.7 all-reduce.10
  449.6 49.6 all-reduce.8
where the time goes:
time: 513 us; the launch traced here: 509 us
  waiting for transfers between devices  227 us (44%)
  blocking collectives  81.7 us (16%)
  matrix products  65.9 us (13%)
  local copies, waits for them, and re-layouts  41.3 us (8%)
  loops' own time  37.2 us (7%)
  starting transfers between devices  30.6 us (6%)
  between operations  15 us (3%)
  other arithmetic  10.5 us (2%)
    psum x1, waiting for transfers between devices, per_device(): lax.psum((probe_total, live_limit.astype(jnp.float32)), ('ty', 'tx', 'sca...  155 us
    psum x1, blocking collectives, per_device(): lax.psum((probe_total, live_limit.astype(jnp.float32)), ('ty', 'tx', 'sca...  81.7 us
    psum x1, waiting for transfers between devices, per_device(): object_grad = lax.psum(folded, 'scan')  50.1 us
    another operation x1, loops' own time, per_device(): lax.scan(visit, start, (starts, patterns, numbers))  37.2 us
    dot_general x48, matrix products, apply_left(): jnp.einsum('jk,mkl->mjl', table, field, precision=lax.Precision.HIGHEST)  33.6 us
    dot_general x48, matrix products, apply_right(): jnp.einsum('mjl,lk->mjk', field, table, precision=lax.Precision.HIGHEST)  32.3 us
    ppermute x4, starting transfers between devices, from_behind(): lax.ppermute(value, axis, [(source, source + steps) for source in range(i...  18.7 us
  transfers between devices with their start and end apart: 10, of which 9 were waited for; matrix products, arithmetic and copies ran while one was open for 4% of the time, Pallas kernels for 0%

commit v1 on v0

v1 whole, which is shorter than its diff:
```python
import functools

import jax
import jax.numpy as jnp
import numpy as np
from jax import lax
from jax.experimental import pallas as pl
from jax.experimental.pallas import tpu as pltpu
from jax.sharding import Mesh
from jax.sharding import PartitionSpec as P

F32 = jnp.float32
BF16 = jnp.bfloat16
VMEM = pl.BlockSpec(memory_space=pltpu.VMEM)
SMEM = pl.BlockSpec(memory_space=pltpu.SMEM)
PARAMS = pltpu.CompilerParams(vmem_limit_bytes=48 * 1024 * 1024)
W = 128
HALF = 64
TILE = 256
MODES = 4


def call(body, outs, args, specs, scratch=(), name=None):
    return pl.pallas_call(
        body,
        out_shape=[jax.ShapeDtypeStruct(shape, F32) for shape in outs],
        in_specs=specs,
        out_specs=[VMEM] * len(outs),
        scratch_shapes=list(scratch),
        compiler_params=PARAMS,
        name=name,
    )(*args)


def low_lanes(rows):
    return lax.broadcasted_iota(jnp.int32, (rows, W), 1) < HALF


def swap(x):
    return pltpu.roll(x, HALF, 1)


def pack_body(meta, tile, to_left, to_right, to_core, to_far, core_left, core_right, far_left, far_right):
    core = meta[0]
    core_row = pl.multiple_of((1 - core) * (TILE - HALF), HALF)
    far_row = pl.multiple_of(core * (TILE - HALF), HALF)
    wide = low_lanes(W)
    short = low_lanes(HALF // 2)
    for part in range(4):
        first, second = tile[part, :W, :W], tile[part, W:, :W]
        to_left[part] = jnp.where(wide, first, swap(second))
        first, second = tile[part, :W, W:], tile[part, W:, W:]
        to_right[part] = jnp.where(wide, swap(first), second)
        for row, strip, left, right in (
            (core_row, to_core, core_left, core_right),
            (far_row, to_far, far_left, far_right),
        ):
            rows = tile[part, pl.ds(row, HALF), :]
            strip[part] = rows
            upper, lower = rows[: HALF // 2], rows[HALF // 2 :]
            left[part] = jnp.where(short, upper[:, :W], swap(lower[:, :W]))
            right[part] = jnp.where(short, swap(upper[:, W:]), lower[:, W:])


def halves(x):
    high = x.astype(BF16)
    return high, (x - high.astype(F32)).astype(BF16)


def times_right(real, imag, table):
    high, low = halves(
        jnp.concatenate([jnp.concatenate([r, i], axis=1) for r, i in zip(real, imag)], axis=0)
    )
    out = jnp.dot(jnp.concatenate([high, low, high], axis=1), table, preferred_element_type=F32)
    blocks = [out[W * m : W * (m + 1)] for m in range(len(real))]
    return [b[:, :W] for b in blocks], [b[:, W:] for b in blocks]


def times_left(table, real, imag):
    high, low = halves(
        jnp.concatenate([jnp.concatenate(real, axis=1), jnp.concatenate(imag, axis=1)], axis=0)
    )
    out = jnp.dot(table, jnp.concatenate([high, low, high], axis=0), preferred_element_type=F32)
    cols = [out[:, W * m : W * (m + 1)] for m in range(len(real))]
    return [c[:W] for c in cols], [c[W:] for c in cols]


def slots_body(
    meta,
    tile,
    from_right,
    from_left,
    from_core,
    from_far,
    core_right,
    core_left,
    far_right,
    far_left,
    probe,
    kernel_real,
    kernel_imag,
    measured,
    right_high,
    right_low,
    left_high,
    left_low,
    out0,
    out1,
    out2,
    out3,
    probe_send,
    probe_keep,
    wide,
    grads,
    probe_sum,
    mid,
    patches,
):
    core, scan, live = meta[0], meta[1], meta[2]
    core_row = pl.multiple_of((1 - core) * (TILE + HALF), HALF)
    far_row = pl.multiple_of(core * (TILE + HALF), HALF)
    tall = low_lanes(W)
    short = low_lanes(HALF // 2)
    for part in range(4):
        wide[part, 0, HALF : HALF + TILE] = tile[part, :, :W]
        wide[part, 1, HALF : HALF + TILE] = tile[part, :, W:]
        right, left = from_right[part], from_left[part]
        wide[part, 2, HALF : HALF + W] = jnp.where(tall, right, swap(left))
        wide[part, 2, HALF + W : HALF + TILE] = jnp.where(tall, swap(right), left)
        for row, strip, corner_right, corner_left in (
            (core_row, from_core, core_right, core_left),
            (far_row, from_far, far_right, far_left),
        ):
            wide[part, 0, pl.ds(row, HALF)] = strip[part, :, :W]
            wide[part, 1, pl.ds(row, HALF)] = strip[part, :, W:]
            right, left = corner_right[part], corner_left[part]
            wide[part, 2, pl.ds(row, HALF // 2)] = jnp.where(short, right, swap(left))
            lower = pl.multiple_of(row + HALF // 2, HALF // 2)
            wide[part, 2, pl.ds(lower, HALF // 2)] = jnp.where(short, swap(right), left)

    forward_right = jnp.concatenate([right_high[...], right_high[...], right_low[...]], axis=0)
    inverse_right = jnp.concatenate([left_high[...], left_high[...], left_low[...]], axis=0)
    forward_left = jnp.concatenate([left_high[...], left_high[...], left_low[...]], axis=1)
    inverse_left = jnp.concatenate([right_high[...], right_high[...], right_low[...]], axis=1)

    def transform(real, imag):
        return times_left(forward_left, *times_right(real, imag, forward_right))

    def untransform(real, imag):
        return times_right(*times_left(inverse_left, real, imag), inverse_right)

    modes = range(MODES)
    lanes = lax.broadcasted_iota(jnp.int32, (W, W), 1)

    def visit(slot, carried):
        row = meta[3 + 2 * slot]
        col = meta[4 + 2 * slot]
        block = col // W
        shift = col - block * W
        after = jnp.where(block == 2, 0, block + 1)
        turn = jnp.where(shift == 0, 0, W - shift)
        for part in range(4):
            one = pltpu.roll(wide[part, block, pl.ds(row, W)], turn, 1)
            two = pltpu.roll(wide[part, after, pl.ds(row, W)], turn, 1)
            patches[part] = jnp.where(lanes < W - shift, one, two)
        near_real, near_imag = patches[0], patches[1]
        real = [probe[2 * m] * near_real - probe[2 * m + 1] * near_imag for m in modes]
        imag = [probe[2 * m] * near_imag + probe[2 * m + 1] * near_real for m in modes]
        real, imag = transform(real, imag)
        kr, ki = kernel_real[...], kernel_imag[...]
        real, imag = (
            [r * kr - i * ki for r, i in zip(real, imag)],
            [r * ki + i * kr for r, i in zip(real, imag)],
        )
        real, imag = untransform(real, imag)
        for m in modes:
            mid[2 * m] = real[m]
            mid[2 * m + 1] = imag[m]
        away_real, away_imag = patches[2], patches[3]
        real, imag = (
            [r * away_real - i * away_imag for r, i in zip(real, imag)],
            [r * away_imag + i * away_real for r, i in zip(real, imag)],
        )
        real, imag = transform(real, imag)
        intensity = functools.reduce(jnp.add, [r * r + i * i for r, i in zip(real, imag)])
        weight = jnp.where(slot < live, 2.0, 0.0).astype(F32)
        residual = (intensity - measured[slot]) * weight
        real, imag = untransform([r * residual for r in real], [i * residual for i in imag])
        grads[2, slot] = functools.reduce(
            jnp.add, [mid[2 * m] * real[m] + mid[2 * m + 1] * imag[m] for m in modes]
        )
        grads[3, slot] = functools.reduce(
            jnp.add, [mid[2 * m] * imag[m] - mid[2 * m + 1] * real[m] for m in modes]
        )
        real, imag = (
            [r * away_real + i * away_imag for r, i in zip(real, imag)],
            [i * away_real - r * away_imag for r, i in zip(real, imag)],
        )
        real, imag = transform(real, imag)
        real, imag = (
            [r * kr + i * ki for r, i in zip(real, imag)],
            [i * kr - r * ki for r, i in zip(real, imag)],
        )
        real, imag = untransform(real, imag)
        grads[0, slot] = functools.reduce(
            jnp.add, [probe[2 * m] * real[m] + probe[2 * m + 1] * imag[m] for m in modes]
        )
        grads[1, slot] = functools.reduce(
            jnp.add, [probe[2 * m] * imag[m] - probe[2 * m + 1] * real[m] for m in modes]
        )
        for m in modes:
            probe_sum[2 * m] += real[m] * near_real + imag[m] * near_imag
            probe_sum[2 * m + 1] += imag[m] * near_real - real[m] * near_imag
        return carried

    probe_sum[...] = jnp.zeros_like(probe_sum)
    lax.fori_loop(0, 2, visit, 0)

    places = lax.broadcasted_iota(jnp.int32, (8, W), 0)
    marks = jnp.zeros((8, W), F32)
    for k in range(4):
        marks = jnp.where(places == k, meta[3 + k].astype(F32), marks)
    for step, out in enumerate((out0, out1, out2, out3)):
        part = lax.rem(scan + step, 4)
        for slot in range(2):
            out[W * slot : W * (slot + 1)] = grads[part, slot]
        out[2 * W :] = marks
    count = jnp.zeros((8, W), F32) + live.astype(F32)
    for half, out in ((core, probe_keep), (1 - core, probe_send)):
        for k in range(MODES):
            out[W * k : W * (k + 1)] = probe_sum[half * MODES + k]
        out[MODES * W :] = count


def spread_body(keep, got, out):
    rows = out.shape[1] - 8
    count = keep[MODES * W :] + got[MODES * W :]
    for k in range(out.shape[0]):
        span = slice(k * rows, (k + 1) * rows)
        out[k, :rows] = keep[span] + got[span]
        out[k, rows:] = count


def place_body(one, two, three, four, chunks, to_left, to_right, keep, spread, wide):
    total = chunks[0]
    for k in range(1, chunks.shape[0]):
        total = total + chunks[k]
    for k in range(spread.shape[0]):
        spread[k] = total
    wide[...] = jnp.zeros_like(wide)
    lanes = lax.broadcasted_iota(jnp.int32, (W, W), 1)
    for message in (one, two, three, four):
        for slot in range(2):
            base = 2 * W + 2 * slot
            row = jnp.max(message[base : base + 1]).astype(jnp.int32)
            col = jnp.max(message[base + 1 : base + 2]).astype(jnp.int32)
            row = jnp.clip(row, 0, TILE)
            col = jnp.clip(col, 0, 3 * W - 1)
            block = col // W
            shift = col - block * W
            after = jnp.where(block == 2, 0, block + 1)
            turned = pltpu.roll(message[W * slot : W * (slot + 1)], shift, 1)
            wide[block, pl.ds(row, W)] += jnp.where(lanes >= shift, turned, 0.0)
            wide[after, pl.ds(row, W)] += jnp.where(lanes < shift, turned, 0.0)
    half = (TILE + 2 * HALF) // 2
    low = low_lanes(half)
    upper, lower = wide[2, :half], wide[2, half:]
    to_right[...] = jnp.where(low, upper, swap(lower))
    to_left[...] = jnp.where(low, swap(upper), lower)
    keep[0] = wide[0]
    keep[1] = wide[1]


def rows_body(meta, from_left, from_right, held, chunks, to_core, to_far, keep, spread, wide):
    total = chunks[0]
    for k in range(1, chunks.shape[0]):
        total = total + chunks[k]
    rows = spread.shape[1]
    mean = total[:rows] / total[rows : rows + 1]
    for k in range(spread.shape[0]):
        spread[k] = mean
    core = meta[0]
    half = (TILE + 2 * HALF) // 2
    low = low_lanes(half)
    left, right = from_left[...], from_right[...]
    wide[0, :half] = held[0, :half] + jnp.where(low, left, 0.0)
    wide[0, half:] = held[0, half:] + jnp.where(low, swap(left), 0.0)
    wide[1, :half] = held[1, :half] + jnp.where(low, 0.0, swap(right))
    wide[1, half:] = held[1, half:] + jnp.where(low, 0.0, right)
    core_row = pl.multiple_of((1 - core) * (TILE + HALF), HALF)
    far_row = pl.multiple_of(core * (TILE + HALF), HALF)
    for k in range(2):
        to_core[k] = wide[k, pl.ds(core_row, HALF)]
        to_far[k] = wide[k, pl.ds(far_row, HALF)]
        keep[k] = wide[k, HALF : HALF + TILE]


def finish_body(meta, from_core, from_far, held, out):
    core = meta[0]
    core_row = pl.multiple_of((1 - core) * (TILE - HALF), HALF)
    far_row = pl.multiple_of(core * (TILE - HALF), HALF)
    for k in range(2):
        span = slice(k * W, (k + 1) * W)
        out[:, span] = held[k]
        out[pl.ds(core_row, HALF), span] += from_core[k]
        out[pl.ds(far_row, HALF), span] += from_far[k]


def gather_body(meta, one, two, three, four, out):
    scan = meta[1]
    for step, part in enumerate((one, two, three, four)):
        out[lax.rem(scan + 4 - step, 4)] = part[...]


def halves_body(meta, mine, other, out):
    core = meta[0]
    out[core] = mine[...]
    out[1 - core] = other[...]


def tables():
    index = np.arange(W)
    angle = 2.0 * np.pi * ((index[:, None] * index[None, :]) % W) / W
    cos, sin = np.cos(angle) / np.sqrt(W), -np.sin(angle) / np.sqrt(W)
    right = np.block([[cos, sin], [-sin, cos]])
    arrays = []
    for table in (right, right.T):
        high = table.astype(BF16)
        low = (table - high.astype(np.float64)).astype(BF16)
        arrays += [high, low]
    return [jnp.asarray(a) for a in arrays]


def per_device(sizes, specimen, probe_modes, kernel_phase, offsets, live_counts, measured):
    nx, ntx, nsc = sizes
    core = lax.axis_index("core")
    scan = lax.axis_index("scan")
    starts = offsets[0, 0]
    rows = jnp.clip(starts[:, 0] + HALF, 0, TILE)
    cols = jnp.clip(starts[:, 1], -HALF, TILE - HALF)
    cols = jnp.where(cols < 0, cols + 3 * W, cols)
    meta = jnp.stack(
        [core, scan, live_counts[0, 0, 0], rows[0], cols[0], rows[1], cols[1]]
    ).astype(jnp.int32)

    def over_grid(target):
        pairs = []
        for x in range(nx):
            for c in range(2):
                for t in range(ntx):
                    x2, c2, t2 = target(x, c, t)
                    pairs.append(((x * 2 + c) * ntx + t, ((x2 % nx) * 2 + c2) * ntx + t2 % ntx))
        return lambda value: lax.ppermute(value, ("x", "core", "tx"), pairs)

    def across(x, c):
        return x + (1 if c else -1), 1 - c

    to_left = over_grid(lambda x, c, t: (x, c, t - 1))
    to_right = over_grid(lambda x, c, t: (x, c, t + 1))
    to_core = over_grid(lambda x, c, t: (x, 1 - c, t))
    to_far = over_grid(lambda x, c, t: (*across(x, c), t))
    core_left = over_grid(lambda x, c, t: (x, 1 - c, t - 1))
    core_right = over_grid(lambda x, c, t: (x, 1 - c, t + 1))
    far_left = over_grid(lambda x, c, t: (*across(x, c), t - 1))
    far_right = over_grid(lambda x, c, t: (*across(x, c), t + 1))

    def to_scan(value, step):
        return lax.ppermute(value, "scan", [(s, (s + step) % nsc) for s in range(nsc)])

    tile = specimen.reshape(4, TILE, TILE)
    edge, strip, corner = (4, W, W), (4, HALF, TILE), (4, HALF // 2, W)
    sent = call(
        pack_body,
        [edge, edge, strip, strip, corner, corner, corner, corner],
        (meta, tile),
        [SMEM, VMEM],
        name="pack",
    )
    moves = (to_left, to_right, to_core, to_far, core_left, core_right, far_left, far_right)
    rim = [move(value) for move, value in zip(moves, sent)]
    message = (2 * W + 8, W)
    share = (MODES * W + 8, W)
    outs = call(
        slots_body,
        [message] * 4 + [share] * 2,
        (
            meta,
            tile,
            *rim,
            probe_modes.reshape(2 * MODES, W, W),
            jnp.cos(kernel_phase),
            jnp.sin(kernel_phase),
            measured[0, 0],
            *tables(),
        ),
        [SMEM] + [VMEM] * 17,
        scratch=[
            pltpu.VMEM((4, 3, TILE + 2 * HALF, W), F32),
            pltpu.VMEM((4, 2, W, W), F32),
            pltpu.VMEM((2 * MODES, W, W), F32),
            pltpu.VMEM((2 * MODES, W, W), F32),
            pltpu.VMEM((4, W, W), F32),
        ],
        name="slots",
    )
    own, away, probe_send, probe_keep = outs[0], outs[1:4], outs[4], outs[5]
    probe_got = to_core(probe_send)
    arrived = [to_scan(value, step) for step, value in enumerate(away, 1)]
    group = nx * nsc
    rows_each = MODES * W // group
    (chunks,) = call(
        spread_body, [(group, rows_each + 8, W)], (probe_keep, probe_got), [VMEM] * 2, name="spread"
    )
    chunks = lax.all_to_all(chunks, ("x", "scan"), 0, 0)
    tall = TILE + 2 * HALF
    left, right, held, spread = call(
        place_body,
        [(tall // 2, W)] * 2 + [(2, tall, W), (ntx, rows_each + 8, W)],
        (own, *arrived, chunks),
        [VMEM] * 5,
        scratch=[pltpu.VMEM((3, tall, W), F32)],
        name="place",
    )
    left, right = to_left(left), to_right(right)
    spread = lax.all_to_all(spread, "tx", 0, 0)
    near, far, held, spread = call(
        rows_body,
        [(2, HALF, W)] * 2 + [(2, TILE, W), (group, rows_each, W)],
        (meta, right, left, held, spread),
        [SMEM] + [VMEM] * 4,
        scratch=[pltpu.VMEM((2, tall, W), F32)],
        name="rows",
    )
    near, far = to_core(near), to_far(far)
    mine = lax.all_to_all(spread, ("x", "scan"), 0, 0).reshape(MODES * W, W)
    (quarter,) = call(
        finish_body, [(TILE, TILE)], (meta, near, far, held), [SMEM] + [VMEM] * 3, name="finish"
    )
    quarters = [quarter] + [to_scan(quarter, step) for step in range(1, nsc)]
    other = to_core(mine)
    (probe_grad,) = call(
        halves_body, [(2, MODES * W, W)], (meta, mine, other), [SMEM] + [VMEM] * 2, name="halves"
    )
    (object_grad,) = call(
        gather_body, [(4, TILE, TILE)], (meta, *quarters), [SMEM] + [VMEM] * 4, name="gather"
    )
    return object_grad.reshape(specimen.shape), probe_grad.reshape(probe_modes.shape)


def solution(mesh):
    ny, ntx, nsc = mesh.devices.shape
    split = Mesh(mesh.devices.reshape(ny // 2, 2, ntx, nsc), ("x", "core", "tx", "scan"))
    rows = ("x", "core")
    placed = (
        P(None, None, rows, "tx"),
        P(),
        P(),
        P(rows, "tx", "scan", None),
        P(rows, "tx", "scan"),
        P(rows, "tx", "scan", None, None),
    )
    return jax.shard_map(
        functools.partial(per_device, (ny // 2, ntx, nsc)),
        mesh=split,
        in_specs=placed,
        out_specs=(P(None, None, rows, "tx"), P()),
        check_vma=False,
    )
```

time: 513 us -> 113 us (0.22)
  waiting for transfers between devices: 227 us -> 36.8 us
  blocking collectives: 81.7 us -> 0 us
  matrix products: 65.9 us -> 0 us
  loops' own time: 37.2 us -> 0 us
  local copies, waits for them, and re-layouts: 41.3 us -> 6.71 us
  Pallas kernels: 0 us -> 18.5 us
  starting transfers between devices: 30.6 us -> 48.6 us
  between operations: 15 us -> 1.45 us
  other arithmetic: 10.5 us -> 0.19 us
    psum x2 -> x0, waiting for transfers between devices: 205 us -> none  [the longest x1 155 us: per_device(): lax.psum((probe_total, live_limit.astype(jnp.float32)), ('ty', 'tx', 'sca...]
    psum x1 -> x0, blocking collectives: 81.7 us -> none  [per_device(): lax.psum((probe_total, live_limit.astype(jnp.float32)), ('ty', 'tx', 'sca...]
    dot_general x96 -> x0, matrix products: 65.9 us -> none  [the longest x48 33.6 us: apply_left(): jnp.einsum('jk,mkl->mjl', table, field, precision=lax.Precision.HIGHEST)]
    another operation x1 -> x0, loops' own time: 37.2 us -> none  [per_device(): lax.scan(visit, start, (starts, patterns, numbers))]
    pallas_call x0 -> x8, Pallas kernels: none -> 18.5 us  [call(): pl.pallas_call(body, out_shape=[jax.ShapeDtypeStruct(shape, F32) for shap...]
    all_to_all x0 -> x3, starting transfers between devices: none -> 15.4 us  [the longest x1 6.13 us: per_device(): chunks = lax.all_to_all(chunks, ('x', 'scan'), 0, 0)]
    ppermute x8 -> x20, waiting for transfers between devices: 21.3 us -> 36.3 us  [the longest x6 20.5 us: to_scan(): lax.ppermute(value, 'scan', [(s, (s + step) % nsc) for s in range(nsc)])]
    slice x9 -> x2, local copies, waits for them, and re-layouts: 12.5 us -> 1.17 us  [the longest x1 0.59 us: per_device(): cols[1]]
  transfers between devices with their start and end apart: 10 -> 23, of which waited for: 9 -> 11; matrix products, arithmetic and copies ran while one was open for 4% -> 1% of each run, Pallas kernels for 0% -> 2%
where the time goes in v1:
time: 113 us; the launch traced here: 112 us
  starting transfers between devices  48.6 us (43%)
  waiting for transfers between devices  36.8 us (33%)
  Pallas kernels  18.5 us (16%)
  local copies, waits for them, and re-layouts  6.71 us (6%)
  between operations  1.45 us (1%)
    ppermute x14, starting transfers between devices, over_grid(): return lambda value: lax.ppermute(value, ('x', 'core', 'tx'), pairs)  24.7 us
    ppermute x6, waiting for transfers between devices, to_scan(): lax.ppermute(value, 'scan', [(s, (s + step) % nsc) for s in range(nsc)])  20.5 us
    pallas_call x8, Pallas kernels, call(): pl.pallas_call(body, out_shape=[jax.ShapeDtypeStruct(shape, F32) for shap...  18.5 us
    ppermute x14, waiting for transfers between devices, over_grid(): return lambda value: lax.ppermute(value, ('x', 'core', 'tx'), pairs)  15.8 us
    ppermute x6, starting transfers between devices, to_scan(): lax.ppermute(value, 'scan', [(s, (s + step) % nsc) for s in range(nsc)])  8.57 us
    all_to_all x1, starting transfers between devices, per_device(): chunks = lax.all_to_all(chunks, ('x', 'scan'), 0, 0)  6.13 us
    all_to_all x1, starting transfers between devices, per_device(): mine = lax.all_to_all(spread, ('x', 'scan'), 0, 0).reshape(MODES * W, W)  5.85 us
    all_to_all x1, starting transfers between devices, per_device(): spread = lax.all_to_all(spread, 'tx', 0, 0)  3.38 us
  transfers between devices with their start and end apart: 23, of which 11 were waited for; matrix products, arithmetic and copies ran while one was open for 1% of the time, Pallas kernels for 2%

profile of v1, /device:TPU:1, one launch (start us, length us, event | category | flops | bytes accessed | tf_op | source)
XLA Modules:
  0.0 112.2 jit_solution(4719225444041768655)
XLA Ops:
  3.3 2.5 %stack.11.meta = s32[7]{0:T(128)S(1)} concatenate(s32[1]{0:T(128)} %bitcast, s32[1]{0:T(128)} %bitcast.1, s32[1]{0:T(128)} %bitcast.12, s32[1]{0:T(128)} %bitcast.4, s32[1]{0:T(128)} %get-tuple-element.53, s32[1]{0:T(128)} %bitcast.5, s32[1]{0:T(128)} %get-tuple-element.52), dimensions={0} | concatenate | bytes 56 | tf_op jit(solution)/shard_map/stack | solution.py:342
  5.9 1.2 %copy-done = f32[2,2,256,256]{3,2,1,0:T(8,128)S(1)} copy-done((f32[2,2,256,256]{3,2,1,0:T(8,128)S(1)}, f32[2,2,256,256]{3,2,1,0:T(8,128)}, u32[]{:S(2)}) %copy-start) | copy-done | bytes 1048600
  7.9 7.0 %collective-permute-start.4 = (f32[4,32,128]{2,1,0:T(8,128)S(1)}, f32[4,32,128]{2,1,0:T(8,128)S(1)}, u32[]{:S(2)}, u32[]{:S(2)}) collective-permute-start(f32[4,32,128]{2,1,0:T(8,128)S(1)} %get-tuple-element.28), channel_id=1, source_target_pairs={{0,60},{4,32},{8,36},{12,40},{16,44},{20,48},{24,52},{28,56},{32,2... | collective-permute-start | bytes 196616 | tf_op jit(solution)/shard_map/ppermute | solution.py:353
  15.0 3.9 %collective-permute-start.6 = (f32[4,32,128]{2,1,0:T(8,128)S(1)}, f32[4,32,128]{2,1,0:T(8,128)S(1)}, u32[]{:S(2)}, u32[]{:S(2)}) collective-permute-start(f32[4,32,128]{2,1,0:T(8,128)S(1)} %get-tuple-element.30), channel_id=1, source_target_pairs={{0,252},{4,224},{8,228},{12,232},{16,236},{20,240},{24,244},{28,24... | collective-permute-start | bytes 196616 | tf_op jit(solution)/shard_map/ppermute | solution.py:353
  18.9 1.5 %collective-permute-start.1 = (f32[4,128,128]{2,1,0:T(8,128)S(1)}, f32[4,128,128]{2,1,0:T(8,128)S(1)}, u32[]{:S(2)}, u32[]{:S(2)}) collective-permute-start(f32[4,128,128]{2,1,0:T(8,128)S(1)} %get-tuple-element.25), channel_id=1, source_target_pairs={{0,4},{4,8},{8,12},{12,16},{16,20},{20,24},{24,28},{28,0},{32,36},... | collective-permute-start | bytes 786440 | tf_op jit(solution)/shard_map/ppermute | solution.py:353
  20.3 1.7 %collective-permute-start.2 = (f32[4,64,256]{2,1,0:T(8,128)S(1)}, f32[4,64,256]{2,1,0:T(8,128)S(1)}, u32[]{:S(2)}, u32[]{:S(2)}) collective-permute-start(f32[4,64,256]{2,1,0:T(8,128)S(1)} %get-tuple-element.26), channel_id=1, source_target_pairs={{0,32},{4,36},{8,40},{12,44},{16,48},{20,52},{24,56},{28,60},{32,0... | collective-permute-start | bytes 786440 | tf_op jit(solution)/shard_map/ppermute | solution.py:353
  22.0 1.2 %collective-permute-start.7 = (f32[4,32,128]{2,1,0:T(8,128)S(1)}, f32[4,32,128]{2,1,0:T(8,128)S(1)}, u32[]{:S(2)}, u32[]{:S(2)}) collective-permute-start(f32[4,32,128]{2,1,0:T(8,128)S(1)} %get-tuple-element.31), channel_id=1, source_target_pairs={{0,228},{4,232},{8,236},{12,240},{16,244},{20,248},{24,252},{28,22... | collective-permute-start | bytes 196616 | tf_op jit(solution)/shard_map/ppermute | solution.py:353
  24.3 6.1 %collective-permute-done.7.far_left = f32[4,32,128]{2,1,0:T(8,128)S(1)} collective-permute-done((f32[4,32,128]{2,1,0:T(8,128)S(1)}, f32[4,32,128]{2,1,0:T(8,128)S(1)}, u32[]{:S(2)}, u32[]{:S(2)}) %collective-permute-start.7) | collective-permute-done | bytes 65568 | tf_op jit(solution)/shard_map/ppermute | solution.py:353
  30.4 10.7 %slots.1 = (f32[264,128]{1,0:T(8,128)S(1)}, f32[264,128]{1,0:T(8,128)S(1)}, f32[264,128]{1,0:T(8,128)S(1)}, f32[264,128]{1,0:T(8,128)S(1)}, f32[520,128]{1,0:T(8,128)S(1)}, /*index=5*/f32[520,128]{1,0:T(8,128)S(1)}) custom-call(s32[7]{0:T(128)S(1)} %stack.11.meta, f32[4,256,256]{2,1,0:T(8,128)S(1)} %bitcast.14, ...), custom_call_target="tpu_custom_call" | custom-call | tf_op jit(solution)/shard_map/slots/pallas_call | solution.py:24
  43.6 6.1 %all-to-all-start = ((f32[16,40,128]{2,1,0:T(8,128)}), f32[16,40,128]{2,1,0:T(8,128)S(1)}, u32[]{:S(2)}, u32[]{:S(2)}) async-start(f32[16,40,128]{2,1,0:T(8,128)} %spread.1), calls=%async_computation | async-start | bytes 655360 | tf_op jit(solution)/shard_map/all_to_all | solution.py:414
  49.7 1.4 %collective-permute-start.8 = (f32[264,128]{1,0:T(8,128)S(1)}, f32[264,128]{1,0:T(8,128)S(1)}, u32[]{:S(2)}, u32[]{:S(2)}) collective-permute-start(f32[264,128]{1,0:T(8,128)S(1)} %get-tuple-element.33), channel_id=1, source_target_pairs={{0,1},{1,2},{2,3},{3,0},{4,5},{5,6},{6,7},{7,4},{8,9},{9,10},{10,1... | collective-permute-start | bytes 405512 | tf_op jit(solution)/shard_map/ppermute | solution.py:368
  51.1 2.4 %collective-permute-start.9 = (f32[264,128]{1,0:T(8,128)S(1)}, f32[264,128]{1,0:T(8,128)S(1)}, u32[]{:S(2)}, u32[]{:S(2)}) collective-permute-start(f32[264,128]{1,0:T(8,128)S(1)} %get-tuple-element.34), channel_id=1, source_target_pairs={{0,2},{1,3},{2,0},{3,1},{4,6},{5,7},{6,4},{7,5},{8,10},{9,11},{10,... | collective-permute-start | bytes 405512 | tf_op jit(solution)/shard_map/ppermute | solution.py:368
  53.5 1.2 %collective-permute-start.10 = (f32[264,128]{1,0:T(8,128)S(1)}, f32[264,128]{1,0:T(8,128)S(1)}, u32[]{:S(2)}, u32[]{:S(2)}) collective-permute-start(f32[264,128]{1,0:T(8,128)S(1)} %get-tuple-element.35), channel_id=1, source_target_pairs={{0,3},{1,0},{2,1},{3,2},{4,7},{5,4},{6,5},{7,6},{8,11},{9,8},{10,9... | collective-permute-start | bytes 405512 | tf_op jit(solution)/shard_map/ppermute | solution.py:368
  54.6 4.1 %collective-permute-done.8.two = f32[264,128]{1,0:T(8,128)S(1)} collective-permute-done((f32[264,128]{1,0:T(8,128)S(1)}, f32[264,128]{1,0:T(8,128)S(1)}, u32[]{:S(2)}, u32[]{:S(2)}) %collective-permute-start.8) | collective-permute-done | bytes 135200 | tf_op jit(solution)/shard_map/ppermute | solution.py:368
  58.8 4.0 %collective-permute-done.9.three = f32[264,128]{1,0:T(8,128)S(1)} collective-permute-done((f32[264,128]{1,0:T(8,128)S(1)}, f32[264,128]{1,0:T(8,128)S(1)}, u32[]{:S(2)}, u32[]{:S(2)}) %collective-permute-start.9) | collective-permute-done | bytes 135200 | tf_op jit(solution)/shard_map/ppermute | solution.py:368
  62.8 1.3 %place.1 = (f32[192,128]{1,0:T(8,128)S(1)}, f32[192,128]{1,0:T(8,128)S(1)}, f32[2,384,128]{2,1,0:T(8,128)S(1)}, f32[8,40,128]{2,1,0:T(8,128)}) custom-call(f32[264,128]{1,0:T(8,128)S(1)} %get-tuple-element.32.one, f32[264,128]{1,0:T(8,128)S(1)} %collective-permute-done.8.two, f32[264,128]{1,0:T(8,128)S(1)} %collective-permute-done.9.three, ...), custom_call_target="tpu_custom_call" | custom-call | tf_op jit(solution)/shard_map/place/pallas_call | solution.py:24
  64.1 3.4 %all-to-all-start.1 = ((f32[8,40,128]{2,1,0:T(8,128)}), f32[8,40,128]{2,1,0:T(8,128)S(1)}, u32[]{:S(2)}, u32[]{:S(2)}) async-start(f32[8,40,128]{2,1,0:T(8,128)} %get-tuple-element.41), calls=%async_computation.1 | async-start | bytes 327680 | tf_op jit(solution)/shard_map/all_to_all | solution.py:425
  67.5 1.4 %collective-permute-start.12 = (f32[192,128]{1,0:T(8,128)S(1)}, f32[192,128]{1,0:T(8,128)S(1)}, u32[]{:S(2)}, u32[]{:S(2)}) collective-permute-start(f32[192,128]{1,0:T(8,128)S(1)} %get-tuple-element.38), channel_id=1, source_target_pairs={{0,4},{4,8},{8,12},{12,16},{16,20},{20,24},{24,28},{28,0},{32,36},... | collective-permute-start | bytes 294920 | tf_op jit(solution)/shard_map/ppermute | solution.py:353
  68.9 1.4 %collective-permute-start.13 = (f32[192,128]{1,0:T(8,128)S(1)}, f32[192,128]{1,0:T(8,128)S(1)}, u32[]{:S(2)}, u32[]{:S(2)}) collective-permute-start(f32[192,128]{1,0:T(8,128)S(1)} %get-tuple-element.39), channel_id=1, source_target_pairs={{0,28},{4,0},{8,4},{12,8},{16,12},{20,16},{24,20},{28,24},{32,60},... | collective-permute-start | bytes 294920 | tf_op jit(solution)/shard_map/ppermute | solution.py:353
  70.2 4.7 %collective-permute-done.12.from_left = f32[192,128]{1,0:T(8,128)S(1)} collective-permute-done((f32[192,128]{1,0:T(8,128)S(1)}, f32[192,128]{1,0:T(8,128)S(1)}, u32[]{:S(2)}, u32[]{:S(2)}) %collective-permute-start.12) | collective-permute-done | bytes 98336 | tf_op jit(solution)/shard_map/ppermute | solution.py:353
  75.6 1.3 %rows.1 = (f32[2,64,128]{2,1,0:T(8,128)S(1)}, f32[2,64,128]{2,1,0:T(8,128)S(1)}, f32[2,256,128]{2,1,0:T(8,128)S(1)}, f32[16,32,128]{2,1,0:T(8,128)}) custom-call(s32[7]{0:T(128)S(1)} %stack.11.meta, f32[192,128]{1,0:T(8,128)S(1)} %collective-permute-done.12.from_left, f32[192,128]{1,0:T(8,128)S(1)} %collective-permute-done.13.from_right, ...), custom_call_target="tpu_custom_call" | custom-call | tf_op jit(solution)/shard_map/rows/pallas_call | solution.py:24
  76.9 5.9 %all-to-all-start.2 = ((f32[16,32,128]{2,1,0:T(8,128)}), f32[16,32,128]{2,1,0:T(8,128)S(1)}, u32[]{:S(2)}, u32[]{:S(2)}) async-start(f32[16,32,128]{2,1,0:T(8,128)} %get-tuple-element.45), calls=%async_computation.2 | async-start | bytes 524288 | tf_op jit(solution)/shard_map/all_to_all | solution.py:435
  82.8 2.8 %collective-permute-start.14 = (f32[2,64,128]{2,1,0:T(8,128)S(1)}, f32[2,64,128]{2,1,0:T(8,128)S(1)}, u32[]{:S(2)}, u32[]{:S(2)}) collective-permute-start(f32[2,64,128]{2,1,0:T(8,128)S(1)} %get-tuple-element.42), channel_id=1, source_target_pairs={{0,32},{4,36},{8,40},{12,44},{16,48},{20,52},{24,56},{28,60},{32,0... | collective-permute-start | bytes 196616 | tf_op jit(solution)/shard_map/ppermute | solution.py:353
  85.6 1.5 %collective-permute-start.15 = (f32[2,64,128]{2,1,0:T(8,128)S(1)}, f32[2,64,128]{2,1,0:T(8,128)S(1)}, u32[]{:S(2)}, u32[]{:S(2)}) collective-permute-start(f32[2,64,128]{2,1,0:T(8,128)S(1)} %get-tuple-element.43), channel_id=1, source_target_pairs={{0,224},{4,228},{8,232},{12,236},{16,240},{20,244},{24,248},{28,25... | collective-permute-start | bytes 196616 | tf_op jit(solution)/shard_map/ppermute | solution.py:353
  87.1 3.7 %collective-permute-done.15.from_far = f32[2,64,128]{2,1,0:T(8,128)S(1)} collective-permute-done((f32[2,64,128]{2,1,0:T(8,128)S(1)}, f32[2,64,128]{2,1,0:T(8,128)S(1)}, u32[]{:S(2)}, u32[]{:S(2)}) %collective-permute-start.15) | collective-permute-done | bytes 65568 | tf_op jit(solution)/shard_map/ppermute | solution.py:353
  91.4 2.5 %collective-permute-start.18 = (f32[256,256]{1,0:T(8,128)S(1)}, f32[256,256]{1,0:T(8,128)S(1)}, u32[]{:S(2)}, u32[]{:S(2)}) collective-permute-start(f32[256,256]{1,0:T(8,128)S(1)} %finish.1.one), channel_id=1, source_target_pairs={{0,3},{1,0},{2,1},{3,2},{4,7},{5,4},{6,5},{7,6},{8,11},{9,8},{10,9... | collective-permute-start | bytes 786440 | tf_op jit(solution)/shard_map/ppermute | solution.py:368
  95.1 1.8 %collective-permute-start.19 = (f32[512,128]{1,0:T(8,128)S(1)}, f32[512,128]{1,0:T(8,128)S(1)}, u32[]{:S(2)}, u32[]{:S(2)}) collective-permute-start(f32[512,128]{1,0:T(8,128)S(1)} %bitcast.15), channel_id=1, source_target_pairs={{0,32},{4,36},{8,40},{12,44},{16,48},{20,52},{24,56},{28,60},{32,0... | collective-permute-start | bytes 786440 | tf_op jit(solution)/shard_map/ppermute | solution.py:353
  96.9 2.0 %collective-permute-done.18.four = f32[256,256]{1,0:T(8,128)S(1)} collective-permute-done((f32[256,256]{1,0:T(8,128)S(1)}, f32[256,256]{1,0:T(8,128)S(1)}, u32[]{:S(2)}, u32[]{:S(2)}) %collective-permute-start.18) | collective-permute-done | bytes 262176 | tf_op jit(solution)/shard_map/ppermute | solution.py:368
  98.9 3.0 %collective-permute-done.17.three = f32[256,256]{1,0:T(8,128)S(1)} collective-permute-done((f32[256,256]{1,0:T(8,128)S(1)}, f32[256,256]{1,0:T(8,128)S(1)}, u32[]{:S(2)}, u32[]{:S(2)}) %collective-permute-start.17) | collective-permute-done | bytes 262176 | tf_op jit(solution)/shard_map/ppermute | solution.py:368
  102.0 7.3 %collective-permute-done.16.two = f32[256,256]{1,0:T(8,128)S(1)} collective-permute-done((f32[256,256]{1,0:T(8,128)S(1)}, f32[256,256]{1,0:T(8,128)S(1)}, u32[]{:S(2)}, u32[]{:S(2)}) %collective-permute-start.16) | collective-permute-done | bytes 262176 | tf_op jit(solution)/shard_map/ppermute | solution.py:368
  109.3 1.6 %gather.1 = f32[4,256,256]{2,1,0:T(8,128)} custom-call(s32[7]{0:T(128)S(1)} %stack.11.meta, f32[256,256]{1,0:T(8,128)S(1)} %finish.1.one, f32[256,256]{1,0:T(8,128)S(1)} %collective-permute-done.16.two, f32[256,256]{1,0:T(8,128)S(1)} %collective-permute-done.17.three, f32[256,256]{1,0:T(8,128)S(1)} %collective-permute-done.18.four), custom_call_target="tpu_custom_call" | custom-call | tf_op jit(solution)/shard_map/gather/pallas_call | solution.py:24
  110.8 1.4 %halves.1 = f32[2,512,128]{2,1,0:T(8,128)} custom-call(s32[7]{0:T(128)S(1)} %stack.11.meta, f32[512,128]{1,0:T(8,128)S(1)} %bitcast.16, f32[512,128]{1,0:T(8,128)S(1)} %collective-permute-done.19.other), custom_call_target="tpu_custom_call" | custom-call | tf_op jit(solution)/shard_map/halves/pallas_call | solution.py:24
  (44 shorter events, 8.8 us)
Async XLA Ops:
  1.3 0.7 copy-start.7
  5.9 1.2 %copy-start = (f32[2,2,256,256]{3,2,1,0:T(8,128)S(1)}, f32[2,2,256,256]{3,2,1,0:T(8,128)}, u32[]{:S(2)}) copy-start(f32[2,2,256,256]{3,2,1,0:T(8,128)} %param.10) | copy-start | bytes 3145732
  7.1 23.3 %copy-start.1 = (f32[4,2,128,128]{3,2,1,0:T(8,128)S(1)}, f32[4,2,128,128]{3,2,1,0:T(8,128)}, u32[]{:S(2)}) copy-start(f32[4,2,128,128]{3,2,1,0:T(8,128)} %param.11) | copy-start | bytes 1572868
  7.1 23.3 %copy-start.3 = (bf16[256,256]{1,0:T(8,128)(2,1)S(1)}, bf16[256,256]{1,0:T(8,128)(2,1)}, u32[]{:S(2)}) copy-start(bf16[256,256]{1,0:T(8,128)(2,1)} %constant.34.clone.left_low) | copy-start | bytes 393220
  7.1 23.3 %copy-start.4 = (bf16[256,256]{1,0:T(8,128)(2,1)S(1)}, bf16[256,256]{1,0:T(8,128)(2,1)}, u32[]{:S(2)}) copy-start(bf16[256,256]{1,0:T(8,128)(2,1)} %constant.33.clone.left_high) | copy-start | bytes 393220
  7.1 23.3 %copy-start.5 = (bf16[256,256]{1,0:T(8,128)(2,1)S(1)}, bf16[256,256]{1,0:T(8,128)(2,1)}, u32[]{:S(2)}) copy-start(bf16[256,256]{1,0:T(8,128)(2,1)} %constant.32.clone.right_low) | copy-start | bytes 393220
  7.1 23.3 %copy-start.6 = (bf16[256,256]{1,0:T(8,128)(2,1)S(1)}, bf16[256,256]{1,0:T(8,128)(2,1)}, u32[]{:S(2)}) copy-start(bf16[256,256]{1,0:T(8,128)(2,1)} %constant.31.clone.right_high) | copy-start | bytes 393220
  7.9 22.5 %copy-start.2 = (f32[1,1,2,128,128]{4,3,2,1,0:T(8,128)S(1)}, f32[1,1,2,128,128]{4,3,2,1,0:T(8,128)}, u32[]{:S(2)}) copy-start(f32[1,1,2,128,128]{4,3,2,1,0:T(8,128)} %param.15) | copy-start | bytes 393220
  7.9 12.4 %collective-permute-start.4 = (f32[4,32,128]{2,1,0:T(8,128)S(1)}, f32[4,32,128]{2,1,0:T(8,128)S(1)}, u32[]{:S(2)}, u32[]{:S(2)}) collective-permute-start(f32[4,32,128]{2,1,0:T(8,128)S(1)} %get-tuple-element.28), channel_id=1, source_target_pairs={{0,60},{4,32},{8,36},{12,40},{16,44},{20,48},{24,52},{28,56},{32,2... | collective-permute-start | bytes 196616 | tf_op jit(solution)/shard_map/ppermute | solution.py:353
  15.0 7.0 %collective-permute-start.5 = (f32[4,32,128]{2,1,0:T(8,128)S(1)}, f32[4,32,128]{2,1,0:T(8,128)S(1)}, u32[]{:S(2)}, u32[]{:S(2)}) collective-permute-start(f32[4,32,128]{2,1,0:T(8,128)S(1)} %get-tuple-element.29), channel_id=1, source_target_pairs={{0,36},{4,40},{8,44},{12,48},{16,52},{20,56},{24,60},{28,32},{32,4... | collective-permute-start | bytes 196616 | tf_op jit(solution)/shard_map/ppermute | solution.py:353
  15.0 7.0 %collective-permute-start.6 = (f32[4,32,128]{2,1,0:T(8,128)S(1)}, f32[4,32,128]{2,1,0:T(8,128)S(1)}, u32[]{:S(2)}, u32[]{:S(2)}) collective-permute-start(f32[4,32,128]{2,1,0:T(8,128)S(1)} %get-tuple-element.30), channel_id=1, source_target_pairs={{0,252},{4,224},{8,228},{12,232},{16,236},{20,240},{24,244},{28,24... | collective-permute-start | bytes 196616 | tf_op jit(solution)/shard_map/ppermute | solution.py:353
  18.9 11.5 %collective-permute-start = (f32[4,128,128]{2,1,0:T(8,128)S(1)}, f32[4,128,128]{2,1,0:T(8,128)S(1)}, u32[]{:S(2)}, u32[]{:S(2)}) collective-permute-start(f32[4,128,128]{2,1,0:T(8,128)S(1)} %get-tuple-element.24), channel_id=1, source_target_pairs={{0,28},{4,0},{8,4},{12,8},{16,12},{20,16},{24,20},{28,24},{32,60},... | collective-permute-start | bytes 786440 | tf_op jit(solution)/shard_map/ppermute | solution.py:353
  18.9 11.5 %collective-permute-start.1 = (f32[4,128,128]{2,1,0:T(8,128)S(1)}, f32[4,128,128]{2,1,0:T(8,128)S(1)}, u32[]{:S(2)}, u32[]{:S(2)}) collective-permute-start(f32[4,128,128]{2,1,0:T(8,128)S(1)} %get-tuple-element.25), channel_id=1, source_target_pairs={{0,4},{4,8},{8,12},{12,16},{16,20},{20,24},{24,28},{28,0},{32,36},... | collective-permute-start | bytes 786440 | tf_op jit(solution)/shard_map/ppermute | solution.py:353
  20.3 10.0 %collective-permute-start.2 = (f32[4,64,256]{2,1,0:T(8,128)S(1)}, f32[4,64,256]{2,1,0:T(8,128)S(1)}, u32[]{:S(2)}, u32[]{:S(2)}) collective-permute-start(f32[4,64,256]{2,1,0:T(8,128)S(1)} %get-tuple-element.26), channel_id=1, source_target_pairs={{0,32},{4,36},{8,40},{12,44},{16,48},{20,52},{24,56},{28,60},{32,0... | collective-permute-start | bytes 786440 | tf_op jit(solution)/shard_map/ppermute | solution.py:353
  22.0 8.3 %collective-permute-start.3 = (f32[4,64,256]{2,1,0:T(8,128)S(1)}, f32[4,64,256]{2,1,0:T(8,128)S(1)}, u32[]{:S(2)}, u32[]{:S(2)}) collective-permute-start(f32[4,64,256]{2,1,0:T(8,128)S(1)} %get-tuple-element.27), channel_id=1, source_target_pairs={{0,224},{4,228},{8,232},{12,236},{16,240},{20,244},{24,248},{28,25... | collective-permute-start | bytes 786440 | tf_op jit(solution)/shard_map/ppermute | solution.py:353
  22.0 8.3 %collective-permute-start.7 = (f32[4,32,128]{2,1,0:T(8,128)S(1)}, f32[4,32,128]{2,1,0:T(8,128)S(1)}, u32[]{:S(2)}, u32[]{:S(2)}) collective-permute-start(f32[4,32,128]{2,1,0:T(8,128)S(1)} %get-tuple-element.31), channel_id=1, source_target_pairs={{0,228},{4,232},{8,236},{12,240},{16,244},{20,248},{24,252},{28,22... | collective-permute-start | bytes 196616 | tf_op jit(solution)/shard_map/ppermute | solution.py:353
  41.1 1.7 %collective-permute-start.11 = (f32[520,128]{1,0:T(8,128)S(1)}, f32[520,128]{1,0:T(8,128)S(1)}, u32[]{:S(2)}, u32[]{:S(2)}) collective-permute-start(f32[520,128]{1,0:T(8,128)S(1)} %get-tuple-element.37), channel_id=1, source_target_pairs={{0,32},{4,36},{8,40},{12,44},{16,48},{20,52},{24,56},{28,60},{32,0... | collective-permute-start | bytes 798728 | tf_op jit(solution)/shard_map/ppermute | solution.py:353
  43.6 19.2 %all-to-all-start = ((f32[16,40,128]{2,1,0:T(8,128)}), f32[16,40,128]{2,1,0:T(8,128)S(1)}, u32[]{:S(2)}, u32[]{:S(2)}) async-start(f32[16,40,128]{2,1,0:T(8,128)} %spread.1), calls=%async_computation | async-start | bytes 655360 | tf_op jit(solution)/shard_map/all_to_all | solution.py:414
  49.7 9.1 %collective-permute-start.8 = (f32[264,128]{1,0:T(8,128)S(1)}, f32[264,128]{1,0:T(8,128)S(1)}, u32[]{:S(2)}, u32[]{:S(2)}) collective-permute-start(f32[264,128]{1,0:T(8,128)S(1)} %get-tuple-element.33), channel_id=1, source_target_pairs={{0,1},{1,2},{2,3},{3,0},{4,5},{5,6},{6,7},{7,4},{8,9},{9,10},{10,1... | collective-permute-start | bytes 405512 | tf_op jit(solution)/shard_map/ppermute | solution.py:368
  51.1 11.7 %collective-permute-start.9 = (f32[264,128]{1,0:T(8,128)S(1)}, f32[264,128]{1,0:T(8,128)S(1)}, u32[]{:S(2)}, u32[]{:S(2)}) collective-permute-start(f32[264,128]{1,0:T(8,128)S(1)} %get-tuple-element.34), channel_id=1, source_target_pairs={{0,2},{1,3},{2,0},{3,1},{4,6},{5,7},{6,4},{7,5},{8,10},{9,11},{10,... | collective-permute-start | bytes 405512 | tf_op jit(solution)/shard_map/ppermute | solution.py:368
  53.5 9.3 %collective-permute-start.10 = (f32[264,128]{1,0:T(8,128)S(1)}, f32[264,128]{1,0:T(8,128)S(1)}, u32[]{:S(2)}, u32[]{:S(2)}) collective-permute-start(f32[264,128]{1,0:T(8,128)S(1)} %get-tuple-element.35), channel_id=1, source_target_pairs={{0,3},{1,0},{2,1},{3,2},{4,7},{5,4},{6,5},{7,6},{8,11},{9,8},{10,9... | collective-permute-start | bytes 405512 | tf_op jit(solution)/shard_map/ppermute | solution.py:368
  64.1 11.5 %all-to-all-start.1 = ((f32[8,40,128]{2,1,0:T(8,128)}), f32[8,40,128]{2,1,0:T(8,128)S(1)}, u32[]{:S(2)}, u32[]{:S(2)}) async-start(f32[8,40,128]{2,1,0:T(8,128)} %get-tuple-element.41), calls=%async_computation.1 | async-start | bytes 327680 | tf_op jit(solution)/shard_map/all_to_all | solution.py:425
  67.5 7.5 %collective-permute-start.12 = (f32[192,128]{1,0:T(8,128)S(1)}, f32[192,128]{1,0:T(8,128)S(1)}, u32[]{:S(2)}, u32[]{:S(2)}) collective-permute-start(f32[192,128]{1,0:T(8,128)S(1)} %get-tuple-element.38), channel_id=1, source_target_pairs={{0,4},{4,8},{8,12},{12,16},{16,20},{20,24},{24,28},{28,0},{32,36},... | collective-permute-start | bytes 294920 | tf_op jit(solution)/shard_map/ppermute | solution.py:353
  68.9 6.2 %collective-permute-start.13 = (f32[192,128]{1,0:T(8,128)S(1)}, f32[192,128]{1,0:T(8,128)S(1)}, u32[]{:S(2)}, u32[]{:S(2)}) collective-permute-start(f32[192,128]{1,0:T(8,128)S(1)} %get-tuple-element.39), channel_id=1, source_target_pairs={{0,28},{4,0},{8,4},{12,8},{16,12},{20,16},{24,20},{28,24},{32,60},... | collective-permute-start | bytes 294920 | tf_op jit(solution)/shard_map/ppermute | solution.py:353
  76.9 18.2 %all-to-all-start.2 = ((f32[16,32,128]{2,1,0:T(8,128)}), f32[16,32,128]{2,1,0:T(8,128)S(1)}, u32[]{:S(2)}, u32[]{:S(2)}) async-start(f32[16,32,128]{2,1,0:T(8,128)} %get-tuple-element.45), calls=%async_computation.2 | async-start | bytes 524288 | tf_op jit(solution)/shard_map/all_to_all | solution.py:435
  82.8 4.3 %collective-permute-start.14 = (f32[2,64,128]{2,1,0:T(8,128)S(1)}, f32[2,64,128]{2,1,0:T(8,128)S(1)}, u32[]{:S(2)}, u32[]{:S(2)}) collective-permute-start(f32[2,64,128]{2,1,0:T(8,128)S(1)} %get-tuple-element.42), channel_id=1, source_target_pairs={{0,32},{4,36},{8,40},{12,44},{16,48},{20,52},{24,56},{28,60},{32,0... | collective-permute-start | bytes 196616 | tf_op jit(solution)/shard_map/ppermute | solution.py:353
  85.6 5.3 %collective-permute-start.15 = (f32[2,64,128]{2,1,0:T(8,128)S(1)}, f32[2,64,128]{2,1,0:T(8,128)S(1)}, u32[]{:S(2)}, u32[]{:S(2)}) collective-permute-start(f32[2,64,128]{2,1,0:T(8,128)S(1)} %get-tuple-element.43), channel_id=1, source_target_pairs={{0,224},{4,228},{8,232},{12,236},{16,240},{20,244},{24,248},{28,25... | collective-permute-start | bytes 196616 | tf_op jit(solution)/shard_map/ppermute | solution.py:353
  91.4 7.5 %collective-permute-start.18 = (f32[256,256]{1,0:T(8,128)S(1)}, f32[256,256]{1,0:T(8,128)S(1)}, u32[]{:S(2)}, u32[]{:S(2)}) collective-permute-start(f32[256,256]{1,0:T(8,128)S(1)} %finish.1.one), channel_id=1, source_target_pairs={{0,3},{1,0},{2,1},{3,2},{4,7},{5,4},{6,5},{7,6},{8,11},{9,8},{10,9... | collective-permute-start | bytes 786440 | tf_op jit(solution)/shard_map/ppermute | solution.py:368
  93.9 8.1 %collective-permute-start.17 = (f32[256,256]{1,0:T(8,128)S(1)}, f32[256,256]{1,0:T(8,128)S(1)}, u32[]{:S(2)}, u32[]{:S(2)}) collective-permute-start(f32[256,256]{1,0:T(8,128)S(1)} %finish.1.one), channel_id=1, source_target_pairs={{0,2},{1,3},{2,0},{3,1},{4,6},{5,7},{6,4},{7,5},{8,10},{9,11},{10,... | collective-permute-start | bytes 786440 | tf_op jit(solution)/shard_map/ppermute | solution.py:368
  94.5 14.8 %collective-permute-start.16 = (f32[256,256]{1,0:T(8,128)S(1)}, f32[256,256]{1,0:T(8,128)S(1)}, u32[]{:S(2)}, u32[]{:S(2)}) collective-permute-start(f32[256,256]{1,0:T(8,128)S(1)} %finish.1.one), channel_id=1, source_target_pairs={{0,1},{1,2},{2,3},{3,0},{4,5},{5,6},{6,7},{7,4},{8,9},{9,10},{10,1... | collective-permute-start | bytes 786440 | tf_op jit(solution)/shard_map/ppermute | solution.py:368
  95.1 15.8 %collective-permute-start.19 = (f32[512,128]{1,0:T(8,128)S(1)}, f32[512,128]{1,0:T(8,128)S(1)}, u32[]{:S(2)}, u32[]{:S(2)}) collective-permute-start(f32[512,128]{1,0:T(8,128)S(1)} %bitcast.15), channel_id=1, source_target_pairs={{0,32},{4,36},{8,40},{12,44},{16,48},{20,52},{24,56},{28,60},{32,0... | collective-permute-start | bytes 786440 | tf_op jit(solution)/shard_map/ppermute | solution.py:353

commit v2 on v1

v2 whole, which is shorter than its diff:
```python
import functools

import jax
import jax.numpy as jnp
import numpy as np
from jax import lax
from jax.experimental import pallas as pl
from jax.experimental.pallas import tpu as pltpu
from jax.sharding import Mesh
from jax.sharding import PartitionSpec as P

F32 = jnp.float32
BF16 = jnp.bfloat16
VMEM = pl.BlockSpec(memory_space=pltpu.VMEM)
SMEM = pl.BlockSpec(memory_space=pltpu.SMEM)
ANY = pl.BlockSpec(memory_space=pl.ANY)
LONG = 10**10
PARAMS = pltpu.CompilerParams(vmem_limit_bytes=48 * 1024 * 1024)
W = 128
HALF = 64
TILE = 256
MODES = 4


def call(body, outs, args, specs, scratch=(), name=None, flops=0):
    return pl.pallas_call(
        body,
        out_shape=[jax.ShapeDtypeStruct(shape, F32) for shape in outs],
        in_specs=specs,
        out_specs=[VMEM] * len(outs),
        scratch_shapes=list(scratch),
        compiler_params=PARAMS,
        cost_estimate=pl.CostEstimate(flops=flops, bytes_accessed=0, transcendentals=0) if flops else None,
        name=name,
    )(*args)


def low_lanes(rows):
    return lax.broadcasted_iota(jnp.int32, (rows, W), 1) < HALF


def swap(x):
    return pltpu.roll(x, HALF, 1)


def rim_rows(core, last):
    return pl.multiple_of((1 - core) * last, HALF), pl.multiple_of(core * last, HALF)


def fold_corner(rows, left, right):
    short = low_lanes(HALF // 2)
    upper, lower = rows[: HALF // 2], rows[HALF // 2 :]
    left[...] = jnp.where(short, upper[:, :W], swap(lower[:, :W]))
    right[...] = jnp.where(short, swap(upper[:, W:]), lower[:, W:])


def pack_body(tile, to_core, to_far, far_left, far_right):
    core_row, far_row = rim_rows(lax.axis_index("core"), TILE - HALF)
    for part in range(4):
        to_core[part] = tile[part, pl.ds(core_row, HALF), :]
        rows = tile[part, pl.ds(far_row, HALF), :]
        to_far[part] = rows
        fold_corner(rows, far_left.at[part], far_right.at[part])


def sides_body(tile, from_core, to_left, to_right):
    wide = low_lanes(W)
    for part in range(4):
        first, second = tile[part, :W, :W], tile[part, W:, :W]
        to_left[part, :W] = jnp.where(wide, first, swap(second))
        first, second = tile[part, :W, W:], tile[part, W:, W:]
        to_right[part, :W] = jnp.where(wide, swap(first), second)
        corners = slice(W, W + HALF // 2)
        fold_corner(from_core[part], to_left.at[part, corners], to_right.at[part, corners])


def phase_body(phase, after, real, imag):
    real[...] = jnp.cos(phase[...])
    imag[...] = jnp.sin(phase[...])


def halves(x):
    high = x.astype(BF16)
    return high, (x - high.astype(F32)).astype(BF16)


def times_right(real, imag, table):
    outs = ([], [])
    for k in range(len(real)):
        high, low = halves(jnp.concatenate([real[k], imag[k]], axis=1))
        out = jnp.dot(jnp.concatenate([high, low, high], axis=1), table, preferred_element_type=F32)
        outs[0].append(out[:, :W])
        outs[1].append(out[:, W:])
    return outs


def times_left(table, real, imag):
    outs = ([], [])
    for k in range(0, len(real), 2):
        high, low = halves(
            jnp.concatenate(
                [jnp.concatenate(real[k : k + 2], axis=1), jnp.concatenate(imag[k : k + 2], axis=1)],
                axis=0,
            )
        )
        out = jnp.dot(table, jnp.concatenate([high, low, high], axis=0), preferred_element_type=F32)
        for m in range(2):
            outs[0].append(out[:W, W * m : W * (m + 1)])
            outs[1].append(out[W:, W * m : W * (m + 1)])
    return outs


def slots_body(
    offsets,
    live_counts,
    tile,
    from_right,
    from_left,
    from_core,
    from_far,
    far_right,
    far_left,
    probe,
    kernel_real,
    kernel_imag,
    measured,
    right_high,
    right_low,
    left_high,
    left_low,
    out0,
    out1,
    out2,
    out3,
    probe_send,
    probe_keep,
    wide,
    grads,
    probe_sum,
    mid,
    patches,
):
    core, scan = lax.axis_index("core"), lax.axis_index("scan")
    live = live_counts[0, 0, 0]
    core_row, far_row = rim_rows(core, TILE + HALF)
    tall = low_lanes(W)
    short = low_lanes(HALF // 2)
    for part in range(4):
        wide[part, 0, HALF : HALF + TILE] = tile[part, :, :W]
        wide[part, 1, HALF : HALF + TILE] = tile[part, :, W:]
        right, left = from_right[part, :W], from_left[part, :W]
        wide[part, 2, HALF : HALF + W] = jnp.where(tall, right, swap(left))
        wide[part, 2, HALF + W : HALF + TILE] = jnp.where(tall, swap(right), left)
        for row, strip, right, left in (
            (core_row, from_core, from_right[part, W:], from_left[part, W:]),
            (far_row, from_far, far_right[part], far_left[part]),
        ):
            wide[part, 0, pl.ds(row, HALF)] = strip[part, :, :W]
            wide[part, 1, pl.ds(row, HALF)] = strip[part, :, W:]
            wide[part, 2, pl.ds(row, HALF // 2)] = jnp.where(short, right, swap(left))
            lower = pl.multiple_of(row + HALF // 2, HALF // 2)
            wide[part, 2, pl.ds(lower, HALF // 2)] = jnp.where(short, swap(right), left)

    def corner(slot):
        row = jnp.clip(offsets[0, 0, slot, 0] + HALF, 0, TILE)
        col = jnp.clip(offsets[0, 0, slot, 1], -HALF, TILE - HALF)
        return row, jnp.where(col < 0, col + 3 * W, col)

    forward_right = jnp.concatenate([right_high[...], right_high[...], right_low[...]], axis=0)
    inverse_right = jnp.concatenate([left_high[...], left_high[...], left_low[...]], axis=0)
    forward_left = jnp.concatenate([left_high[...], left_high[...], left_low[...]], axis=1)
    inverse_left = jnp.concatenate([right_high[...], right_high[...], right_low[...]], axis=1)

    def transform(real, imag):
        return times_left(forward_left, *times_right(real, imag, forward_right))

    def untransform(real, imag):
        return times_right(*times_left(inverse_left, real, imag), inverse_right)

    modes = range(MODES)
    lanes = lax.broadcasted_iota(jnp.int32, (W, W), 1)

    for slot in range(2):
        row, col = corner(slot)
        block = col // W
        shift = col - block * W
        after = jnp.where(block == 2, 0, block + 1)
        turn = jnp.where(shift == 0, 0, W - shift)
        for part in range(4):
            one = pltpu.roll(wide[part, block, pl.ds(row, W)], turn, 1)
            two = pltpu.roll(wide[part, after, pl.ds(row, W)], turn, 1)
            patches[4 * slot + part] = jnp.where(lanes < W - shift, one, two)
    slots = range(2)
    pairs = [(slot, m) for slot in slots for m in modes]

    def patch(part):
        return [patches[4 * slot + part] for slot in slots]

    def times(real, imag, by_real, by_imag):
        return (
            [r * by_real[s] - i * by_imag[s] for (s, m), r, i in zip(pairs, real, imag)],
            [r * by_imag[s] + i * by_real[s] for (s, m), r, i in zip(pairs, real, imag)],
        )

    def times_conj(real, imag, by_real, by_imag):
        return (
            [r * by_real[s] + i * by_imag[s] for (s, m), r, i in zip(pairs, real, imag)],
            [i * by_real[s] - r * by_imag[s] for (s, m), r, i in zip(pairs, real, imag)],
        )

    def total(terms):
        return [functools.reduce(jnp.add, terms[MODES * s : MODES * (s + 1)]) for s in slots]

    near_real, near_imag = patch(0), patch(1)
    real, imag = times(
        [probe[2 * m] for s, m in pairs], [probe[2 * m + 1] for s, m in pairs], near_real, near_imag
    )
    real, imag = transform(real, imag)
    kr, ki = [kernel_real[...]] * 2, [kernel_imag[...]] * 2
    real, imag = times(real, imag, kr, ki)
    real, imag = untransform(real, imag)
    for n in range(2 * MODES):
        mid[2 * n] = real[n]
        mid[2 * n + 1] = imag[n]
    away_real, away_imag = patch(2), patch(3)
    real, imag = times(real, imag, away_real, away_imag)
    real, imag = transform(real, imag)
    intensity = total([r * r + i * i for r, i in zip(real, imag)])
    residual = [
        (intensity[s] - measured[s]) * jnp.where(s < live, 2.0, 0.0).astype(F32) for s in slots
    ]
    real = [r * residual[s] for (s, m), r in zip(pairs, real)]
    imag = [i * residual[s] for (s, m), i in zip(pairs, imag)]
    real, imag = untransform(real, imag)
    both = range(2 * MODES)
    grad_real = total([mid[2 * n] * real[n] + mid[2 * n + 1] * imag[n] for n in both])
    grad_imag = total([mid[2 * n] * imag[n] - mid[2 * n + 1] * real[n] for n in both])
    for s in slots:
        grads[2, s] = grad_real[s]
        grads[3, s] = grad_imag[s]
    real, imag = times_conj(real, imag, patch(2), patch(3))
    real, imag = transform(real, imag)
    real, imag = times_conj(real, imag, kr, ki)
    real, imag = untransform(real, imag)
    grad_real = total([probe[2 * m] * real[n] + probe[2 * m + 1] * imag[n] for n, (s, m) in enumerate(pairs)])
    grad_imag = total([probe[2 * m] * imag[n] - probe[2 * m + 1] * real[n] for n, (s, m) in enumerate(pairs)])
    for s in slots:
        grads[0, s] = grad_real[s]
        grads[1, s] = grad_imag[s]
    real, imag = times_conj(real, imag, patch(0), patch(1))
    for m in modes:
        probe_sum[2 * m] = real[m] + real[MODES + m]
        probe_sum[2 * m + 1] = imag[m] + imag[MODES + m]

    places = lax.broadcasted_iota(jnp.int32, (8, W), 0)
    marks = jnp.zeros((8, W), F32)
    for k, value in enumerate((*corner(0), *corner(1))):
        marks = jnp.where(places == k, value.astype(F32), marks)
    for step, out in enumerate((out0, out1, out2, out3)):
        part = lax.rem(scan + step, 4)
        for slot in range(2):
            out[W * slot : W * (slot + 1)] = grads[part, slot]
        out[2 * W :] = marks
    count = jnp.zeros((8, W), F32) + live.astype(F32)
    for half, out in ((core, probe_keep), (1 - core, probe_send)):
        for k in range(MODES):
            out[W * k : W * (k + 1)] = probe_sum[half * MODES + k]
        out[MODES * W :] = count


def spread_body(keep, got, out):
    rows = out.shape[1] - 8
    count = keep[MODES * W :] + got[MODES * W :]
    for k in range(out.shape[0]):
        span = slice(k * rows, (k + 1) * rows)
        out[k, :rows] = keep[span] + got[span]
        out[k, rows:] = count


def total_of(chunks):
    total = chunks[0]
    for k in range(1, chunks.shape[0]):
        total = total + chunks[k]
    return total


def sum_body(chunks, after, spread):
    total = total_of(chunks)
    for k in range(spread.shape[0]):
        spread[k] = total


def mean_body(chunks, after, spread):
    total = total_of(chunks)
    rows = spread.shape[1]
    mean = total[:rows] / total[rows : rows + 1]
    for k in range(spread.shape[0]):
        spread[k] = mean


def place_body(one, two, three, four, wide):
    wide[...] = jnp.zeros_like(wide)
    lanes = lax.broadcasted_iota(jnp.int32, (W, W), 1)
    for message in (one, two, three, four):
        for slot in range(2):
            base = 2 * W + 2 * slot
            row = jnp.max(message[base : base + 1]).astype(jnp.int32)
            col = jnp.max(message[base + 1 : base + 2]).astype(jnp.int32)
            row = jnp.clip(row, 0, TILE)
            col = jnp.clip(col, 0, 3 * W - 1)
            block = col // W
            shift = col - block * W
            after = jnp.where(block == 2, 0, block + 1)
            turned = pltpu.roll(message[W * slot : W * (slot + 1)], shift, 1)
            wide[block, pl.ds(row, W)] += jnp.where(lanes >= shift, turned, 0.0)
            wide[after, pl.ds(row, W)] += jnp.where(lanes < shift, turned, 0.0)


def edges_body(wide, after, to_left, to_right):
    half = (TILE + 2 * HALF) // 2
    low = low_lanes(half)
    upper, lower = wide[2, :half], wide[2, half:]
    to_right[...] = jnp.where(low, upper, swap(lower))
    to_left[...] = jnp.where(low, swap(upper), lower)


def rows_body(from_left, from_right, held, to_core, to_far, keep, wide):
    half = (TILE + 2 * HALF) // 2
    low = low_lanes(half)
    left, right = from_left[...], from_right[...]
    wide[0, :half] = held[0, :half] + jnp.where(low, left, 0.0)
    wide[0, half:] = held[0, half:] + jnp.where(low, swap(left), 0.0)
    wide[1, :half] = held[1, :half] + jnp.where(low, 0.0, swap(right))
    wide[1, half:] = held[1, half:] + jnp.where(low, 0.0, right)
    core_row, far_row = rim_rows(lax.axis_index("core"), TILE + HALF)
    for k in range(2):
        to_core[k] = wide[k, pl.ds(core_row, HALF)]
        to_far[k] = wide[k, pl.ds(far_row, HALF)]
        keep[k] = wide[k, HALF : HALF + TILE]


def finish_body(from_core, from_far, held, out):
    core_row, far_row = rim_rows(lax.axis_index("core"), TILE - HALF)
    for k in range(2):
        span = slice(k * W, (k + 1) * W)
        out[:, span] = held[k]
        out[pl.ds(core_row, HALF), span] += from_core[k]
        out[pl.ds(far_row, HALF), span] += from_far[k]


def gather_body(one, two, three, four, out):
    scan = lax.axis_index("scan")
    for step, part in enumerate((one, two, three, four)):
        out[lax.rem(scan + 4 - step, 4)] = part[...]


def halves_body(mine, other, out):
    core = lax.axis_index("core")
    out[core] = mine[...]
    out[1 - core] = other[...]


def tables():
    index = np.arange(W)
    angle = 2.0 * np.pi * ((index[:, None] * index[None, :]) % W) / W
    cos, sin = np.cos(angle) / np.sqrt(W), -np.sin(angle) / np.sqrt(W)
    right = np.block([[cos, sin], [-sin, cos]])
    arrays = []
    for table in (right, right.T):
        high = table.astype(BF16)
        low = (table - high.astype(np.float64)).astype(BF16)
        arrays += [high, low]
    return [jnp.asarray(a) for a in arrays]


def run_slots(*args):
    message = (2 * W + 8, W)
    share = (MODES * W + 8, W)
    return call(
        slots_body,
        [message] * 4 + [share] * 2,
        (*args, *tables()),
        [SMEM] * 2 + [VMEM] * 15,
        scratch=[
            pltpu.VMEM((4, 3, TILE + 2 * HALF, W), F32),
            pltpu.VMEM((4, 2, W, W), F32),
            pltpu.VMEM((2 * MODES, W, W), F32),
            pltpu.VMEM((4 * MODES, W, W), F32),
            pltpu.VMEM((8, W, W), F32),
        ],
        name="slots",
    )


def per_device(sizes, specimen, probe_modes, kernel_phase, offsets, live_counts, measured):
    nx, ntx, nsc = sizes

    def over_grid(target):
        pairs = []
        for x in range(nx):
            for c in range(2):
                for t in range(ntx):
                    x2, c2, t2 = target(x, c, t)
                    pairs.append(((x * 2 + c) * ntx + t, ((x2 % nx) * 2 + c2) * ntx + t2 % ntx))
        return lambda value: lax.ppermute(value, ("x", "core", "tx"), pairs)

    def across(x, c):
        return x + (1 if c else -1), 1 - c

    to_left = over_grid(lambda x, c, t: (x, c, t - 1))
    to_right = over_grid(lambda x, c, t: (x, c, t + 1))
    to_core = over_grid(lambda x, c, t: (x, 1 - c, t))
    to_far = over_grid(lambda x, c, t: (*across(x, c), t))
    far_left = over_grid(lambda x, c, t: (*across(x, c), t - 1))
    far_right = over_grid(lambda x, c, t: (*across(x, c), t + 1))

    def to_scan(value, step):
        return lax.ppermute(value, "scan", [(s, (s + step) % nsc) for s in range(nsc)])

    tile = specimen.reshape(4, TILE, TILE)
    strip, corner, side = (4, HALF, TILE), (4, HALF // 2, W), (4, W + HALF // 2, W)
    near, far, left, right = call(
        pack_body, [strip, strip, corner, corner], (tile,), [VMEM], name="pack"
    )
    marker = far
    from_core = to_core(near)
    from_far, corner_right, corner_left = to_far(far), far_left(left), far_right(right)
    left, right = call(
        sides_body, [side, side], (tile, from_core), [VMEM] * 2, name="sides", flops=LONG
    )
    from_right, from_left = to_left(left), to_right(right)
    kernel_real, kernel_imag = call(
        phase_body, [(W, W)] * 2, (kernel_phase, marker), [VMEM, ANY], name="phase", flops=10**9
    )
    outs = run_slots(
        offsets,
        live_counts,
        tile,
        from_right,
        from_left,
        from_core,
        from_far,
        corner_right,
        corner_left,
        probe_modes.reshape(2 * MODES, W, W),
        kernel_real,
        kernel_imag,
        measured[0, 0],
    )
    own, away, probe_send, probe_keep = outs[0], outs[1:4], outs[4], outs[5]
    arrived = [to_scan(value, step) for step, value in enumerate(away, 1)]
    probe_got = to_core(probe_send)
    group = nx * nsc
    rows_each = MODES * W // group
    (chunks,) = call(
        spread_body,
        [(group, rows_each + 8, W)],
        (probe_keep, probe_got),
        [VMEM] * 2,
        name="spread",
        flops=LONG,
    )
    chunks = lax.all_to_all(chunks, ("x", "scan"), 0, 0)
    tall = TILE + 2 * HALF
    (held,) = call(
        place_body, [(3, tall, W)], (own, *arrived), [VMEM] * 4, name="place", flops=LONG
    )
    left, right = call(
        edges_body, [(tall // 2, W)] * 2, (held, chunks), [VMEM, ANY], name="edges"
    )
    left, right = to_left(left), to_right(right)
    near, far, held = call(
        rows_body,
        [(2, HALF, W)] * 2 + [(2, TILE, W)],
        (right, left, held),
        [VMEM] * 3,
        scratch=[pltpu.VMEM((2, tall, W), F32)],
        name="rows",
        flops=LONG,
    )
    (spread,) = call(
        sum_body,
        [(ntx, rows_each + 8, W)],
        (chunks, near),
        [VMEM, ANY],
        name="sum",
        flops=LONG,
    )
    near, far = to_core(near), to_far(far)
    spread = lax.all_to_all(spread, "tx", 0, 0)
    (quarter,) = call(
        finish_body, [(TILE, TILE)], (near, far, held), [VMEM] * 3, name="finish", flops=LONG
    )
    (spread,) = call(
        mean_body,
        [(group, rows_each, W)],
        (spread, quarter),
        [VMEM, ANY],
        name="mean",
        flops=LONG,
    )
    mine = lax.all_to_all(spread, ("x", "scan"), 0, 0).reshape(MODES * W, W)
    quarters = [quarter] + [to_scan(quarter, step) for step in range(1, nsc)]
    other = to_core(mine)
    (probe_grad,) = call(
        halves_body, [(2, MODES * W, W)], (mine, other), [VMEM] * 2, name="halves", flops=LONG
    )
    (object_grad,) = call(gather_body, [(4, TILE, TILE)], quarters, [VMEM] * 4, name="gather", flops=LONG)
    return object_grad.reshape(specimen.shape), probe_grad.reshape(probe_modes.shape)


def solution(mesh):
    ny, ntx, nsc = mesh.devices.shape
    split = Mesh(mesh.devices.reshape(ny // 2, 2, ntx, nsc), ("x", "core", "tx", "scan"))
    rows = ("x", "core")
    placed = (
        P(None, None, rows, "tx"),
        P(),
        P(),
        P(rows, "tx", "scan", None),
        P(rows, "tx", "scan"),
        P(rows, "tx", "scan", None, None),
    )
    return jax.shard_map(
        functools.partial(per_device, (ny // 2, ntx, nsc)),
        mesh=split,
        in_specs=placed,
        out_specs=(P(None, None, rows, "tx"), P()),
        check_vma=False,
    )
```

time: 113 us -> 89.7 us (0.79)
  blocking collectives: 0 us -> 14.1 us
  waiting for transfers between devices: 36.8 us -> 23.1 us
  starting transfers between devices: 48.6 us -> 37 us
  Pallas kernels: 18.5 us -> 11.7 us
  local copies, waits for them, and re-layouts: 6.71 us -> 1.88 us
    ppermute x6, waiting for transfers between devices: 20.5 us -> 1.18 us  [to_scan(): lax.ppermute(value, 'scan', [(s, (s + step) % nsc) for s in range(nsc)])]
    all_to_all x0 -> x1, blocking collectives: none -> 14.1 us  [per_device(): mine = lax.all_to_all(spread, ('x', 'scan'), 0, 0).reshape(MODES * W, W)]
    pallas_call x8 -> x13, Pallas kernels: 18.5 us -> 11.7 us  [call(): pl.pallas_call(body, out_shape=[jax.ShapeDtypeStruct(shape, F32) for shap...]
    all_to_all x1, waiting for transfers between devices: 0.01 us -> 6.1 us  [per_device(): chunks = lax.all_to_all(chunks, ('x', 'scan'), 0, 0)]
    all_to_all x1 -> x0, starting transfers between devices: 5.85 us -> none  [per_device(): mine = lax.all_to_all(spread, ('x', 'scan'), 0, 0).reshape(MODES * W, W)]
    ppermute x14 -> x12, waiting for transfers between devices: 15.8 us -> 10.9 us  [over_grid(): return lambda value: lax.ppermute(value, ('x', 'core', 'tx'), pairs)]
    all_to_all x1, waiting for transfers between devices: 0.57 us -> 4.91 us  [per_device(): spread = lax.all_to_all(spread, 'tx', 0, 0)]
    ppermute x14 -> x12, starting transfers between devices: 24.7 us -> 20.8 us  [over_grid(): return lambda value: lax.ppermute(value, ('x', 'core', 'tx'), pairs)]
  transfers between devices with their start and end apart: 23 -> 20, of which waited for: 11 -> 8; matrix products, arithmetic and copies ran while one was open for 1% -> 0% of each run, Pallas kernels for 2% -> 4%
where the time goes in v2:
time: 89.7 us; the launch traced here: 89.3 us
  starting transfers between devices  37 us (41%)
  waiting for transfers between devices  23.1 us (26%)
  blocking collectives  14.1 us (16%)
  Pallas kernels  11.7 us (13%)
  local copies, waits for them, and re-layouts  1.88 us (2%)
  between operations  1.55 us (2%)
    ppermute x12, starting transfers between devices, over_grid(): return lambda value: lax.ppermute(value, ('x', 'core', 'tx'), pairs)  20.8 us
    all_to_all x1, blocking collectives, per_device(): mine = lax.all_to_all(spread, ('x', 'scan'), 0, 0).reshape(MODES * W, W)  14.1 us
    pallas_call x13, Pallas kernels, call(): pl.pallas_call(body, out_shape=[jax.ShapeDtypeStruct(shape, F32) for shap...  11.7 us
    ppermute x12, waiting for transfers between devices, over_grid(): return lambda value: lax.ppermute(value, ('x', 'core', 'tx'), pairs)  10.9 us
    ppermute x6, starting transfers between devices, to_scan(): lax.ppermute(value, 'scan', [(s, (s + step) % nsc) for s in range(nsc)])  8.39 us
    all_to_all x1, waiting for transfers between devices, per_device(): chunks = lax.all_to_all(chunks, ('x', 'scan'), 0, 0)  6.1 us
    all_to_all x1, waiting for transfers between devices, per_device(): spread = lax.all_to_all(spread, 'tx', 0, 0)  4.91 us
    all_to_all x1, starting transfers between devices, per_device(): spread = lax.all_to_all(spread, 'tx', 0, 0)  4.23 us
  transfers between devices with their start and end apart: 20, of which 8 were waited for; matrix products, arithmetic and copies ran while one was open for 0% of the time, Pallas kernels for 4%

profile of v2, /device:TPU:1, one launch (start us, length us, event | category | flops | bytes accessed | tf_op | source)
XLA Modules:
  0.0 89.3 jit_solution(12587588940426290918)
XLA Ops:
  0.6 1.2 %copy-done = f32[2,2,256,256]{3,2,1,0:T(8,128)S(1)} copy-done((f32[2,2,256,256]{3,2,1,0:T(8,128)S(1)}, f32[2,2,256,256]{3,2,1,0:T(8,128)}, u32[]{:S(2)}) %copy-start) | copy-done | bytes 1048600
  2.0 3.3 %collective-permute-start = (f32[4,64,256]{2,1,0:T(8,128)S(1)}, f32[4,64,256]{2,1,0:T(8,128)S(1)}, u32[]{:S(2)}, u32[]{:S(2)}) collective-permute-start(f32[4,64,256]{2,1,0:T(8,128)S(1)} %get-tuple-element.21), channel_id=1, source_target_pairs={{0,32},{4,36},{8,40},{12,44},{16,48},{20,52},{24,56},{28,60},{32,0... | collective-permute-start | bytes 786440 | tf_op jit(solution)/shard_map/ppermute | solution.py:405
  5.3 1.2 %collective-permute-done.from_core = f32[4,64,256]{2,1,0:T(8,128)S(1)} collective-permute-done((f32[4,64,256]{2,1,0:T(8,128)S(1)}, f32[4,64,256]{2,1,0:T(8,128)S(1)}, u32[]{:S(2)}, u32[]{:S(2)}) %collective-permute-start) | collective-permute-done | bytes 262176 | tf_op jit(solution)/shard_map/ppermute | solution.py:405
  6.7 3.9 %collective-permute-start.1 = (f32[4,160,128]{2,1,0:T(8,128)S(1)}, f32[4,160,128]{2,1,0:T(8,128)S(1)}, u32[]{:S(2)}, u32[]{:S(2)}) collective-permute-start(f32[4,160,128]{2,1,0:T(8,128)S(1)} %get-tuple-element.22), channel_id=1, source_target_pairs={{0,28},{4,0},{8,4},{12,8},{16,12},{20,16},{24,20},{28,24},{32,60},... | collective-permute-start | bytes 983048 | tf_op jit(solution)/shard_map/ppermute | solution.py:405
  10.6 1.8 %collective-permute-start.3 = (f32[4,64,256]{2,1,0:T(8,128)S(1)}, f32[4,64,256]{2,1,0:T(8,128)S(1)}, u32[]{:S(2)}, u32[]{:S(2)}) collective-permute-start(f32[4,64,256]{2,1,0:T(8,128)S(1)} %get-tuple-element.24.after), channel_id=1, source_target_pairs={{0,224},{4,228},{8,232},{12,236},{16,240},{20,244},{24,248},{28,25... | collective-permute-start | bytes 786440 | tf_op jit(solution)/shard_map/ppermute | solution.py:405
  12.4 2.7 %collective-permute-start.4 = (f32[4,32,128]{2,1,0:T(8,128)S(1)}, f32[4,32,128]{2,1,0:T(8,128)S(1)}, u32[]{:S(2)}, u32[]{:S(2)}) collective-permute-start(f32[4,32,128]{2,1,0:T(8,128)S(1)} %get-tuple-element.25), channel_id=1, source_target_pairs={{0,252},{4,224},{8,228},{12,232},{16,236},{20,240},{24,244},{28,24... | collective-permute-start | bytes 196616 | tf_op jit(solution)/shard_map/ppermute | solution.py:405
  15.8 0.4 phase.2
  16.3 2.5 %collective-permute-done.4.far_right = f32[4,32,128]{2,1,0:T(8,128)S(1)} collective-permute-done((f32[4,32,128]{2,1,0:T(8,128)S(1)}, f32[4,32,128]{2,1,0:T(8,128)S(1)}, u32[]{:S(2)}, u32[]{:S(2)}) %collective-permute-start.4) | collective-permute-done | bytes 65568 | tf_op jit(solution)/shard_map/ppermute | solution.py:405
  18.8 5.1 %collective-permute-done.5.far_left = f32[4,32,128]{2,1,0:T(8,128)S(1)} collective-permute-done((f32[4,32,128]{2,1,0:T(8,128)S(1)}, f32[4,32,128]{2,1,0:T(8,128)S(1)}, u32[]{:S(2)}, u32[]{:S(2)}) %collective-permute-start.5) | collective-permute-done | bytes 65568 | tf_op jit(solution)/shard_map/ppermute | solution.py:405
  24.0 0.6 copy-done.8
  24.6 6.8 %slots.1 = (f32[264,128]{1,0:T(8,128)S(1)}, f32[264,128]{1,0:T(8,128)S(1)}, f32[264,128]{1,0:T(8,128)S(1)}, f32[264,128]{1,0:T(8,128)S(1)}, f32[520,128]{1,0:T(8,128)S(1)}, /*index=5*/f32[520,128]{1,0:T(8,128)S(1)}) custom-call(s32[1,1,2,2]{3,2,1,0:T(2,128)S(1)} %copy-done.8, s32[1,1,1]{2,1,0:T(1,128)S(6)} %copy.12.live_counts, f32[4,256,256]{2,1,0:T(8,128)S(1)} %bitcast.8, ...), custom_call_target="tpu_custom_call" | custom-call | tf_op jit(solution)/shard_map/slots/pallas_call | solution.py:26
  31.4 0.9 collective-permute-start.9
  32.3 1.3 %collective-permute-start.6 = (f32[264,128]{1,0:T(8,128)S(1)}, f32[264,128]{1,0:T(8,128)S(1)}, u32[]{:S(2)}, u32[]{:S(2)}) collective-permute-start(f32[264,128]{1,0:T(8,128)S(1)} %get-tuple-element.30), channel_id=1, source_target_pairs={{0,1},{1,2},{2,3},{3,0},{4,5},{5,6},{6,7},{7,4},{8,9},{9,10},{10,1... | collective-permute-start | bytes 405512 | tf_op jit(solution)/shard_map/ppermute | solution.py:418
  33.6 2.6 %collective-permute-start.7 = (f32[264,128]{1,0:T(8,128)S(1)}, f32[264,128]{1,0:T(8,128)S(1)}, u32[]{:S(2)}, u32[]{:S(2)}) collective-permute-start(f32[264,128]{1,0:T(8,128)S(1)} %get-tuple-element.31), channel_id=1, source_target_pairs={{0,2},{1,3},{2,0},{3,1},{4,6},{5,7},{6,4},{7,5},{8,10},{9,11},{10,... | collective-permute-start | bytes 405512 | tf_op jit(solution)/shard_map/ppermute | solution.py:418
  36.2 1.1 %collective-permute-start.8 = (f32[264,128]{1,0:T(8,128)S(1)}, f32[264,128]{1,0:T(8,128)S(1)}, u32[]{:S(2)}, u32[]{:S(2)}) collective-permute-start(f32[264,128]{1,0:T(8,128)S(1)} %get-tuple-element.32), channel_id=1, source_target_pairs={{0,3},{1,0},{2,1},{3,2},{4,7},{5,4},{6,5},{7,6},{8,11},{9,8},{10,9... | collective-permute-start | bytes 405512 | tf_op jit(solution)/shard_map/ppermute | solution.py:418
  37.3 0.8 spread.1
  38.1 3.5 %all-to-all-start = ((f32[16,40,128]{2,1,0:T(8,128)}), f32[16,40,128]{2,1,0:T(8,128)S(1)}, u32[]{:S(2)}, u32[]{:S(2)}) async-start(f32[16,40,128]{2,1,0:T(8,128)} %spread.1), calls=%async_computation | async-start | bytes 655360 | tf_op jit(solution)/shard_map/all_to_all | solution.py:463
  41.6 1.2 %collective-permute-done.7.three = f32[264,128]{1,0:T(8,128)S(1)} collective-permute-done((f32[264,128]{1,0:T(8,128)S(1)}, f32[264,128]{1,0:T(8,128)S(1)}, u32[]{:S(2)}, u32[]{:S(2)}) %collective-permute-start.7) | collective-permute-done | bytes 135200 | tf_op jit(solution)/shard_map/ppermute | solution.py:418
  42.8 0.4 place.1.wide.held
  43.2 6.1 %all-to-all-done.after.chunks = f32[16,40,128]{2,1,0:T(8,128)S(1)} async-done(((f32[16,40,128]{2,1,0:T(8,128)}), f32[16,40,128]{2,1,0:T(8,128)S(1)}, u32[]{:S(2)}, u32[]{:S(2)}) %all-to-all-start) | async-done | bytes 327712 | tf_op jit(solution)/shard_map/all_to_all | solution.py:463
  49.5 2.7 %collective-permute-start.11 = (f32[192,128]{1,0:T(8,128)S(1)}, f32[192,128]{1,0:T(8,128)S(1)}, u32[]{:S(2)}, u32[]{:S(2)}) collective-permute-start(f32[192,128]{1,0:T(8,128)S(1)} %get-tuple-element.36), channel_id=1, source_target_pairs={{0,28},{4,0},{8,4},{12,8},{16,12},{20,16},{24,20},{28,24},{32,60},... | collective-permute-start | bytes 294920 | tf_op jit(solution)/shard_map/ppermute | solution.py:405
  52.2 2.0 %collective-permute-done.10.from_left = f32[192,128]{1,0:T(8,128)S(1)} collective-permute-done((f32[192,128]{1,0:T(8,128)S(1)}, f32[192,128]{1,0:T(8,128)S(1)}, u32[]{:S(2)}, u32[]{:S(2)}) %collective-permute-start.10) | collective-permute-done | bytes 98336 | tf_op jit(solution)/shard_map/ppermute | solution.py:405
  54.4 3.6 %collective-permute-start.12 = (f32[2,64,128]{2,1,0:T(8,128)S(1)}, f32[2,64,128]{2,1,0:T(8,128)S(1)}, u32[]{:S(2)}, u32[]{:S(2)}) collective-permute-start(f32[2,64,128]{2,1,0:T(8,128)S(1)} %get-tuple-element.37.after), channel_id=1, source_target_pairs={{0,32},{4,36},{8,40},{12,44},{16,48},{20,52},{24,56},{28,60},{32,0... | collective-permute-start | bytes 196616 | tf_op jit(solution)/shard_map/ppermute | solution.py:405
  57.9 0.7 sum.1
  58.6 4.2 %all-to-all-start.1 = ((f32[8,40,128]{2,1,0:T(8,128)}), f32[8,40,128]{2,1,0:T(8,128)S(1)}, u32[]{:S(2)}, u32[]{:S(2)}) async-start(f32[8,40,128]{2,1,0:T(8,128)} %sum.1), calls=%async_computation.1 | async-start | bytes 327680 | tf_op jit(solution)/shard_map/all_to_all | solution.py:490
  63.1 1.7 %collective-permute-start.15 = (f32[256,256]{1,0:T(8,128)S(1)}, f32[256,256]{1,0:T(8,128)S(1)}, u32[]{:S(2)}, u32[]{:S(2)}) collective-permute-start(f32[256,256]{1,0:T(8,128)S(1)} %finish.1.one.after), channel_id=1, source_target_pairs={{0,2},{1,3},{2,0},{3,1},{4,6},{5,7},{6,4},{7,5},{8,10},{9,11},{10,... | collective-permute-start | bytes 786440 | tf_op jit(solution)/shard_map/ppermute | solution.py:418
  64.9 1.4 %collective-permute-start.16 = (f32[256,256]{1,0:T(8,128)S(1)}, f32[256,256]{1,0:T(8,128)S(1)}, u32[]{:S(2)}, u32[]{:S(2)}) collective-permute-start(f32[256,256]{1,0:T(8,128)S(1)} %finish.1.one.after), channel_id=1, source_target_pairs={{0,3},{1,0},{2,1},{3,2},{4,7},{5,4},{6,5},{7,6},{8,11},{9,8},{10,9... | collective-permute-start | bytes 786440 | tf_op jit(solution)/shard_map/ppermute | solution.py:418
  66.3 4.9 %all-to-all-done.1.chunks = f32[8,40,128]{2,1,0:T(8,128)S(1)} async-done(((f32[8,40,128]{2,1,0:T(8,128)}), f32[8,40,128]{2,1,0:T(8,128)S(1)}, u32[]{:S(2)}, u32[]{:S(2)}) %all-to-all-start.1) | async-done | bytes 163872 | tf_op jit(solution)/shard_map/all_to_all | solution.py:490
  71.3 14.1 %all_to_all.15 = f32[16,32,128]{2,1,0:T(8,128)S(1)} all-to-all(f32[16,32,128]{2,1,0:T(8,128)S(1)} %mean.1), channel_id=1, replica_groups=mesh['x'=4,'core'=2,'tx'=8,'scan'=4] {'x','scan'}, dimensions={0} | all-to-all | bytes 524288 | tf_op jit(solution)/shard_map/all_to_all | solution.py:502
  85.4 1.9 %collective-permute-start.17 = (f32[512,128]{1,0:T(8,128)S(1)}, f32[512,128]{1,0:T(8,128)S(1)}, u32[]{:S(2)}, u32[]{:S(2)}) collective-permute-start(f32[512,128]{1,0:T(8,128)S(1)} %bitcast.10), channel_id=1, source_target_pairs={{0,32},{4,36},{8,40},{12,44},{16,48},{20,52},{24,56},{28,60},{32,0... | collective-permute-start | bytes 786440 | tf_op jit(solution)/shard_map/ppermute | solution.py:405
  87.3 1.1 %gather.1 = f32[4,256,256]{2,1,0:T(8,128)} custom-call(f32[256,256]{1,0:T(8,128)S(1)} %finish.1.one.after, f32[256,256]{1,0:T(8,128)S(1)} %collective-permute-done.14.two, f32[256,256]{1,0:T(8,128)S(1)} %collective-permute-done.15.three, f32[256,256]{1,0:T(8,128)S(1)} %collective-permute-done.16.four), custom_call_target="tpu_custom_call" | custom-call | flops 10000000000 | tf_op jit(solution)/shard_map/gather/pallas_call | solution.py:26
  88.5 0.8 halves.1
  (42 shorter events, 1.2 us)
Async XLA Ops:
  0.6 1.2 %copy-start = (f32[2,2,256,256]{3,2,1,0:T(8,128)S(1)}, f32[2,2,256,256]{3,2,1,0:T(8,128)}, u32[]{:S(2)}) copy-start(f32[2,2,256,256]{3,2,1,0:T(8,128)} %param.10) | copy-start | bytes 3145732
  2.0 13.8 %copy-start.9 = (f32[128,128]{1,0:T(8,128)S(1)}, f32[128,128]{1,0:T(8,128)}, u32[]{:S(2)}) copy-start(f32[128,128]{1,0:T(8,128)} %phase.3) | copy-start | bytes 196612
  2.0 4.5 %collective-permute-start = (f32[4,64,256]{2,1,0:T(8,128)S(1)}, f32[4,64,256]{2,1,0:T(8,128)S(1)}, u32[]{:S(2)}, u32[]{:S(2)}) collective-permute-start(f32[4,64,256]{2,1,0:T(8,128)S(1)} %get-tuple-element.21), channel_id=1, source_target_pairs={{0,32},{4,36},{8,40},{12,44},{16,48},{20,52},{24,56},{28,60},{32,0... | collective-permute-start | bytes 786440 | tf_op jit(solution)/shard_map/ppermute | solution.py:405
  6.7 17.2 %collective-permute-start.1 = (f32[4,160,128]{2,1,0:T(8,128)S(1)}, f32[4,160,128]{2,1,0:T(8,128)S(1)}, u32[]{:S(2)}, u32[]{:S(2)}) collective-permute-start(f32[4,160,128]{2,1,0:T(8,128)S(1)} %get-tuple-element.22), channel_id=1, source_target_pairs={{0,28},{4,0},{8,4},{12,8},{16,12},{20,16},{24,20},{28,24},{32,60},... | collective-permute-start | bytes 983048 | tf_op jit(solution)/shard_map/ppermute | solution.py:405
  10.6 13.3 %collective-permute-start.2 = (f32[4,160,128]{2,1,0:T(8,128)S(1)}, f32[4,160,128]{2,1,0:T(8,128)S(1)}, u32[]{:S(2)}, u32[]{:S(2)}) collective-permute-start(f32[4,160,128]{2,1,0:T(8,128)S(1)} %get-tuple-element.23), channel_id=1, source_target_pairs={{0,4},{4,8},{8,12},{12,16},{16,20},{20,24},{24,28},{28,0},{32,36},... | collective-permute-start | bytes 983048 | tf_op jit(solution)/shard_map/ppermute | solution.py:405
  10.6 13.3 %collective-permute-start.3 = (f32[4,64,256]{2,1,0:T(8,128)S(1)}, f32[4,64,256]{2,1,0:T(8,128)S(1)}, u32[]{:S(2)}, u32[]{:S(2)}) collective-permute-start(f32[4,64,256]{2,1,0:T(8,128)S(1)} %get-tuple-element.24.after), channel_id=1, source_target_pairs={{0,224},{4,228},{8,232},{12,236},{16,240},{20,244},{24,248},{28,25... | collective-permute-start | bytes 786440 | tf_op jit(solution)/shard_map/ppermute | solution.py:405
  12.4 6.4 %collective-permute-start.4 = (f32[4,32,128]{2,1,0:T(8,128)S(1)}, f32[4,32,128]{2,1,0:T(8,128)S(1)}, u32[]{:S(2)}, u32[]{:S(2)}) collective-permute-start(f32[4,32,128]{2,1,0:T(8,128)S(1)} %get-tuple-element.25), channel_id=1, source_target_pairs={{0,252},{4,224},{8,228},{12,232},{16,236},{20,240},{24,244},{28,24... | collective-permute-start | bytes 196616 | tf_op jit(solution)/shard_map/ppermute | solution.py:405
  15.1 8.8 %collective-permute-start.5 = (f32[4,32,128]{2,1,0:T(8,128)S(1)}, f32[4,32,128]{2,1,0:T(8,128)S(1)}, u32[]{:S(2)}, u32[]{:S(2)}) collective-permute-start(f32[4,32,128]{2,1,0:T(8,128)S(1)} %get-tuple-element.26), channel_id=1, source_target_pairs={{0,228},{4,232},{8,236},{12,240},{16,244},{20,248},{24,252},{28,22... | collective-permute-start | bytes 196616 | tf_op jit(solution)/shard_map/ppermute | solution.py:405
  15.7 8.2 %copy-start.1 = (f32[2,2,256,256]{3,2,1,0:T(8,128)S(1)}, f32[2,2,256,256]{3,2,1,0:T(8,128)}, u32[]{:S(2)}) copy-start(f32[2,2,256,256]{3,2,1,0:T(8,128)} %param.10) | copy-start | bytes 3145732
  15.7 8.2 %copy-start.2 = (f32[4,2,128,128]{3,2,1,0:T(8,128)S(1)}, f32[4,2,128,128]{3,2,1,0:T(8,128)}, u32[]{:S(2)}) copy-start(f32[4,2,128,128]{3,2,1,0:T(8,128)} %param.11) | copy-start | bytes 1572868
  15.8 8.2 %copy-start.3 = (f32[1,1,2,128,128]{4,3,2,1,0:T(8,128)S(1)}, f32[1,1,2,128,128]{4,3,2,1,0:T(8,128)}, u32[]{:S(2)}) copy-start(f32[1,1,2,128,128]{4,3,2,1,0:T(8,128)} %param.15) | copy-start | bytes 393220
  15.8 8.2 %copy-start.4 = (bf16[256,256]{1,0:T(8,128)(2,1)S(1)}, bf16[256,256]{1,0:T(8,128)(2,1)}, u32[]{:S(2)}) copy-start(bf16[256,256]{1,0:T(8,128)(2,1)} %constant.8.clone.right_high) | copy-start | bytes 393220
  15.8 8.2 %copy-start.5 = (bf16[256,256]{1,0:T(8,128)(2,1)S(1)}, bf16[256,256]{1,0:T(8,128)(2,1)}, u32[]{:S(2)}) copy-start(bf16[256,256]{1,0:T(8,128)(2,1)} %constant.9.clone.right_low) | copy-start | bytes 393220
  15.8 8.2 %copy-start.6 = (bf16[256,256]{1,0:T(8,128)(2,1)S(1)}, bf16[256,256]{1,0:T(8,128)(2,1)}, u32[]{:S(2)}) copy-start(bf16[256,256]{1,0:T(8,128)(2,1)} %constant.10.clone.left_high) | copy-start | bytes 393220
  15.8 8.2 %copy-start.7 = (bf16[256,256]{1,0:T(8,128)(2,1)S(1)}, bf16[256,256]{1,0:T(8,128)(2,1)}, u32[]{:S(2)}) copy-start(bf16[256,256]{1,0:T(8,128)(2,1)} %constant.11.clone.left_low) | copy-start | bytes 393220
  23.9 0.7 copy-start.8
  31.4 5.9 %collective-permute-start.9 = (f32[520,128]{1,0:T(8,128)S(1)}, f32[520,128]{1,0:T(8,128)S(1)}, u32[]{:S(2)}, u32[]{:S(2)}) collective-permute-start(f32[520,128]{1,0:T(8,128)S(1)} %get-tuple-element.34), channel_id=1, source_target_pairs={{0,32},{4,36},{8,40},{12,44},{16,48},{20,52},{24,56},{28,60},{32,0... | collective-permute-start | bytes 798728 | tf_op jit(solution)/shard_map/ppermute | solution.py:405
  32.3 9.3 %collective-permute-start.6 = (f32[264,128]{1,0:T(8,128)S(1)}, f32[264,128]{1,0:T(8,128)S(1)}, u32[]{:S(2)}, u32[]{:S(2)}) collective-permute-start(f32[264,128]{1,0:T(8,128)S(1)} %get-tuple-element.30), channel_id=1, source_target_pairs={{0,1},{1,2},{2,3},{3,0},{4,5},{5,6},{6,7},{7,4},{8,9},{9,10},{10,1... | collective-permute-start | bytes 405512 | tf_op jit(solution)/shard_map/ppermute | solution.py:418
  33.6 9.2 %collective-permute-start.7 = (f32[264,128]{1,0:T(8,128)S(1)}, f32[264,128]{1,0:T(8,128)S(1)}, u32[]{:S(2)}, u32[]{:S(2)}) collective-permute-start(f32[264,128]{1,0:T(8,128)S(1)} %get-tuple-element.31), channel_id=1, source_target_pairs={{0,2},{1,3},{2,0},{3,1},{4,6},{5,7},{6,4},{7,5},{8,10},{9,11},{10,... | collective-permute-start | bytes 405512 | tf_op jit(solution)/shard_map/ppermute | solution.py:418
  36.2 6.6 %collective-permute-start.8 = (f32[264,128]{1,0:T(8,128)S(1)}, f32[264,128]{1,0:T(8,128)S(1)}, u32[]{:S(2)}, u32[]{:S(2)}) collective-permute-start(f32[264,128]{1,0:T(8,128)S(1)} %get-tuple-element.32), channel_id=1, source_target_pairs={{0,3},{1,0},{2,1},{3,2},{4,7},{5,4},{6,5},{7,6},{8,11},{9,8},{10,9... | collective-permute-start | bytes 405512 | tf_op jit(solution)/shard_map/ppermute | solution.py:418
  38.1 11.3 %all-to-all-start = ((f32[16,40,128]{2,1,0:T(8,128)}), f32[16,40,128]{2,1,0:T(8,128)S(1)}, u32[]{:S(2)}, u32[]{:S(2)}) async-start(f32[16,40,128]{2,1,0:T(8,128)} %spread.1), calls=%async_computation | async-start | bytes 655360 | tf_op jit(solution)/shard_map/all_to_all | solution.py:463
  49.5 4.8 %collective-permute-start.10 = (f32[192,128]{1,0:T(8,128)S(1)}, f32[192,128]{1,0:T(8,128)S(1)}, u32[]{:S(2)}, u32[]{:S(2)}) collective-permute-start(f32[192,128]{1,0:T(8,128)S(1)} %get-tuple-element.35), channel_id=1, source_target_pairs={{0,4},{4,8},{8,12},{12,16},{16,20},{20,24},{24,28},{28,0},{32,36},... | collective-permute-start | bytes 294920 | tf_op jit(solution)/shard_map/ppermute | solution.py:405
  49.5 4.7 %collective-permute-start.11 = (f32[192,128]{1,0:T(8,128)S(1)}, f32[192,128]{1,0:T(8,128)S(1)}, u32[]{:S(2)}, u32[]{:S(2)}) collective-permute-start(f32[192,128]{1,0:T(8,128)S(1)} %get-tuple-element.36), channel_id=1, source_target_pairs={{0,28},{4,0},{8,4},{12,8},{16,12},{20,16},{24,20},{28,24},{32,60},... | collective-permute-start | bytes 294920 | tf_op jit(solution)/shard_map/ppermute | solution.py:405
  54.4 8.5 %collective-permute-start.12 = (f32[2,64,128]{2,1,0:T(8,128)S(1)}, f32[2,64,128]{2,1,0:T(8,128)S(1)}, u32[]{:S(2)}, u32[]{:S(2)}) collective-permute-start(f32[2,64,128]{2,1,0:T(8,128)S(1)} %get-tuple-element.37.after), channel_id=1, source_target_pairs={{0,32},{4,36},{8,40},{12,44},{16,48},{20,52},{24,56},{28,60},{32,0... | collective-permute-start | bytes 196616 | tf_op jit(solution)/shard_map/ppermute | solution.py:405
  57.9 4.9 %collective-permute-start.13 = (f32[2,64,128]{2,1,0:T(8,128)S(1)}, f32[2,64,128]{2,1,0:T(8,128)S(1)}, u32[]{:S(2)}, u32[]{:S(2)}) collective-permute-start(f32[2,64,128]{2,1,0:T(8,128)S(1)} %get-tuple-element.38), channel_id=1, source_target_pairs={{0,224},{4,228},{8,232},{12,236},{16,240},{20,244},{24,248},{28,25... | collective-permute-start | bytes 196616 | tf_op jit(solution)/shard_map/ppermute | solution.py:405
  58.6 12.6 %all-to-all-start.1 = ((f32[8,40,128]{2,1,0:T(8,128)}), f32[8,40,128]{2,1,0:T(8,128)S(1)}, u32[]{:S(2)}, u32[]{:S(2)}) async-start(f32[8,40,128]{2,1,0:T(8,128)} %sum.1), calls=%async_computation.1 | async-start | bytes 327680 | tf_op jit(solution)/shard_map/all_to_all | solution.py:490
  62.9 24.4 %collective-permute-start.14 = (f32[256,256]{1,0:T(8,128)S(1)}, f32[256,256]{1,0:T(8,128)S(1)}, u32[]{:S(2)}, u32[]{:S(2)}) collective-permute-start(f32[256,256]{1,0:T(8,128)S(1)} %finish.1.one.after), channel_id=1, source_target_pairs={{0,1},{1,2},{2,3},{3,0},{4,5},{5,6},{6,7},{7,4},{8,9},{9,10},{10,1... | collective-permute-start | bytes 786440 | tf_op jit(solution)/shard_map/ppermute | solution.py:418
  63.1 24.2 %collective-permute-start.15 = (f32[256,256]{1,0:T(8,128)S(1)}, f32[256,256]{1,0:T(8,128)S(1)}, u32[]{:S(2)}, u32[]{:S(2)}) collective-permute-start(f32[256,256]{1,0:T(8,128)S(1)} %finish.1.one.after), channel_id=1, source_target_pairs={{0,2},{1,3},{2,0},{3,1},{4,6},{5,7},{6,4},{7,5},{8,10},{9,11},{10,... | collective-permute-start | bytes 786440 | tf_op jit(solution)/shard_map/ppermute | solution.py:418
  64.9 22.4 %collective-permute-start.16 = (f32[256,256]{1,0:T(8,128)S(1)}, f32[256,256]{1,0:T(8,128)S(1)}, u32[]{:S(2)}, u32[]{:S(2)}) collective-permute-start(f32[256,256]{1,0:T(8,128)S(1)} %finish.1.one.after), channel_id=1, source_target_pairs={{0,3},{1,0},{2,1},{3,2},{4,7},{5,4},{6,5},{7,6},{8,11},{9,8},{10,9... | collective-permute-start | bytes 786440 | tf_op jit(solution)/shard_map/ppermute | solution.py:418
  85.4 3.1 %collective-permute-start.17 = (f32[512,128]{1,0:T(8,128)S(1)}, f32[512,128]{1,0:T(8,128)S(1)}, u32[]{:S(2)}, u32[]{:S(2)}) collective-permute-start(f32[512,128]{1,0:T(8,128)S(1)} %bitcast.10), channel_id=1, source_target_pairs={{0,32},{4,36},{8,40},{12,44},{16,48},{20,52},{24,56},{28,60},{32,0... | collective-permute-start | bytes 786440 | tf_op jit(solution)/shard_map/ppermute | solution.py:405

commit v3 on v2

--- a/solution.py
+++ b/solution.py
@@ -54,7 +54,16 @@
     right[...] = jnp.where(short, swap(upper[:, W:]), lower[:, W:])
 
 
-def pack_body(tile, to_core, to_far, far_left, far_right):
+def sides_body(tile, to_left, to_right):
+    wide = low_lanes(W)
+    for part in range(4):
+        first, second = tile[part, :W, :W], tile[part, W:, :W]
+        to_left[part] = jnp.where(wide, first, swap(second))
+        first, second = tile[part, :W, W:], tile[part, W:, W:]
+        to_right[part] = jnp.where(wide, swap(first), second)
+
+
+def strips_body(tile, after, to_core, to_far, far_left, far_right):
     core_row, far_row = rim_rows(lax.axis_index("core"), TILE - HALF)
     for part in range(4):
         to_core[part] = tile[part, pl.ds(core_row, HALF), :]
@@ -63,18 +72,18 @@
         fold_corner(rows, far_left.at[part], far_right.at[part])
 
 
-def sides_body(tile, from_core, to_left, to_right):
-    wide = low_lanes(W)
+def corners_body(from_right, from_left, far, far_right, far_left, out):
+    core = lax.axis_index("core")
+    low = low_lanes(HALF)
+    span = pl.ds(pl.multiple_of((1 - core) * HALF, HALF), HALF)
     for part in range(4):
-        first, second = tile[part, :W, :W], tile[part, W:, :W]
-        to_left[part, :W] = jnp.where(wide, first, swap(second))
-        first, second = tile[part, :W, W:], tile[part, W:, W:]
-        to_right[part, :W] = jnp.where(wide, swap(first), second)
-        corners = slice(W, W + HALF // 2)
-        fold_corner(from_core[part], to_left.at[part, corners], to_right.at[part, corners])
-
-
-def phase_body(phase, after, real, imag):
+        right, left = from_right[part, span], from_left[part, span]
+        right = jnp.where(core == 0, swap(right), right)
+        left = jnp.where(core == 0, left, swap(left))
+        out[part] = jnp.where(low, right, left)
+
+
+def phase_body(phase, right, left, real, imag):
     real[...] = jnp.cos(phase[...])
     imag[...] = jnp.sin(phase[...])
 
@@ -111,7 +120,7 @@
 
 
 def slots_body(
-    offsets,
+    starts,
     live_counts,
     tile,
     from_right,
@@ -120,6 +129,7 @@
     from_far,
     far_right,
     far_left,
+    corners,
     probe,
     kernel_real,
     kernel_imag,
@@ -148,23 +158,20 @@
     for part in range(4):
         wide[part, 0, HALF : HALF + TILE] = tile[part, :, :W]
         wide[part, 1, HALF : HALF + TILE] = tile[part, :, W:]
-        right, left = from_right[part, :W], from_left[part, :W]
+        right, left = from_right[part], from_left[part]
         wide[part, 2, HALF : HALF + W] = jnp.where(tall, right, swap(left))
         wide[part, 2, HALF + W : HALF + TILE] = jnp.where(tall, swap(right), left)
-        for row, strip, right, left in (
-            (core_row, from_core, from_right[part, W:], from_left[part, W:]),
-            (far_row, from_far, far_right[part], far_left[part]),
-        ):
+        for row, strip in ((core_row, from_core), (far_row, from_far)):
             wide[part, 0, pl.ds(row, HALF)] = strip[part, :, :W]
             wide[part, 1, pl.ds(row, HALF)] = strip[part, :, W:]
-            wide[part, 2, pl.ds(row, HALF // 2)] = jnp.where(short, right, swap(left))
-            lower = pl.multiple_of(row + HALF // 2, HALF // 2)
-            wide[part, 2, pl.ds(lower, HALF // 2)] = jnp.where(short, swap(right), left)
+        wide[part, 2, pl.ds(core_row, HALF)] = corners[part]
+        right, left = far_right[part], far_left[part]
+        wide[part, 2, pl.ds(far_row, HALF // 2)] = jnp.where(short, right, swap(left))
+        lower = pl.multiple_of(far_row + HALF // 2, HALF // 2)
+        wide[part, 2, pl.ds(lower, HALF // 2)] = jnp.where(short, swap(right), left)
 
     def corner(slot):
-        row = jnp.clip(offsets[0, 0, slot, 0] + HALF, 0, TILE)
-        col = jnp.clip(offsets[0, 0, slot, 1], -HALF, TILE - HALF)
-        return row, jnp.where(col < 0, col + 3 * W, col)
+        return starts[2 * slot], starts[2 * slot + 1]
 
     forward_right = jnp.concatenate([right_high[...], right_high[...], right_low[...]], axis=0)
     inverse_right = jnp.concatenate([left_high[...], left_high[...], left_low[...]], axis=0)
@@ -277,28 +284,23 @@
         out[k, rows:] = count
 
 
-def total_of(chunks):
-    total = chunks[0]
-    for k in range(1, chunks.shape[0]):
-        total = total + chunks[k]
-    return total
-
-
-def sum_body(chunks, after, spread):
-    total = total_of(chunks)
-    for k in range(spread.shape[0]):
-        spread[k] = total
-
-
-def mean_body(chunks, after, spread):
-    total = total_of(chunks)
+def sum_body(chunks, after, out):
+    out[...] = functools.reduce(jnp.add, [chunks[k] for k in range(chunks.shape[0])])
+
+
+def group_body(zero, one, two, three, after, out):
+    out[...] = (zero[...] + one[...]) + (two[...] + three[...])
+
+
+def mean_body(own, got, spread):
+    total = own[...] + got[...]
     rows = spread.shape[1]
     mean = total[:rows] / total[rows : rows + 1]
     for k in range(spread.shape[0]):
         spread[k] = mean
 
 
-def place_body(one, two, three, four, wide):
+def place_body(one, two, three, four, to_left, to_right, wide):
     wide[...] = jnp.zeros_like(wide)
     lanes = lax.broadcasted_iota(jnp.int32, (W, W), 1)
     for message in (one, two, three, four):
@@ -314,9 +316,6 @@
             turned = pltpu.roll(message[W * slot : W * (slot + 1)], shift, 1)
             wide[block, pl.ds(row, W)] += jnp.where(lanes >= shift, turned, 0.0)
             wide[after, pl.ds(row, W)] += jnp.where(lanes < shift, turned, 0.0)
-
-
-def edges_body(wide, after, to_left, to_right):
     half = (TILE + 2 * HALF) // 2
     low = low_lanes(half)
     upper, lower = wide[2, :half], wide[2, half:]
@@ -324,7 +323,7 @@
     to_left[...] = jnp.where(low, swap(upper), lower)
 
 
-def rows_body(from_left, from_right, held, to_core, to_far, keep, wide):
+def rows_body(from_left, from_right, held, after, to_core, to_far, keep, wide):
     half = (TILE + 2 * HALF) // 2
     low = low_lanes(half)
     left, right = from_left[...], from_right[...]
@@ -339,7 +338,7 @@
         keep[k] = wide[k, HALF : HALF + TILE]
 
 
-def finish_body(from_core, from_far, held, out):
+def finish_body(from_core, from_far, held, after, out):
     core_row, far_row = rim_rows(lax.axis_index("core"), TILE - HALF)
     for k in range(2):
         span = slice(k * W, (k + 1) * W)
@@ -348,16 +347,39 @@
         out[pl.ds(far_row, HALF), span] += from_far[k]
 
 
-def gather_body(one, two, three, four, out):
+def copy_all(pairs, sems):
+    copies = [
+        pltpu.make_async_copy(source, target, sems.at[k])
+        for k, (source, target) in enumerate(pairs)
+    ]
+    for copy in copies:
+        copy.start()
+    for copy in copies:
+        copy.wait()
+
+
+def gather_body(one, two, three, four, out, sems):
     scan = lax.axis_index("scan")
-    for step, part in enumerate((one, two, three, four)):
-        out[lax.rem(scan + 4 - step, 4)] = part[...]
-
-
-def halves_body(mine, other, out):
+    parts = enumerate((one, two, three, four))
+    copy_all([(part, out.at[lax.rem(scan + 4 - step, 4)]) for step, part in parts], sems)
+
+
+def halves_body(mine, other, out, sems):
     core = lax.axis_index("core")
-    out[core] = mine[...]
-    out[1 - core] = other[...]
+    copy_all([(mine, out.at[core]), (other, out.at[1 - core])], sems)
+
+
+def place_parts(body, shape, parts, name):
+    return pl.pallas_call(
+        body,
+        out_shape=jax.ShapeDtypeStruct(shape, F32),
+        in_specs=[ANY] * len(parts),
+        out_specs=ANY,
+        scratch_shapes=[pltpu.SemaphoreType.DMA((len(parts),))],
+        compiler_params=PARAMS,
+        cost_estimate=pl.CostEstimate(flops=LONG, bytes_accessed=0, transcendentals=0),
+        name=name,
+    )(*parts)
 
 
 def tables():
@@ -380,7 +402,7 @@
         slots_body,
         [message] * 4 + [share] * 2,
         (*args, *tables()),
-        [SMEM] * 2 + [VMEM] * 15,
+        [SMEM] * 2 + [VMEM] * 16,
         scratch=[
             pltpu.VMEM((4, 3, TILE + 2 * HALF, W), F32),
             pltpu.VMEM((4, 2, W, W), F32),
@@ -417,23 +439,45 @@
     def to_scan(value, step):
         return lax.ppermute(value, "scan", [(s, (s + step) % nsc) for s in range(nsc)])
 
+    def to_pair(value, mask):
+        return lax.ppermute(value, "tx", [(t, t ^ mask) for t in range(ntx)])
+
     tile = specimen.reshape(4, TILE, TILE)
-    strip, corner, side = (4, HALF, TILE), (4, HALF // 2, W), (4, W + HALF // 2, W)
-    near, far, left, right = call(
-        pack_body, [strip, strip, corner, corner], (tile,), [VMEM], name="pack"
-    )
-    marker = far
-    from_core = to_core(near)
-    from_far, corner_right, corner_left = to_far(far), far_left(left), far_right(right)
-    left, right = call(
-        sides_body, [side, side], (tile, from_core), [VMEM] * 2, name="sides", flops=LONG
+    strip, corner, side = (4, HALF, TILE), (4, HALF // 2, W), (4, W, W)
+    left, right = call(sides_body, [side, side], (tile,), [VMEM], name="sides")
+    near, far, corner_left, corner_right = call(
+        strips_body,
+        [strip, strip, corner, corner],
+        (tile, left),
+        [VMEM, ANY],
+        name="strips",
+        flops=LONG,
     )
     from_right, from_left = to_left(left), to_right(right)
+    from_core, from_far = to_core(near), to_far(far)
+    corner_right, corner_left = far_left(corner_left), far_right(corner_right)
     kernel_real, kernel_imag = call(
-        phase_body, [(W, W)] * 2, (kernel_phase, marker), [VMEM, ANY], name="phase", flops=10**9
-    )
+        phase_body,
+        [(W, W)] * 2,
+        (kernel_phase, from_right, from_left),
+        [VMEM] + [ANY] * 2,
+        name="phase",
+        flops=LONG,
+    )
+    (corners,) = call(
+        corners_body,
+        [(4, HALF, W)],
+        (from_right, from_left, from_far, corner_right, corner_left),
+        [VMEM] * 2 + [ANY] * 3,
+        name="corners",
+        flops=LONG,
+    )
+    corners = to_core(corners)
+    rows = jnp.clip(offsets[0, 0, :, 0] + HALF, 0, TILE)
+    cols = jnp.clip(offsets[0, 0, :, 1], -HALF, TILE - HALF)
+    starts = jnp.stack([rows, jnp.where(cols < 0, cols + 3 * W, cols)], axis=1).reshape(4)
     outs = run_slots(
-        offsets,
+        starts,
         live_counts,
         tile,
         from_right,
@@ -442,6 +486,7 @@
         from_far,
         corner_right,
         corner_left,
+        corners,
         probe_modes.reshape(2 * MODES, W, W),
         kernel_real,
         kernel_imag,
@@ -450,11 +495,11 @@
     own, away, probe_send, probe_keep = outs[0], outs[1:4], outs[4], outs[5]
     arrived = [to_scan(value, step) for step, value in enumerate(away, 1)]
     probe_got = to_core(probe_send)
-    group = nx * nsc
-    rows_each = MODES * W // group
+    peers = nx * nsc
+    rows = MODES * W // peers
     (chunks,) = call(
         spread_body,
-        [(group, rows_each + 8, W)],
+        [(peers, rows + 8, W)],
         (probe_keep, probe_got),
         [VMEM] * 2,
         name="spread",
@@ -462,50 +507,54 @@
     )
     chunks = lax.all_to_all(chunks, ("x", "scan"), 0, 0)
     tall = TILE + 2 * HALF
-    (held,) = call(
-        place_body, [(3, tall, W)], (own, *arrived), [VMEM] * 4, name="place", flops=LONG
-    )
-    left, right = call(
-        edges_body, [(tall // 2, W)] * 2, (held, chunks), [VMEM, ANY], name="edges"
+    left, right, held = call(
+        place_body,
+        [(tall // 2, W)] * 2 + [(3, tall, W)],
+        (own, *arrived),
+        [VMEM] * 4,
+        name="place",
+        flops=LONG,
+    )
+    (share,) = call(
+        sum_body, [(rows + 8, W)], (chunks, left), [VMEM, ANY], name="sum", flops=LONG
     )
     left, right = to_left(left), to_right(right)
+    group = [share] + [to_pair(share, mask) for mask in range(1, 4)]
     near, far, held = call(
         rows_body,
         [(2, HALF, W)] * 2 + [(2, TILE, W)],
-        (right, left, held),
-        [VMEM] * 3,
+        (right, left, held, share),
+        [VMEM] * 3 + [ANY],
         scratch=[pltpu.VMEM((2, tall, W), F32)],
         name="rows",
         flops=LONG,
     )
-    (spread,) = call(
-        sum_body,
-        [(ntx, rows_each + 8, W)],
-        (chunks, near),
-        [VMEM, ANY],
-        name="sum",
-        flops=LONG,
+    (share,) = call(
+        group_body, [(rows + 8, W)], (*group, near), [VMEM] * 4 + [ANY], name="group", flops=LONG
     )
     near, far = to_core(near), to_far(far)
-    spread = lax.all_to_all(spread, "tx", 0, 0)
     (quarter,) = call(
-        finish_body, [(TILE, TILE)], (near, far, held), [VMEM] * 3, name="finish", flops=LONG
-    )
+        finish_body,
+        [(TILE, TILE)],
+        (near, far, held, share),
+        [VMEM] * 3 + [ANY],
+        name="finish",
+        flops=LONG,
+    )
+    quarters = [quarter] + [to_scan(quarter, step) for step in range(1, nsc)]
+    got = to_pair(share, ntx - 1)
     (spread,) = call(
         mean_body,
-        [(group, rows_each, W)],
-        (spread, quarter),
-        [VMEM, ANY],
+        [(peers, rows, W)],
+        (share, got),
+        [VMEM] * 2,
         name="mean",
         flops=LONG,
     )
     mine = lax.all_to_all(spread, ("x", "scan"), 0, 0).reshape(MODES * W, W)
-    quarters = [quarter] + [to_scan(quarter, step) for step in range(1, nsc)]
     other = to_core(mine)
-    (probe_grad,) = call(
-        halves_body, [(2, MODES * W, W)], (mine, other), [VMEM] * 2, name="halves", flops=LONG
-    )
-    (object_grad,) = call(gather_body, [(4, TILE, TILE)], quarters, [VMEM] * 4, name="gather", flops=LONG)
+    probe_grad = place_parts(halves_body, (2, MODES * W, W), (mine, other), "halves")
+    object_grad = place_parts(gather_body, (4, TILE, TILE), quarters, "gather")
     return object_grad.reshape(specimen.shape), probe_grad.reshape(probe_modes.shape)
 
 

time: 89.7 us -> 80.4 us (0.90)
  waiting for transfers between devices: 23.1 us -> 11.2 us
  starting transfers between devices: 37 us -> 40.3 us
    all_to_all x1 -> x0, waiting for transfers between devices: 4.91 us -> none  [per_device(): spread = lax.all_to_all(spread, 'tx', 0, 0)]
    all_to_all x1 -> x0, starting transfers between devices: 4.23 us -> none  [per_device(): spread = lax.all_to_all(spread, 'tx', 0, 0)]
    ppermute x12 -> x13, waiting for transfers between devices: 10.9 us -> 6.96 us  [over_grid(): return lambda value: lax.ppermute(value, ('x', 'core', 'tx'), pairs)]
    ppermute x12 -> x13, starting transfers between devices: 20.8 us -> 24.7 us  [over_grid(): return lambda value: lax.ppermute(value, ('x', 'core', 'tx'), pairs)]
    ppermute x0 -> x4, starting transfers between devices: none -> 3.71 us  [to_pair(): return lax.ppermute(value, 'tx', [(t, t ^ mask) for t in range(ntx)])]
    all_to_all x1, waiting for transfers between devices: 6.1 us -> 3.27 us  [per_device(): chunks = lax.all_to_all(chunks, ('x', 'scan'), 0, 0)]
    pallas_call x13 -> x12, Pallas kernels: 11.7 us -> 9.4 us  [call(): pl.pallas_call(body, out_shape=[jax.ShapeDtypeStruct(shape, F32) for shap...]
    pallas_call x0 -> x2, Pallas kernels: none -> 1.81 us  [place_parts(): pl.pallas_call(body, out_shape=jax.ShapeDtypeStruct(shape, F32), in_specs...]
  transfers between devices with their start and end apart: 20 -> 24, of which waited for: 8 -> 8; matrix products, arithmetic and copies ran while one was open for 0% -> 0% of each run, Pallas kernels for 4% -> 4%
where the time goes in v3:
time: 80.4 us; the launch traced here: 80.1 us
  starting transfers between devices  40.3 us (50%)
  blocking collectives  14 us (17%)
  Pallas kernels  11.2 us (14%)
  waiting for transfers between devices  11.2 us (14%)
  between operations  1.73 us (2%)
  local copies, waits for them, and re-layouts  1.45 us (2%)
    ppermute x13, starting transfers between devices, over_grid(): return lambda value: lax.ppermute(value, ('x', 'core', 'tx'), pairs)  24.7 us
    all_to_all x1, blocking collectives, per_device(): mine = lax.all_to_all(spread, ('x', 'scan'), 0, 0).reshape(MODES * W, W)  14 us
    pallas_call x12, Pallas kernels, call(): pl.pallas_call(body, out_shape=[jax.ShapeDtypeStruct(shape, F32) for shap...  9.4 us
    ppermute x6, starting transfers between devices, to_scan(): lax.ppermute(value, 'scan', [(s, (s + step) % nsc) for s in range(nsc)])  8.3 us
    ppermute x13, waiting for transfers between devices, over_grid(): return lambda value: lax.ppermute(value, ('x', 'core', 'tx'), pairs)  6.96 us
    ppermute x4, starting transfers between devices, to_pair(): return lax.ppermute(value, 'tx', [(t, t ^ mask) for t in range(ntx)])  3.71 us
    all_to_all x1, starting transfers between devices, per_device(): chunks = lax.all_to_all(chunks, ('x', 'scan'), 0, 0)  3.54 us
    all_to_all x1, waiting for transfers between devices, per_device(): chunks = lax.all_to_all(chunks, ('x', 'scan'), 0, 0)  3.27 us
  transfers between devices with their start and end apart: 24, of which 8 were waited for; matrix products, arithmetic and copies ran while one was open for 0% of the time, Pallas kernels for 4%

profile of v3, /device:TPU:1, one launch (start us, length us, event | category | flops | bytes accessed | tf_op | source)
XLA Modules:
  0.0 80.1 jit_solution(46866151745542596)
XLA Ops:
  0.6 1.2 %copy-done = f32[2,2,256,256]{3,2,1,0:T(8,128)S(1)} copy-done((f32[2,2,256,256]{3,2,1,0:T(8,128)S(1)}, f32[2,2,256,256]{3,2,1,0:T(8,128)}, u32[]{:S(2)}) %copy-start) | copy-done | bytes 1048600
  2.1 6.5 %collective-permute-start = (f32[4,128,128]{2,1,0:T(8,128)S(1)}, f32[4,128,128]{2,1,0:T(8,128)S(1)}, u32[]{:S(2)}, u32[]{:S(2)}) collective-permute-start(f32[4,128,128]{2,1,0:T(8,128)S(1)} %get-tuple-element.22.after), channel_id=1, source_target_pairs={{0,28},{4,0},{8,4},{12,8},{16,12},{20,16},{24,20},{28,24},{32,60},... | collective-permute-start | bytes 786440 | tf_op jit(solution)/shard_map/ppermute | solution.py:427
  8.7 2.1 %collective-permute-start.3 = (f32[4,64,256]{2,1,0:T(8,128)S(1)}, f32[4,64,256]{2,1,0:T(8,128)S(1)}, u32[]{:S(2)}, u32[]{:S(2)}) collective-permute-start(f32[4,64,256]{2,1,0:T(8,128)S(1)} %get-tuple-element.25), channel_id=1, source_target_pairs={{0,224},{4,228},{8,232},{12,236},{16,240},{20,244},{24,248},{28,25... | collective-permute-start | bytes 786440 | tf_op jit(solution)/shard_map/ppermute | solution.py:427
  10.8 2.8 %collective-permute-start.4 = (f32[4,32,128]{2,1,0:T(8,128)S(1)}, f32[4,32,128]{2,1,0:T(8,128)S(1)}, u32[]{:S(2)}, u32[]{:S(2)}) collective-permute-start(f32[4,32,128]{2,1,0:T(8,128)S(1)} %get-tuple-element.26), channel_id=1, source_target_pairs={{0,252},{4,224},{8,228},{12,232},{16,236},{20,240},{24,244},{28,24... | collective-permute-start | bytes 196616 | tf_op jit(solution)/shard_map/ppermute | solution.py:427
  14.6 1.1 %collective-permute-done.4.far_right = f32[4,32,128]{2,1,0:T(8,128)S(1)} collective-permute-done((f32[4,32,128]{2,1,0:T(8,128)S(1)}, f32[4,32,128]{2,1,0:T(8,128)S(1)}, u32[]{:S(2)}, u32[]{:S(2)}) %collective-permute-start.4) | collective-permute-done | bytes 65568 | tf_op jit(solution)/shard_map/ppermute | solution.py:427
  15.7 2.4 %collective-permute-start.2 = (f32[4,64,256]{2,1,0:T(8,128)S(1)}, f32[4,64,256]{2,1,0:T(8,128)S(1)}, u32[]{:S(2)}, u32[]{:S(2)}) collective-permute-start(f32[4,64,256]{2,1,0:T(8,128)S(1)} %get-tuple-element.24), channel_id=1, source_target_pairs={{0,32},{4,36},{8,40},{12,44},{16,48},{20,52},{24,56},{28,60},{32,0... | collective-permute-start | bytes 786440 | tf_op jit(solution)/shard_map/ppermute | solution.py:427
  18.1 1.4 %collective-permute-done.5.far_left = f32[4,32,128]{2,1,0:T(8,128)S(1)} collective-permute-done((f32[4,32,128]{2,1,0:T(8,128)S(1)}, f32[4,32,128]{2,1,0:T(8,128)S(1)}, u32[]{:S(2)}, u32[]{:S(2)}) %collective-permute-start.5) | collective-permute-done | bytes 65568 | tf_op jit(solution)/shard_map/ppermute | solution.py:427
  19.7 3.0 %collective-permute-start.6 = (f32[4,64,128]{2,1,0:T(8,128)S(1)}, f32[4,64,128]{2,1,0:T(8,128)S(1)}, u32[]{:S(2)}, u32[]{:S(2)}) collective-permute-start(f32[4,64,128]{2,1,0:T(8,128)S(1)} %corners.1), channel_id=1, source_target_pairs={{0,32},{4,36},{8,40},{12,44},{16,48},{20,52},{24,56},{28,60},{32,0... | collective-permute-start | bytes 393224 | tf_op jit(solution)/shard_map/ppermute | solution.py:427
  22.7 0.4 phase.2
  23.1 0.5 collective-permute-done.6.corners
  23.7 6.8 %slots.1 = (f32[264,128]{1,0:T(8,128)S(1)}, f32[264,128]{1,0:T(8,128)S(1)}, f32[264,128]{1,0:T(8,128)S(1)}, f32[264,128]{1,0:T(8,128)S(1)}, f32[520,128]{1,0:T(8,128)S(1)}, /*index=5*/f32[520,128]{1,0:T(8,128)S(1)}) custom-call(s32[4]{0:T(128)S(1)} %reshape.62.starts, s32[1,1,1]{2,1,0:T(1,128)S(6)} %copy.13.live_counts, f32[4,256,256]{2,1,0:T(8,128)S(1)} %bitcast.11, ...), custom_call_target="tpu_custom_call" | custom-call | tf_op jit(solution)/shard_map/slots/pallas_call | solution.py:26
  30.5 0.5 collective-permute-start.12
  31.0 1.3 %collective-permute-start.7 = (f32[264,128]{1,0:T(8,128)S(1)}, f32[264,128]{1,0:T(8,128)S(1)}, u32[]{:S(2)}, u32[]{:S(2)}) collective-permute-start(f32[264,128]{1,0:T(8,128)S(1)} %get-tuple-element.31), channel_id=1, source_target_pairs={{0,1},{1,2},{2,3},{3,0},{4,5},{5,6},{6,7},{7,4},{8,9},{9,10},{10,1... | collective-permute-start | bytes 405512 | tf_op jit(solution)/shard_map/ppermute | solution.py:440
  32.3 2.6 %collective-permute-start.8 = (f32[264,128]{1,0:T(8,128)S(1)}, f32[264,128]{1,0:T(8,128)S(1)}, u32[]{:S(2)}, u32[]{:S(2)}) collective-permute-start(f32[264,128]{1,0:T(8,128)S(1)} %get-tuple-element.32), channel_id=1, source_target_pairs={{0,2},{1,3},{2,0},{3,1},{4,6},{5,7},{6,4},{7,5},{8,10},{9,11},{10,... | collective-permute-start | bytes 405512 | tf_op jit(solution)/shard_map/ppermute | solution.py:440
  34.9 1.1 %collective-permute-start.9 = (f32[264,128]{1,0:T(8,128)S(1)}, f32[264,128]{1,0:T(8,128)S(1)}, u32[]{:S(2)}, u32[]{:S(2)}) collective-permute-start(f32[264,128]{1,0:T(8,128)S(1)} %get-tuple-element.33), channel_id=1, source_target_pairs={{0,3},{1,0},{2,1},{3,2},{4,7},{5,4},{6,5},{7,6},{8,11},{9,8},{10,9... | collective-permute-start | bytes 405512 | tf_op jit(solution)/shard_map/ppermute | solution.py:440
  36.0 0.8 spread.1
  36.7 3.5 %all-to-all-start = ((f32[16,40,128]{2,1,0:T(8,128)}), f32[16,40,128]{2,1,0:T(8,128)S(1)}, u32[]{:S(2)}, u32[]{:S(2)}) async-start(f32[16,40,128]{2,1,0:T(8,128)} %spread.1), calls=%async_computation | async-start | bytes 655360 | tf_op jit(solution)/shard_map/all_to_all | solution.py:508
  40.3 1.0 %collective-permute-done.8.three = f32[264,128]{1,0:T(8,128)S(1)} collective-permute-done((f32[264,128]{1,0:T(8,128)S(1)}, f32[264,128]{1,0:T(8,128)S(1)}, u32[]{:S(2)}, u32[]{:S(2)}) %collective-permute-start.8) | collective-permute-done | bytes 135200 | tf_op jit(solution)/shard_map/ppermute | solution.py:440
  41.2 0.7 place.1
  42.1 2.7 %collective-permute-start.11 = (f32[192,128]{1,0:T(8,128)S(1)}, f32[192,128]{1,0:T(8,128)S(1)}, u32[]{:S(2)}, u32[]{:S(2)}) collective-permute-start(f32[192,128]{1,0:T(8,128)S(1)} %get-tuple-element.35.after), channel_id=1, source_target_pairs={{0,28},{4,0},{8,4},{12,8},{16,12},{20,16},{24,20},{28,24},{32,60},... | collective-permute-start | bytes 294920 | tf_op jit(solution)/shard_map/ppermute | solution.py:427
  44.7 3.3 %all-to-all-done.chunks = f32[16,40,128]{2,1,0:T(8,128)S(1)} async-done(((f32[16,40,128]{2,1,0:T(8,128)}), f32[16,40,128]{2,1,0:T(8,128)S(1)}, u32[]{:S(2)}, u32[]{:S(2)}) %all-to-all-start) | async-done | bytes 327712 | tf_op jit(solution)/shard_map/all_to_all | solution.py:508
  48.2 3.4 %collective-permute-start.17 = (f32[40,128]{1,0:T(8,128)S(1)}, f32[40,128]{1,0:T(8,128)S(1)}, u32[]{:S(2)}, u32[]{:S(2)}) collective-permute-start(f32[40,128]{1,0:T(8,128)S(1)} %sum.1.after.zero), channel_id=1, source_target_pairs={{0,12},{4,8},{8,4},{12,0},{16,28},{20,24},{24,20},{28,16},{1,13},{... | collective-permute-start | bytes 61448 | tf_op jit(solution)/shard_map/ppermute | solution.py:443
  51.8 3.3 %collective-permute-start.13 = (f32[2,64,128]{2,1,0:T(8,128)S(1)}, f32[2,64,128]{2,1,0:T(8,128)S(1)}, u32[]{:S(2)}, u32[]{:S(2)}) collective-permute-start(f32[2,64,128]{2,1,0:T(8,128)S(1)} %get-tuple-element.39.after), channel_id=1, source_target_pairs={{0,32},{4,36},{8,40},{12,44},{16,48},{20,52},{24,56},{28,60},{32,0... | collective-permute-start | bytes 196616 | tf_op jit(solution)/shard_map/ppermute | solution.py:427
  55.2 0.8 collective-permute-done.13.from_core
  56.0 3.1 %collective-permute-done.14.from_far = f32[2,64,128]{2,1,0:T(8,128)S(1)} collective-permute-done((f32[2,64,128]{2,1,0:T(8,128)S(1)}, f32[2,64,128]{2,1,0:T(8,128)S(1)}, u32[]{:S(2)}, u32[]{:S(2)}) %collective-permute-start.14) | collective-permute-done | bytes 65568 | tf_op jit(solution)/shard_map/ppermute | solution.py:427
  59.1 0.2 collective-permute-start.18
  59.3 1.7 %collective-permute-start.19 = (f32[256,256]{1,0:T(8,128)S(1)}, f32[256,256]{1,0:T(8,128)S(1)}, u32[]{:S(2)}, u32[]{:S(2)}) collective-permute-start(f32[256,256]{1,0:T(8,128)S(1)} %finish.1.one), channel_id=1, source_target_pairs={{0,2},{1,3},{2,0},{3,1},{4,6},{5,7},{6,4},{7,5},{8,10},{9,11},{10,... | collective-permute-start | bytes 786440 | tf_op jit(solution)/shard_map/ppermute | solution.py:440
  61.1 1.4 %collective-permute-start.20 = (f32[256,256]{1,0:T(8,128)S(1)}, f32[256,256]{1,0:T(8,128)S(1)}, u32[]{:S(2)}, u32[]{:S(2)}) collective-permute-start(f32[256,256]{1,0:T(8,128)S(1)} %finish.1.one), channel_id=1, source_target_pairs={{0,3},{1,0},{2,1},{3,2},{4,7},{5,4},{6,5},{7,6},{8,11},{9,8},{10,9... | collective-permute-start | bytes 786440 | tf_op jit(solution)/shard_map/ppermute | solution.py:440
  62.5 14.0 %all_to_all.10 = f32[16,32,128]{2,1,0:T(8,128)S(1)} all-to-all(f32[16,32,128]{2,1,0:T(8,128)S(1)} %mean.1), channel_id=1, replica_groups=mesh['x'=4,'core'=2,'tx'=8,'scan'=4] {'x','scan'}, dimensions={0} | all-to-all | bytes 524288 | tf_op jit(solution)/shard_map/all_to_all | solution.py:554
  76.5 1.5 %collective-permute-start.22 = (f32[512,128]{1,0:T(8,128)S(1)}, f32[512,128]{1,0:T(8,128)S(1)}, u32[]{:S(2)}, u32[]{:S(2)}) collective-permute-start(f32[512,128]{1,0:T(8,128)S(1)} %bitcast.13), channel_id=1, source_target_pairs={{0,32},{4,36},{8,40},{12,44},{16,48},{20,52},{24,56},{28,60},{32,0... | collective-permute-start | bytes 786440 | tf_op jit(solution)/shard_map/ppermute | solution.py:427
  78.0 1.0 %gather.1 = f32[4,256,256]{2,1,0:T(8,128)} custom-call(f32[256,256]{1,0:T(8,128)S(1)} %finish.1.one, f32[256,256]{1,0:T(8,128)S(1)} %collective-permute-done.18.two, f32[256,256]{1,0:T(8,128)S(1)} %collective-permute-done.19.three, f32[256,256]{1,0:T(8,128)S(1)} %collective-permute-done.20.four), custom_call_target="tpu_custom_call" | custom-call | flops 10000000000 | tf_op jit(solution)/shard_map/gather/pallas_call | solution.py:373
  79.2 0.8 %halves.1 = f32[2,512,128]{2,1,0:T(8,128)} custom-call(f32[512,128]{1,0:T(8,128)S(1)} %bitcast.14, f32[512,128]{1,0:T(8,128)S(1)} %collective-permute-done.22.other), custom_call_target="tpu_custom_call" | custom-call | flops 10000000000 | tf_op jit(solution)/shard_map/halves/pallas_call | solution.py:373
  (56 shorter events, 1.7 us)
Async XLA Ops:
  2.1 17.4 %collective-permute-start = (f32[4,128,128]{2,1,0:T(8,128)S(1)}, f32[4,128,128]{2,1,0:T(8,128)S(1)}, u32[]{:S(2)}, u32[]{:S(2)}) collective-permute-start(f32[4,128,128]{2,1,0:T(8,128)S(1)} %get-tuple-element.22.after), channel_id=1, source_target_pairs={{0,28},{4,0},{8,4},{12,8},{16,12},{20,16},{24,20},{28,24},{32,60},... | collective-permute-start | bytes 786440 | tf_op jit(solution)/shard_map/ppermute | solution.py:427
  8.5 10.9 %collective-permute-start.1 = (f32[4,128,128]{2,1,0:T(8,128)S(1)}, f32[4,128,128]{2,1,0:T(8,128)S(1)}, u32[]{:S(2)}, u32[]{:S(2)}) collective-permute-start(f32[4,128,128]{2,1,0:T(8,128)S(1)} %get-tuple-element.23), channel_id=1, source_target_pairs={{0,4},{4,8},{8,12},{12,16},{16,20},{20,24},{24,28},{28,0},{32,36},... | collective-permute-start | bytes 786440 | tf_op jit(solution)/shard_map/ppermute | solution.py:427
  8.7 10.8 %collective-permute-start.3 = (f32[4,64,256]{2,1,0:T(8,128)S(1)}, f32[4,64,256]{2,1,0:T(8,128)S(1)}, u32[]{:S(2)}, u32[]{:S(2)}) collective-permute-start(f32[4,64,256]{2,1,0:T(8,128)S(1)} %get-tuple-element.25), channel_id=1, source_target_pairs={{0,224},{4,228},{8,232},{12,236},{16,240},{20,244},{24,248},{28,25... | collective-permute-start | bytes 786440 | tf_op jit(solution)/shard_map/ppermute | solution.py:427
  10.8 4.9 %collective-permute-start.4 = (f32[4,32,128]{2,1,0:T(8,128)S(1)}, f32[4,32,128]{2,1,0:T(8,128)S(1)}, u32[]{:S(2)}, u32[]{:S(2)}) collective-permute-start(f32[4,32,128]{2,1,0:T(8,128)S(1)} %get-tuple-element.26), channel_id=1, source_target_pairs={{0,252},{4,224},{8,228},{12,232},{16,236},{20,240},{24,244},{28,24... | collective-permute-start | bytes 196616 | tf_op jit(solution)/shard_map/ppermute | solution.py:427
  13.6 5.8 %collective-permute-start.5 = (f32[4,32,128]{2,1,0:T(8,128)S(1)}, f32[4,32,128]{2,1,0:T(8,128)S(1)}, u32[]{:S(2)}, u32[]{:S(2)}) collective-permute-start(f32[4,32,128]{2,1,0:T(8,128)S(1)} %get-tuple-element.27), channel_id=1, source_target_pairs={{0,228},{4,232},{8,236},{12,240},{16,244},{20,248},{24,252},{28,22... | collective-permute-start | bytes 196616 | tf_op jit(solution)/shard_map/ppermute | solution.py:427
  15.7 7.0 %copy-start.8 = (f32[128,128]{1,0:T(8,128)S(1)}, f32[128,128]{1,0:T(8,128)}, u32[]{:S(2)}) copy-start(f32[128,128]{1,0:T(8,128)} %phase.3) | copy-start | bytes 196612
  15.7 7.4 %collective-permute-start.2 = (f32[4,64,256]{2,1,0:T(8,128)S(1)}, f32[4,64,256]{2,1,0:T(8,128)S(1)}, u32[]{:S(2)}, u32[]{:S(2)}) collective-permute-start(f32[4,64,256]{2,1,0:T(8,128)S(1)} %get-tuple-element.24), channel_id=1, source_target_pairs={{0,32},{4,36},{8,40},{12,44},{16,48},{20,52},{24,56},{28,60},{32,0... | collective-permute-start | bytes 786440 | tf_op jit(solution)/shard_map/ppermute | solution.py:427
  19.6 4.1 %copy-start.1 = (f32[2,2,256,256]{3,2,1,0:T(8,128)S(1)}, f32[2,2,256,256]{3,2,1,0:T(8,128)}, u32[]{:S(2)}) copy-start(f32[2,2,256,256]{3,2,1,0:T(8,128)} %param.10) | copy-start | bytes 3145732
  19.6 4.1 %copy-start.2 = (f32[4,2,128,128]{3,2,1,0:T(8,128)S(1)}, f32[4,2,128,128]{3,2,1,0:T(8,128)}, u32[]{:S(2)}) copy-start(f32[4,2,128,128]{3,2,1,0:T(8,128)} %param.11) | copy-start | bytes 1572868
  19.6 4.1 %copy-start.3 = (f32[1,1,2,128,128]{4,3,2,1,0:T(8,128)S(1)}, f32[1,1,2,128,128]{4,3,2,1,0:T(8,128)}, u32[]{:S(2)}) copy-start(f32[1,1,2,128,128]{4,3,2,1,0:T(8,128)} %param.15) | copy-start | bytes 393220
  19.6 4.1 %copy-start.4 = (bf16[256,256]{1,0:T(8,128)(2,1)S(1)}, bf16[256,256]{1,0:T(8,128)(2,1)}, u32[]{:S(2)}) copy-start(bf16[256,256]{1,0:T(8,128)(2,1)} %constant.9.clone.right_high) | copy-start | bytes 393220
  19.6 4.1 %copy-start.5 = (bf16[256,256]{1,0:T(8,128)(2,1)S(1)}, bf16[256,256]{1,0:T(8,128)(2,1)}, u32[]{:S(2)}) copy-start(bf16[256,256]{1,0:T(8,128)(2,1)} %constant.22.clone.right_low) | copy-start | bytes 393220
  19.6 4.1 %copy-start.6 = (bf16[256,256]{1,0:T(8,128)(2,1)S(1)}, bf16[256,256]{1,0:T(8,128)(2,1)}, u32[]{:S(2)}) copy-start(bf16[256,256]{1,0:T(8,128)(2,1)} %constant.23.clone.left_high) | copy-start | bytes 393220
  19.7 4.1 %copy-start.7 = (bf16[256,256]{1,0:T(8,128)(2,1)S(1)}, bf16[256,256]{1,0:T(8,128)(2,1)}, u32[]{:S(2)}) copy-start(bf16[256,256]{1,0:T(8,128)(2,1)} %constant.24.clone.left_low) | copy-start | bytes 393220
  19.7 4.0 %collective-permute-start.6 = (f32[4,64,128]{2,1,0:T(8,128)S(1)}, f32[4,64,128]{2,1,0:T(8,128)S(1)}, u32[]{:S(2)}, u32[]{:S(2)}) collective-permute-start(f32[4,64,128]{2,1,0:T(8,128)S(1)} %corners.1), channel_id=1, source_target_pairs={{0,32},{4,36},{8,40},{12,44},{16,48},{20,52},{24,56},{28,60},{32,0... | collective-permute-start | bytes 393224 | tf_op jit(solution)/shard_map/ppermute | solution.py:427
  30.5 5.4 %collective-permute-start.12 = (f32[520,128]{1,0:T(8,128)S(1)}, f32[520,128]{1,0:T(8,128)S(1)}, u32[]{:S(2)}, u32[]{:S(2)}) collective-permute-start(f32[520,128]{1,0:T(8,128)S(1)} %get-tuple-element.38), channel_id=1, source_target_pairs={{0,32},{4,36},{8,40},{12,44},{16,48},{20,52},{24,56},{28,60},{32,0... | collective-permute-start | bytes 798728 | tf_op jit(solution)/shard_map/ppermute | solution.py:427
  31.0 9.3 %collective-permute-start.7 = (f32[264,128]{1,0:T(8,128)S(1)}, f32[264,128]{1,0:T(8,128)S(1)}, u32[]{:S(2)}, u32[]{:S(2)}) collective-permute-start(f32[264,128]{1,0:T(8,128)S(1)} %get-tuple-element.31), channel_id=1, source_target_pairs={{0,1},{1,2},{2,3},{3,0},{4,5},{5,6},{6,7},{7,4},{8,9},{9,10},{10,1... | collective-permute-start | bytes 405512 | tf_op jit(solution)/shard_map/ppermute | solution.py:440
  32.3 9.0 %collective-permute-start.8 = (f32[264,128]{1,0:T(8,128)S(1)}, f32[264,128]{1,0:T(8,128)S(1)}, u32[]{:S(2)}, u32[]{:S(2)}) collective-permute-start(f32[264,128]{1,0:T(8,128)S(1)} %get-tuple-element.32), channel_id=1, source_target_pairs={{0,2},{1,3},{2,0},{3,1},{4,6},{5,7},{6,4},{7,5},{8,10},{9,11},{10,... | collective-permute-start | bytes 405512 | tf_op jit(solution)/shard_map/ppermute | solution.py:440
  34.9 6.3 %collective-permute-start.9 = (f32[264,128]{1,0:T(8,128)S(1)}, f32[264,128]{1,0:T(8,128)S(1)}, u32[]{:S(2)}, u32[]{:S(2)}) collective-permute-start(f32[264,128]{1,0:T(8,128)S(1)} %get-tuple-element.33), channel_id=1, source_target_pairs={{0,3},{1,0},{2,1},{3,2},{4,7},{5,4},{6,5},{7,6},{8,11},{9,8},{10,9... | collective-permute-start | bytes 405512 | tf_op jit(solution)/shard_map/ppermute | solution.py:440
  36.7 11.3 %all-to-all-start = ((f32[16,40,128]{2,1,0:T(8,128)}), f32[16,40,128]{2,1,0:T(8,128)S(1)}, u32[]{:S(2)}, u32[]{:S(2)}) async-start(f32[16,40,128]{2,1,0:T(8,128)} %spread.1), calls=%async_computation | async-start | bytes 655360 | tf_op jit(solution)/shard_map/all_to_all | solution.py:508
  42.0 9.7 %collective-permute-start.10 = (f32[192,128]{1,0:T(8,128)S(1)}, f32[192,128]{1,0:T(8,128)S(1)}, u32[]{:S(2)}, u32[]{:S(2)}) collective-permute-start(f32[192,128]{1,0:T(8,128)S(1)} %get-tuple-element.34), channel_id=1, source_target_pairs={{0,4},{4,8},{8,12},{12,16},{16,20},{20,24},{24,28},{28,0},{32,36},... | collective-permute-start | bytes 294920 | tf_op jit(solution)/shard_map/ppermute | solution.py:427
  42.1 9.6 %collective-permute-start.11 = (f32[192,128]{1,0:T(8,128)S(1)}, f32[192,128]{1,0:T(8,128)S(1)}, u32[]{:S(2)}, u32[]{:S(2)}) collective-permute-start(f32[192,128]{1,0:T(8,128)S(1)} %get-tuple-element.35.after), channel_id=1, source_target_pairs={{0,28},{4,0},{8,4},{12,8},{16,12},{20,16},{24,20},{28,24},{32,60},... | collective-permute-start | bytes 294920 | tf_op jit(solution)/shard_map/ppermute | solution.py:427
  48.0 7.1 %collective-permute-start.15 = (f32[40,128]{1,0:T(8,128)S(1)}, f32[40,128]{1,0:T(8,128)S(1)}, u32[]{:S(2)}, u32[]{:S(2)}) collective-permute-start(f32[40,128]{1,0:T(8,128)S(1)} %sum.1.after.zero), channel_id=1, source_target_pairs={{0,4},{4,0},{8,12},{12,8},{16,20},{20,16},{24,28},{28,24},{1,5},{5... | collective-permute-start | bytes 61448 | tf_op jit(solution)/shard_map/ppermute | solution.py:443
  48.1 7.0 %collective-permute-start.16 = (f32[40,128]{1,0:T(8,128)S(1)}, f32[40,128]{1,0:T(8,128)S(1)}, u32[]{:S(2)}, u32[]{:S(2)}) collective-permute-start(f32[40,128]{1,0:T(8,128)S(1)} %sum.1.after.zero), channel_id=1, source_target_pairs={{0,8},{4,12},{8,0},{12,4},{16,24},{20,28},{24,16},{28,20},{1,9},{5... | collective-permute-start | bytes 61448 | tf_op jit(solution)/shard_map/ppermute | solution.py:443
  48.2 6.9 %collective-permute-start.17 = (f32[40,128]{1,0:T(8,128)S(1)}, f32[40,128]{1,0:T(8,128)S(1)}, u32[]{:S(2)}, u32[]{:S(2)}) collective-permute-start(f32[40,128]{1,0:T(8,128)S(1)} %sum.1.after.zero), channel_id=1, source_target_pairs={{0,12},{4,8},{8,4},{12,0},{16,28},{20,24},{24,20},{28,16},{1,13},{... | collective-permute-start | bytes 61448 | tf_op jit(solution)/shard_map/ppermute | solution.py:443
  51.8 4.2 %collective-permute-start.13 = (f32[2,64,128]{2,1,0:T(8,128)S(1)}, f32[2,64,128]{2,1,0:T(8,128)S(1)}, u32[]{:S(2)}, u32[]{:S(2)}) collective-permute-start(f32[2,64,128]{2,1,0:T(8,128)S(1)} %get-tuple-element.39.after), channel_id=1, source_target_pairs={{0,32},{4,36},{8,40},{12,44},{16,48},{20,52},{24,56},{28,60},{32,0... | collective-permute-start | bytes 196616 | tf_op jit(solution)/shard_map/ppermute | solution.py:427
  55.1 4.0 %collective-permute-start.14 = (f32[2,64,128]{2,1,0:T(8,128)S(1)}, f32[2,64,128]{2,1,0:T(8,128)S(1)}, u32[]{:S(2)}, u32[]{:S(2)}) collective-permute-start(f32[2,64,128]{2,1,0:T(8,128)S(1)} %get-tuple-element.40), channel_id=1, source_target_pairs={{0,224},{4,228},{8,232},{12,236},{16,240},{20,244},{24,248},{28,25... | collective-permute-start | bytes 196616 | tf_op jit(solution)/shard_map/ppermute | solution.py:427
  55.1 7.3 %collective-permute-start.21 = (f32[40,128]{1,0:T(8,128)S(1)}, f32[40,128]{1,0:T(8,128)S(1)}, u32[]{:S(2)}, u32[]{:S(2)}) collective-permute-start(f32[40,128]{1,0:T(8,128)S(1)} %group.1.after.own), channel_id=1, source_target_pairs={{0,28},{4,24},{8,20},{12,16},{16,12},{20,8},{24,4},{28,0},{1,29},{... | collective-permute-start | bytes 61448 | tf_op jit(solution)/shard_map/ppermute | solution.py:443
  59.1 18.9 %collective-permute-start.18 = (f32[256,256]{1,0:T(8,128)S(1)}, f32[256,256]{1,0:T(8,128)S(1)}, u32[]{:S(2)}, u32[]{:S(2)}) collective-permute-start(f32[256,256]{1,0:T(8,128)S(1)} %finish.1.one), channel_id=1, source_target_pairs={{0,1},{1,2},{2,3},{3,0},{4,5},{5,6},{6,7},{7,4},{8,9},{9,10},{10,1... | collective-permute-start | bytes 786440 | tf_op jit(solution)/shard_map/ppermute | solution.py:440
  59.3 18.7 %collective-permute-start.19 = (f32[256,256]{1,0:T(8,128)S(1)}, f32[256,256]{1,0:T(8,128)S(1)}, u32[]{:S(2)}, u32[]{:S(2)}) collective-permute-start(f32[256,256]{1,0:T(8,128)S(1)} %finish.1.one), channel_id=1, source_target_pairs={{0,2},{1,3},{2,0},{3,1},{4,6},{5,7},{6,4},{7,5},{8,10},{9,11},{10,... | collective-permute-start | bytes 786440 | tf_op jit(solution)/shard_map/ppermute | solution.py:440
  61.1 16.9 %collective-permute-start.20 = (f32[256,256]{1,0:T(8,128)S(1)}, f32[256,256]{1,0:T(8,128)S(1)}, u32[]{:S(2)}, u32[]{:S(2)}) collective-permute-start(f32[256,256]{1,0:T(8,128)S(1)} %finish.1.one), channel_id=1, source_target_pairs={{0,3},{1,0},{2,1},{3,2},{4,7},{5,4},{6,5},{7,6},{8,11},{9,8},{10,9... | collective-permute-start | bytes 786440 | tf_op jit(solution)/shard_map/ppermute | solution.py:440
  76.5 2.6 %collective-permute-start.22 = (f32[512,128]{1,0:T(8,128)S(1)}, f32[512,128]{1,0:T(8,128)S(1)}, u32[]{:S(2)}, u32[]{:S(2)}) collective-permute-start(f32[512,128]{1,0:T(8,128)S(1)} %bitcast.13), channel_id=1, source_target_pairs={{0,32},{4,36},{8,40},{12,44},{16,48},{20,52},{24,56},{28,60},{32,0... | collective-permute-start | bytes 786440 | tf_op jit(solution)/shard_map/ppermute | solution.py:427
  (2 other events, 4.0 us)

commit v4 on v3

--- a/solution.py
+++ b/solution.py
@@ -15,6 +15,7 @@
 SMEM = pl.BlockSpec(memory_space=pltpu.SMEM)
 ANY = pl.BlockSpec(memory_space=pl.ANY)
 LONG = 10**10
+CODE = 512
 PARAMS = pltpu.CompilerParams(vmem_limit_bytes=48 * 1024 * 1024)
 W = 128
 HALF = 64
@@ -35,6 +36,17 @@
     )(*args)
 
 
+def copy_all(pairs, sems):
+    copies = [
+        pltpu.make_async_copy(source, target, sems.at[k])
+        for k, (source, target) in enumerate(pairs)
+    ]
+    for copy in copies:
+        copy.start()
+    for copy in copies:
+        copy.wait()
+
+
 def low_lanes(rows):
     return lax.broadcasted_iota(jnp.int32, (rows, W), 1) < HALF
 
@@ -72,7 +84,7 @@
         fold_corner(rows, far_left.at[part], far_right.at[part])
 
 
-def corners_body(from_right, from_left, far, far_right, far_left, out):
+def corners_body(from_right, from_left, out):
     core = lax.axis_index("core")
     low = low_lanes(HALF)
     span = pl.ds(pl.multiple_of((1 - core) * HALF, HALF), HALF)
@@ -83,7 +95,7 @@
         out[part] = jnp.where(low, right, left)
 
 
-def phase_body(phase, right, left, real, imag):
+def phase_body(phase, far, right, left, real, imag):
     real[...] = jnp.cos(phase[...])
     imag[...] = jnp.sin(phase[...])
 
@@ -95,11 +107,17 @@
 
 def times_right(real, imag, table):
     outs = ([], [])
-    for k in range(len(real)):
-        high, low = halves(jnp.concatenate([real[k], imag[k]], axis=1))
+    for k in range(0, len(real), 2):
+        high, low = halves(
+            jnp.concatenate(
+                [jnp.concatenate([r, i], axis=1) for r, i in zip(real[k : k + 2], imag[k : k + 2])],
+                axis=0,
+            )
+        )
         out = jnp.dot(jnp.concatenate([high, low, high], axis=1), table, preferred_element_type=F32)
-        outs[0].append(out[:, :W])
-        outs[1].append(out[:, W:])
+        for m in range(2):
+            outs[0].append(out[W * m : W * (m + 1), :W])
+            outs[1].append(out[W * m : W * (m + 1), W:])
     return outs
 
 
@@ -261,8 +279,9 @@
 
     places = lax.broadcasted_iota(jnp.int32, (8, W), 0)
     marks = jnp.zeros((8, W), F32)
-    for k, value in enumerate((*corner(0), *corner(1))):
-        marks = jnp.where(places == k, value.astype(F32), marks)
+    for slot in range(2):
+        row, col = corner(slot)
+        marks = jnp.where(places == slot, (row * CODE + col).astype(F32), marks)
     for step, out in enumerate((out0, out1, out2, out3)):
         part = lax.rem(scan + step, 4)
         for slot in range(2):
@@ -288,8 +307,8 @@
     out[...] = functools.reduce(jnp.add, [chunks[k] for k in range(chunks.shape[0])])
 
 
-def group_body(zero, one, two, three, after, out):
-    out[...] = (zero[...] + one[...]) + (two[...] + three[...])
+def pair_body(own, got, after, out):
+    out[...] = own[...] + got[...]
 
 
 def mean_body(own, got, spread):
@@ -301,18 +320,22 @@
 
 
 def place_body(one, two, three, four, to_left, to_right, wide):
-    wide[...] = jnp.zeros_like(wide)
-    lanes = lax.broadcasted_iota(jnp.int32, (W, W), 1)
-    for message in (one, two, three, four):
+    messages = (one, two, three, four)
+    spots = []
+    for message in messages:
         for slot in range(2):
-            base = 2 * W + 2 * slot
-            row = jnp.max(message[base : base + 1]).astype(jnp.int32)
-            col = jnp.max(message[base + 1 : base + 2]).astype(jnp.int32)
+            code = jnp.max(message[2 * W + slot : 2 * W + slot + 1]).astype(jnp.int32)
+            row, col = code // CODE, lax.rem(code, CODE)
             row = jnp.clip(row, 0, TILE)
             col = jnp.clip(col, 0, 3 * W - 1)
             block = col // W
-            shift = col - block * W
             after = jnp.where(block == 2, 0, block + 1)
+            spots.append((row, block, after, col - block * W))
+    wide[...] = jnp.zeros_like(wide)
+    lanes = lax.broadcasted_iota(jnp.int32, (W, W), 1)
+    for k, message in enumerate(messages):
+        for slot in range(2):
+            row, block, after, shift = spots[2 * k + slot]
             turned = pltpu.roll(message[W * slot : W * (slot + 1)], shift, 1)
             wide[block, pl.ds(row, W)] += jnp.where(lanes >= shift, turned, 0.0)
             wide[after, pl.ds(row, W)] += jnp.where(lanes < shift, turned, 0.0)
@@ -345,17 +368,6 @@
         out[:, span] = held[k]
         out[pl.ds(core_row, HALF), span] += from_core[k]
         out[pl.ds(far_row, HALF), span] += from_far[k]
-
-
-def copy_all(pairs, sems):
-    copies = [
-        pltpu.make_async_copy(source, target, sems.at[k])
-        for k, (source, target) in enumerate(pairs)
-    ]
-    for copy in copies:
-        copy.start()
-    for copy in copies:
-        copy.wait()
 
 
 def gather_body(one, two, three, four, out, sems):
@@ -456,23 +468,18 @@
     from_right, from_left = to_left(left), to_right(right)
     from_core, from_far = to_core(near), to_far(far)
     corner_right, corner_left = far_left(corner_left), far_right(corner_right)
+    (corners,) = call(
+        corners_body, [(4, HALF, W)], (from_right, from_left), [VMEM] * 2, name="corners"
+    )
+    corners = to_core(corners)
     kernel_real, kernel_imag = call(
         phase_body,
         [(W, W)] * 2,
-        (kernel_phase, from_right, from_left),
-        [VMEM] + [ANY] * 2,
+        (kernel_phase, from_far, corner_right, corner_left),
+        [VMEM] + [ANY] * 3,
         name="phase",
         flops=LONG,
     )
-    (corners,) = call(
-        corners_body,
-        [(4, HALF, W)],
-        (from_right, from_left, from_far, corner_right, corner_left),
-        [VMEM] * 2 + [ANY] * 3,
-        name="corners",
-        flops=LONG,
-    )
-    corners = to_core(corners)
     rows = jnp.clip(offsets[0, 0, :, 0] + HALF, 0, TILE)
     cols = jnp.clip(offsets[0, 0, :, 1], -HALF, TILE - HALF)
     starts = jnp.stack([rows, jnp.where(cols < 0, cols + 3 * W, cols)], axis=1).reshape(4)
@@ -519,7 +526,7 @@
         sum_body, [(rows + 8, W)], (chunks, left), [VMEM, ANY], name="sum", flops=LONG
     )
     left, right = to_left(left), to_right(right)
-    group = [share] + [to_pair(share, mask) for mask in range(1, 4)]
+    got = to_pair(share, 1)
     near, far, held = call(
         rows_body,
         [(2, HALF, W)] * 2 + [(2, TILE, W)],
@@ -530,8 +537,9 @@
         flops=LONG,
     )
     (share,) = call(
-        group_body, [(rows + 8, W)], (*group, near), [VMEM] * 4 + [ANY], name="group", flops=LONG
-    )
+        pair_body, [(rows + 8, W)], (share, got, near), [VMEM] * 2 + [ANY], name="pair", flops=LONG
+    )
+    got = to_pair(share, 2)
     near, far = to_core(near), to_far(far)
     (quarter,) = call(
         finish_body,
@@ -542,6 +550,9 @@
         flops=LONG,
     )
     quarters = [quarter] + [to_scan(quarter, step) for step in range(1, nsc)]
+    (share,) = call(
+        pair_body, [(rows + 8, W)], (share, got, quarter), [VMEM] * 2 + [ANY], name="pair", flops=LONG
+    )
     got = to_pair(share, ntx - 1)
     (spread,) = call(
         mean_body,

time: 80.4 us -> 77.2 us (0.960)
  blocking collectives: 14 us -> 11.3 us
  waiting for transfers between devices: 11.2 us -> 9.15 us
  starting transfers between devices: 40.3 us -> 42 us
    all_to_all x1, blocking collectives: 14 us -> 11.3 us  [per_device(): mine = lax.all_to_all(spread, ('x', 'scan'), 0, 0).reshape(MODES * W, W)]
    ppermute x13, starting transfers between devices: 24.7 us -> 27.2 us  [over_grid(): return lambda value: lax.ppermute(value, ('x', 'core', 'tx'), pairs)]
    ppermute x13, waiting for transfers between devices: 6.96 us -> 4.66 us  [over_grid(): return lambda value: lax.ppermute(value, ('x', 'core', 'tx'), pairs)]
    ppermute x4 -> x3, starting transfers between devices: 3.71 us -> 1.84 us  [to_pair(): return lax.ppermute(value, 'tx', [(t, t ^ mask) for t in range(ntx)])]
    ppermute x6, starting transfers between devices: 8.3 us -> 9.45 us  [to_scan(): lax.ppermute(value, 'scan', [(s, (s + step) % nsc) for s in range(nsc)])]
    pallas_call x12 -> x13, Pallas kernels: 9.4 us -> 9.12 us  [call(): pl.pallas_call(body, out_shape=[jax.ShapeDtypeStruct(shape, F32) for shap...]
  transfers between devices with their start and end apart: 24 -> 23, of which waited for: 8 -> 6; matrix products, arithmetic and copies ran while one was open for 0% -> 0% of each run, Pallas kernels for 4% -> 4%
where the time goes in v4:
time: 77.2 us; the launch traced here: 76.9 us
  starting transfers between devices  42 us (54%)
  blocking collectives  11.3 us (15%)
  Pallas kernels  10.9 us (14%)
  waiting for transfers between devices  9.15 us (12%)
  between operations  1.78 us (2%)
  local copies, waits for them, and re-layouts  1.45 us (2%)
    ppermute x13, starting transfers between devices, over_grid(): return lambda value: lax.ppermute(value, ('x', 'core', 'tx'), pairs)  27.2 us
    all_to_all x1, blocking collectives, per_device(): mine = lax.all_to_all(spread, ('x', 'scan'), 0, 0).reshape(MODES * W, W)  11.3 us
    ppermute x6, starting transfers between devices, to_scan(): lax.ppermute(value, 'scan', [(s, (s + step) % nsc) for s in range(nsc)])  9.45 us
    pallas_call x13, Pallas kernels, call(): pl.pallas_call(body, out_shape=[jax.ShapeDtypeStruct(shape, F32) for shap...  9.12 us
    ppermute x13, waiting for transfers between devices, over_grid(): return lambda value: lax.ppermute(value, ('x', 'core', 'tx'), pairs)  4.66 us
    all_to_all x1, starting transfers between devices, per_device(): chunks = lax.all_to_all(chunks, ('x', 'scan'), 0, 0)  3.54 us
    all_to_all x1, waiting for transfers between devices, per_device(): chunks = lax.all_to_all(chunks, ('x', 'scan'), 0, 0)  3.54 us
    ppermute x3, starting transfers between devices, to_pair(): return lax.ppermute(value, 'tx', [(t, t ^ mask) for t in range(ntx)])  1.84 us
  transfers between devices with their start and end apart: 23, of which 6 were waited for; matrix products, arithmetic and copies ran while one was open for 0% of the time, Pallas kernels for 4%

profile of v4, /device:TPU:1, one launch (start us, length us, event | category | flops | bytes accessed | tf_op | source)
XLA Modules:
  0.0 76.9 jit_solution(15429364111904716114)
XLA Ops:
  0.6 1.2 %copy-done = f32[2,2,256,256]{3,2,1,0:T(8,128)S(1)} copy-done((f32[2,2,256,256]{3,2,1,0:T(8,128)S(1)}, f32[2,2,256,256]{3,2,1,0:T(8,128)}, u32[]{:S(2)}) %copy-start) | copy-done | bytes 1048600
  1.9 0.2 sides.1
  2.1 6.5 %collective-permute-start = (f32[4,128,128]{2,1,0:T(8,128)S(1)}, f32[4,128,128]{2,1,0:T(8,128)S(1)}, u32[]{:S(2)}, u32[]{:S(2)}) collective-permute-start(f32[4,128,128]{2,1,0:T(8,128)S(1)} %get-tuple-element.22.after), channel_id=1, source_target_pairs={{0,28},{4,0},{8,4},{12,8},{16,12},{20,16},{24,20},{28,24},{32,60},... | collective-permute-start | bytes 786440 | tf_op jit(solution)/shard_map/ppermute | solution.py:439
  8.7 2.1 %collective-permute-start.3 = (f32[4,64,256]{2,1,0:T(8,128)S(1)}, f32[4,64,256]{2,1,0:T(8,128)S(1)}, u32[]{:S(2)}, u32[]{:S(2)}) collective-permute-start(f32[4,64,256]{2,1,0:T(8,128)S(1)} %get-tuple-element.25), channel_id=1, source_target_pairs={{0,224},{4,228},{8,232},{12,236},{16,240},{20,244},{24,248},{28,25... | collective-permute-start | bytes 786440 | tf_op jit(solution)/shard_map/ppermute | solution.py:439
  10.8 2.8 %collective-permute-start.4 = (f32[4,32,128]{2,1,0:T(8,128)S(1)}, f32[4,32,128]{2,1,0:T(8,128)S(1)}, u32[]{:S(2)}, u32[]{:S(2)}) collective-permute-start(f32[4,32,128]{2,1,0:T(8,128)S(1)} %get-tuple-element.26), channel_id=1, source_target_pairs={{0,252},{4,224},{8,228},{12,232},{16,236},{20,240},{24,244},{28,24... | collective-permute-start | bytes 196616 | tf_op jit(solution)/shard_map/ppermute | solution.py:439
  13.6 0.2 clamp_reduce_fusion.1
  14.6 2.0 %collective-permute-start.2 = (f32[4,64,256]{2,1,0:T(8,128)S(1)}, f32[4,64,256]{2,1,0:T(8,128)S(1)}, u32[]{:S(2)}, u32[]{:S(2)}) collective-permute-start(f32[4,64,256]{2,1,0:T(8,128)S(1)} %get-tuple-element.24), channel_id=1, source_target_pairs={{0,32},{4,36},{8,40},{12,44},{16,48},{20,52},{24,56},{28,60},{32,0... | collective-permute-start | bytes 786440 | tf_op jit(solution)/shard_map/ppermute | solution.py:439
  16.9 1.9 %collective-permute-start.6 = (f32[4,64,128]{2,1,0:T(8,128)S(1)}, f32[4,64,128]{2,1,0:T(8,128)S(1)}, u32[]{:S(2)}, u32[]{:S(2)}) collective-permute-start(f32[4,64,128]{2,1,0:T(8,128)S(1)} %corners.1), channel_id=1, source_target_pairs={{0,32},{4,36},{8,40},{12,44},{16,48},{20,52},{24,56},{28,60},{32,0... | collective-permute-start | bytes 393224 | tf_op jit(solution)/shard_map/ppermute | solution.py:439
  18.8 0.6 collective-permute-done.5.left.far_left
  19.4 0.4 phase.2
  19.9 6.8 %slots.1 = (f32[264,128]{1,0:T(8,128)S(1)}, f32[264,128]{1,0:T(8,128)S(1)}, f32[264,128]{1,0:T(8,128)S(1)}, f32[264,128]{1,0:T(8,128)S(1)}, f32[520,128]{1,0:T(8,128)S(1)}, /*index=5*/f32[520,128]{1,0:T(8,128)S(1)}) custom-call(s32[4]{0:T(128)S(1)} %reshape.62.starts, s32[1,1,1]{2,1,0:T(1,128)S(6)} %copy.13.live_counts, f32[4,256,256]{2,1,0:T(8,128)S(1)} %bitcast.11, ...), custom_call_target="tpu_custom_call" | custom-call | tf_op jit(solution)/shard_map/slots/pallas_call | solution.py:27
  26.7 3.0 %collective-permute-start.12 = (f32[520,128]{1,0:T(8,128)S(1)}, f32[520,128]{1,0:T(8,128)S(1)}, u32[]{:S(2)}, u32[]{:S(2)}) collective-permute-start(f32[520,128]{1,0:T(8,128)S(1)} %get-tuple-element.38), channel_id=1, source_target_pairs={{0,32},{4,36},{8,40},{12,44},{16,48},{20,52},{24,56},{28,60},{32,0... | collective-permute-start | bytes 798728 | tf_op jit(solution)/shard_map/ppermute | solution.py:439
  29.7 1.3 %collective-permute-start.7 = (f32[264,128]{1,0:T(8,128)S(1)}, f32[264,128]{1,0:T(8,128)S(1)}, u32[]{:S(2)}, u32[]{:S(2)}) collective-permute-start(f32[264,128]{1,0:T(8,128)S(1)} %get-tuple-element.31), channel_id=1, source_target_pairs={{0,1},{1,2},{2,3},{3,0},{4,5},{5,6},{6,7},{7,4},{8,9},{9,10},{10,1... | collective-permute-start | bytes 405512 | tf_op jit(solution)/shard_map/ppermute | solution.py:452
  31.0 2.6 %collective-permute-start.8 = (f32[264,128]{1,0:T(8,128)S(1)}, f32[264,128]{1,0:T(8,128)S(1)}, u32[]{:S(2)}, u32[]{:S(2)}) collective-permute-start(f32[264,128]{1,0:T(8,128)S(1)} %get-tuple-element.32), channel_id=1, source_target_pairs={{0,2},{1,3},{2,0},{3,1},{4,6},{5,7},{6,4},{7,5},{8,10},{9,11},{10,... | collective-permute-start | bytes 405512 | tf_op jit(solution)/shard_map/ppermute | solution.py:452
  33.6 1.1 %collective-permute-start.9 = (f32[264,128]{1,0:T(8,128)S(1)}, f32[264,128]{1,0:T(8,128)S(1)}, u32[]{:S(2)}, u32[]{:S(2)}) collective-permute-start(f32[264,128]{1,0:T(8,128)S(1)} %get-tuple-element.33), channel_id=1, source_target_pairs={{0,3},{1,0},{2,1},{3,2},{4,7},{5,4},{6,5},{7,6},{8,11},{9,8},{10,9... | collective-permute-start | bytes 405512 | tf_op jit(solution)/shard_map/ppermute | solution.py:452
  34.7 0.8 spread.1
  35.5 3.5 %all-to-all-start = ((f32[16,40,128]{2,1,0:T(8,128)}), f32[16,40,128]{2,1,0:T(8,128)S(1)}, u32[]{:S(2)}, u32[]{:S(2)}) async-start(f32[16,40,128]{2,1,0:T(8,128)} %spread.1), calls=%async_computation | async-start | bytes 655360 | tf_op jit(solution)/shard_map/all_to_all | solution.py:515
  39.0 0.9 %collective-permute-done.8.three = f32[264,128]{1,0:T(8,128)S(1)} collective-permute-done((f32[264,128]{1,0:T(8,128)S(1)}, f32[264,128]{1,0:T(8,128)S(1)}, u32[]{:S(2)}, u32[]{:S(2)}) %collective-permute-start.8) | collective-permute-done | bytes 135200 | tf_op jit(solution)/shard_map/ppermute | solution.py:452
  40.0 0.5 place.1
  40.5 2.7 %collective-permute-start.11 = (f32[192,128]{1,0:T(8,128)S(1)}, f32[192,128]{1,0:T(8,128)S(1)}, u32[]{:S(2)}, u32[]{:S(2)}) collective-permute-start(f32[192,128]{1,0:T(8,128)S(1)} %get-tuple-element.35.after), channel_id=1, source_target_pairs={{0,28},{4,0},{8,4},{12,8},{16,12},{20,16},{24,20},{28,24},{32,60},... | collective-permute-start | bytes 294920 | tf_op jit(solution)/shard_map/ppermute | solution.py:439
  43.2 3.5 %all-to-all-done.chunks = f32[16,40,128]{2,1,0:T(8,128)S(1)} async-done(((f32[16,40,128]{2,1,0:T(8,128)}), f32[16,40,128]{2,1,0:T(8,128)S(1)}, u32[]{:S(2)}, u32[]{:S(2)}) %all-to-all-start) | async-done | bytes 327712 | tf_op jit(solution)/shard_map/all_to_all | solution.py:515
  47.0 2.4 %collective-permute-start.13 = (f32[2,64,128]{2,1,0:T(8,128)S(1)}, f32[2,64,128]{2,1,0:T(8,128)S(1)}, u32[]{:S(2)}, u32[]{:S(2)}) collective-permute-start(f32[2,64,128]{2,1,0:T(8,128)S(1)} %get-tuple-element.39.after), channel_id=1, source_target_pairs={{0,32},{4,36},{8,40},{12,44},{16,48},{20,52},{24,56},{28,60},{32,0... | collective-permute-start | bytes 196616 | tf_op jit(solution)/shard_map/ppermute | solution.py:439
  49.6 0.8 %collective-permute-done.13.from_core = f32[2,64,128]{2,1,0:T(8,128)S(1)} collective-permute-done((f32[2,64,128]{2,1,0:T(8,128)S(1)}, f32[2,64,128]{2,1,0:T(8,128)S(1)}, u32[]{:S(2)}, u32[]{:S(2)}) %collective-permute-start.13) | collective-permute-done | bytes 65568 | tf_op jit(solution)/shard_map/ppermute | solution.py:439
  50.4 3.1 %collective-permute-done.14.from_far = f32[2,64,128]{2,1,0:T(8,128)S(1)} collective-permute-done((f32[2,64,128]{2,1,0:T(8,128)S(1)}, f32[2,64,128]{2,1,0:T(8,128)S(1)}, u32[]{:S(2)}, u32[]{:S(2)}) %collective-permute-start.14) | collective-permute-done | bytes 65568 | tf_op jit(solution)/shard_map/ppermute | solution.py:439
  53.5 1.7 %collective-permute-start.20 = (f32[40,128]{1,0:T(8,128)S(1)}, f32[40,128]{1,0:T(8,128)S(1)}, u32[]{:S(2)}, u32[]{:S(2)}) collective-permute-start(f32[40,128]{1,0:T(8,128)S(1)} %pair.3.own), channel_id=1, source_target_pairs={{0,28},{4,24},{8,20},{12,16},{16,12},{20,8},{24,4},{28,0},{1,29},{... | collective-permute-start | bytes 61448 | tf_op jit(solution)/shard_map/ppermute | solution.py:455
  55.2 0.9 %collective-permute-start.16 = (f32[256,256]{1,0:T(8,128)S(1)}, f32[256,256]{1,0:T(8,128)S(1)}, u32[]{:S(2)}, u32[]{:S(2)}) collective-permute-start(f32[256,256]{1,0:T(8,128)S(1)} %finish.1.one.after), channel_id=1, source_target_pairs={{0,1},{1,2},{2,3},{3,0},{4,5},{5,6},{6,7},{7,4},{8,9},{9,10},{10,1... | collective-permute-start | bytes 786440 | tf_op jit(solution)/shard_map/ppermute | solution.py:452
  56.1 2.4 %collective-permute-start.17 = (f32[256,256]{1,0:T(8,128)S(1)}, f32[256,256]{1,0:T(8,128)S(1)}, u32[]{:S(2)}, u32[]{:S(2)}) collective-permute-start(f32[256,256]{1,0:T(8,128)S(1)} %finish.1.one.after), channel_id=1, source_target_pairs={{0,2},{1,3},{2,0},{3,1},{4,6},{5,7},{6,4},{7,5},{8,10},{9,11},{10,... | collective-permute-start | bytes 786440 | tf_op jit(solution)/shard_map/ppermute | solution.py:452
  58.5 1.2 %collective-permute-start.18 = (f32[256,256]{1,0:T(8,128)S(1)}, f32[256,256]{1,0:T(8,128)S(1)}, u32[]{:S(2)}, u32[]{:S(2)}) collective-permute-start(f32[256,256]{1,0:T(8,128)S(1)} %finish.1.one.after), channel_id=1, source_target_pairs={{0,3},{1,0},{2,1},{3,2},{4,7},{5,4},{6,5},{7,6},{8,11},{9,8},{10,9... | collective-permute-start | bytes 786440 | tf_op jit(solution)/shard_map/ppermute | solution.py:452
  59.7 11.3 %all_to_all.10 = f32[16,32,128]{2,1,0:T(8,128)S(1)} all-to-all(f32[16,32,128]{2,1,0:T(8,128)S(1)} %mean.1), channel_id=1, replica_groups=mesh['x'=4,'core'=2,'tx'=8,'scan'=4] {'x','scan'}, dimensions={0} | all-to-all | bytes 524288 | tf_op jit(solution)/shard_map/all_to_all | solution.py:565
  71.0 3.7 %collective-permute-start.21 = (f32[512,128]{1,0:T(8,128)S(1)}, f32[512,128]{1,0:T(8,128)S(1)}, u32[]{:S(2)}, u32[]{:S(2)}) collective-permute-start(f32[512,128]{1,0:T(8,128)S(1)} %bitcast.13), channel_id=1, source_target_pairs={{0,32},{4,36},{8,40},{12,44},{16,48},{20,52},{24,56},{28,60},{32,0... | collective-permute-start | bytes 786440 | tf_op jit(solution)/shard_map/ppermute | solution.py:439
  74.7 1.0 %gather.1 = f32[4,256,256]{2,1,0:T(8,128)} custom-call(f32[256,256]{1,0:T(8,128)S(1)} %finish.1.one.after, f32[256,256]{1,0:T(8,128)S(1)} %collective-permute-done.16.two, f32[256,256]{1,0:T(8,128)S(1)} %collective-permute-done.17.three, f32[256,256]{1,0:T(8,128)S(1)} %collective-permute-done.18.four), custom_call_target="tpu_custom_call" | custom-call | flops 10000000000 | tf_op jit(solution)/shard_map/gather/pallas_call | solution.py:385
  75.9 0.8 %halves.1 = f32[2,512,128]{2,1,0:T(8,128)} custom-call(f32[512,128]{1,0:T(8,128)S(1)} %bitcast.14, f32[512,128]{1,0:T(8,128)S(1)} %collective-permute-done.21.other), custom_call_target="tpu_custom_call" | custom-call | flops 10000000000 | tf_op jit(solution)/shard_map/halves/pallas_call | solution.py:385
  (55 shorter events, 1.2 us)
Async XLA Ops:
  2.1 12.6 %collective-permute-start = (f32[4,128,128]{2,1,0:T(8,128)S(1)}, f32[4,128,128]{2,1,0:T(8,128)S(1)}, u32[]{:S(2)}, u32[]{:S(2)}) collective-permute-start(f32[4,128,128]{2,1,0:T(8,128)S(1)} %get-tuple-element.22.after), channel_id=1, source_target_pairs={{0,28},{4,0},{8,4},{12,8},{16,12},{20,16},{24,20},{28,24},{32,60},... | collective-permute-start | bytes 786440 | tf_op jit(solution)/shard_map/ppermute | solution.py:439
  8.5 8.1 %collective-permute-start.1 = (f32[4,128,128]{2,1,0:T(8,128)S(1)}, f32[4,128,128]{2,1,0:T(8,128)S(1)}, u32[]{:S(2)}, u32[]{:S(2)}) collective-permute-start(f32[4,128,128]{2,1,0:T(8,128)S(1)} %get-tuple-element.23), channel_id=1, source_target_pairs={{0,4},{4,8},{8,12},{12,16},{16,20},{20,24},{24,28},{28,0},{32,36},... | collective-permute-start | bytes 786440 | tf_op jit(solution)/shard_map/ppermute | solution.py:439
  8.7 10.8 %collective-permute-start.3 = (f32[4,64,256]{2,1,0:T(8,128)S(1)}, f32[4,64,256]{2,1,0:T(8,128)S(1)}, u32[]{:S(2)}, u32[]{:S(2)}) collective-permute-start(f32[4,64,256]{2,1,0:T(8,128)S(1)} %get-tuple-element.25), channel_id=1, source_target_pairs={{0,224},{4,228},{8,232},{12,236},{16,240},{20,244},{24,248},{28,25... | collective-permute-start | bytes 786440 | tf_op jit(solution)/shard_map/ppermute | solution.py:439
  10.8 2.8 %copy-start.9 = (s32[1,1,2,2]{3,2,1,0:T(2,128)S(1)}, s32[1,1,2,2]{3,2,1,0:T(2,128)}, u32[]{:S(2)}) copy-start(s32[1,1,2,2]{3,2,1,0:T(2,128)} %param.13) | copy-start | bytes 52
  10.8 8.0 %collective-permute-start.4 = (f32[4,32,128]{2,1,0:T(8,128)S(1)}, f32[4,32,128]{2,1,0:T(8,128)S(1)}, u32[]{:S(2)}, u32[]{:S(2)}) collective-permute-start(f32[4,32,128]{2,1,0:T(8,128)S(1)} %get-tuple-element.26), channel_id=1, source_target_pairs={{0,252},{4,224},{8,228},{12,232},{16,236},{20,240},{24,244},{28,24... | collective-permute-start | bytes 196616 | tf_op jit(solution)/shard_map/ppermute | solution.py:439
  13.6 5.8 %collective-permute-start.5 = (f32[4,32,128]{2,1,0:T(8,128)S(1)}, f32[4,32,128]{2,1,0:T(8,128)S(1)}, u32[]{:S(2)}, u32[]{:S(2)}) collective-permute-start(f32[4,32,128]{2,1,0:T(8,128)S(1)} %get-tuple-element.27), channel_id=1, source_target_pairs={{0,228},{4,232},{8,236},{12,240},{16,244},{20,248},{24,252},{28,22... | collective-permute-start | bytes 196616 | tf_op jit(solution)/shard_map/ppermute | solution.py:439
  14.6 4.8 %copy-start.8 = (f32[128,128]{1,0:T(8,128)S(1)}, f32[128,128]{1,0:T(8,128)}, u32[]{:S(2)}) copy-start(f32[128,128]{1,0:T(8,128)} %phase.3) | copy-start | bytes 196612
  14.6 5.2 %collective-permute-start.2 = (f32[4,64,256]{2,1,0:T(8,128)S(1)}, f32[4,64,256]{2,1,0:T(8,128)S(1)}, u32[]{:S(2)}, u32[]{:S(2)}) collective-permute-start(f32[4,64,256]{2,1,0:T(8,128)S(1)} %get-tuple-element.24), channel_id=1, source_target_pairs={{0,32},{4,36},{8,40},{12,44},{16,48},{20,52},{24,56},{28,60},{32,0... | collective-permute-start | bytes 786440 | tf_op jit(solution)/shard_map/ppermute | solution.py:439
  16.8 3.1 %copy-start.1 = (f32[2,2,256,256]{3,2,1,0:T(8,128)S(1)}, f32[2,2,256,256]{3,2,1,0:T(8,128)}, u32[]{:S(2)}) copy-start(f32[2,2,256,256]{3,2,1,0:T(8,128)} %param.10) | copy-start | bytes 3145732
  16.8 3.1 %copy-start.2 = (f32[4,2,128,128]{3,2,1,0:T(8,128)S(1)}, f32[4,2,128,128]{3,2,1,0:T(8,128)}, u32[]{:S(2)}) copy-start(f32[4,2,128,128]{3,2,1,0:T(8,128)} %param.11) | copy-start | bytes 1572868
  16.8 3.1 %copy-start.3 = (f32[1,1,2,128,128]{4,3,2,1,0:T(8,128)S(1)}, f32[1,1,2,128,128]{4,3,2,1,0:T(8,128)}, u32[]{:S(2)}) copy-start(f32[1,1,2,128,128]{4,3,2,1,0:T(8,128)} %param.15) | copy-start | bytes 393220
  16.8 3.1 %copy-start.4 = (bf16[256,256]{1,0:T(8,128)(2,1)S(1)}, bf16[256,256]{1,0:T(8,128)(2,1)}, u32[]{:S(2)}) copy-start(bf16[256,256]{1,0:T(8,128)(2,1)} %constant.9.clone.right_high) | copy-start | bytes 393220
  16.8 3.1 %copy-start.5 = (bf16[256,256]{1,0:T(8,128)(2,1)S(1)}, bf16[256,256]{1,0:T(8,128)(2,1)}, u32[]{:S(2)}) copy-start(bf16[256,256]{1,0:T(8,128)(2,1)} %constant.22.clone.right_low) | copy-start | bytes 393220
  16.8 3.1 %copy-start.6 = (bf16[256,256]{1,0:T(8,128)(2,1)S(1)}, bf16[256,256]{1,0:T(8,128)(2,1)}, u32[]{:S(2)}) copy-start(bf16[256,256]{1,0:T(8,128)(2,1)} %constant.23.clone.left_high) | copy-start | bytes 393220
  16.9 3.1 %copy-start.7 = (bf16[256,256]{1,0:T(8,128)(2,1)S(1)}, bf16[256,256]{1,0:T(8,128)(2,1)}, u32[]{:S(2)}) copy-start(bf16[256,256]{1,0:T(8,128)(2,1)} %constant.24.clone.left_low) | copy-start | bytes 393220
  16.9 3.0 %collective-permute-start.6 = (f32[4,64,128]{2,1,0:T(8,128)S(1)}, f32[4,64,128]{2,1,0:T(8,128)S(1)}, u32[]{:S(2)}, u32[]{:S(2)}) collective-permute-start(f32[4,64,128]{2,1,0:T(8,128)S(1)} %corners.1), channel_id=1, source_target_pairs={{0,32},{4,36},{8,40},{12,44},{16,48},{20,52},{24,56},{28,60},{32,0... | collective-permute-start | bytes 393224 | tf_op jit(solution)/shard_map/ppermute | solution.py:439
  26.7 8.0 %collective-permute-start.12 = (f32[520,128]{1,0:T(8,128)S(1)}, f32[520,128]{1,0:T(8,128)S(1)}, u32[]{:S(2)}, u32[]{:S(2)}) collective-permute-start(f32[520,128]{1,0:T(8,128)S(1)} %get-tuple-element.38), channel_id=1, source_target_pairs={{0,32},{4,36},{8,40},{12,44},{16,48},{20,52},{24,56},{28,60},{32,0... | collective-permute-start | bytes 798728 | tf_op jit(solution)/shard_map/ppermute | solution.py:439
  29.7 9.3 %collective-permute-start.7 = (f32[264,128]{1,0:T(8,128)S(1)}, f32[264,128]{1,0:T(8,128)S(1)}, u32[]{:S(2)}, u32[]{:S(2)}) collective-permute-start(f32[264,128]{1,0:T(8,128)S(1)} %get-tuple-element.31), channel_id=1, source_target_pairs={{0,1},{1,2},{2,3},{3,0},{4,5},{5,6},{6,7},{7,4},{8,9},{9,10},{10,1... | collective-permute-start | bytes 405512 | tf_op jit(solution)/shard_map/ppermute | solution.py:452
  31.0 8.9 %collective-permute-start.8 = (f32[264,128]{1,0:T(8,128)S(1)}, f32[264,128]{1,0:T(8,128)S(1)}, u32[]{:S(2)}, u32[]{:S(2)}) collective-permute-start(f32[264,128]{1,0:T(8,128)S(1)} %get-tuple-element.32), channel_id=1, source_target_pairs={{0,2},{1,3},{2,0},{3,1},{4,6},{5,7},{6,4},{7,5},{8,10},{9,11},{10,... | collective-permute-start | bytes 405512 | tf_op jit(solution)/shard_map/ppermute | solution.py:452
  33.6 6.3 %collective-permute-start.9 = (f32[264,128]{1,0:T(8,128)S(1)}, f32[264,128]{1,0:T(8,128)S(1)}, u32[]{:S(2)}, u32[]{:S(2)}) collective-permute-start(f32[264,128]{1,0:T(8,128)S(1)} %get-tuple-element.33), channel_id=1, source_target_pairs={{0,3},{1,0},{2,1},{3,2},{4,7},{5,4},{6,5},{7,6},{8,11},{9,8},{10,9... | collective-permute-start | bytes 405512 | tf_op jit(solution)/shard_map/ppermute | solution.py:452
  35.5 11.3 %all-to-all-start = ((f32[16,40,128]{2,1,0:T(8,128)}), f32[16,40,128]{2,1,0:T(8,128)S(1)}, u32[]{:S(2)}, u32[]{:S(2)}) async-start(f32[16,40,128]{2,1,0:T(8,128)} %spread.1), calls=%async_computation | async-start | bytes 655360 | tf_op jit(solution)/shard_map/all_to_all | solution.py:515
  40.5 6.4 %collective-permute-start.10 = (f32[192,128]{1,0:T(8,128)S(1)}, f32[192,128]{1,0:T(8,128)S(1)}, u32[]{:S(2)}, u32[]{:S(2)}) collective-permute-start(f32[192,128]{1,0:T(8,128)S(1)} %get-tuple-element.34), channel_id=1, source_target_pairs={{0,4},{4,8},{8,12},{12,16},{16,20},{20,24},{24,28},{28,0},{32,36},... | collective-permute-start | bytes 294920 | tf_op jit(solution)/shard_map/ppermute | solution.py:439
  40.5 6.3 %collective-permute-start.11 = (f32[192,128]{1,0:T(8,128)S(1)}, f32[192,128]{1,0:T(8,128)S(1)}, u32[]{:S(2)}, u32[]{:S(2)}) collective-permute-start(f32[192,128]{1,0:T(8,128)S(1)} %get-tuple-element.35.after), channel_id=1, source_target_pairs={{0,28},{4,0},{8,4},{12,8},{16,12},{20,16},{24,20},{28,24},{32,60},... | collective-permute-start | bytes 294920 | tf_op jit(solution)/shard_map/ppermute | solution.py:439
  46.8 2.7 %collective-permute-start.15 = (f32[40,128]{1,0:T(8,128)S(1)}, f32[40,128]{1,0:T(8,128)S(1)}, u32[]{:S(2)}, u32[]{:S(2)}) collective-permute-start(f32[40,128]{1,0:T(8,128)S(1)} %sum.1.after.own), channel_id=1, source_target_pairs={{0,4},{4,0},{8,12},{12,8},{16,20},{20,16},{24,28},{28,24},{1,5},{5... | collective-permute-start | bytes 61448 | tf_op jit(solution)/shard_map/ppermute | solution.py:455
  47.0 3.3 %collective-permute-start.13 = (f32[2,64,128]{2,1,0:T(8,128)S(1)}, f32[2,64,128]{2,1,0:T(8,128)S(1)}, u32[]{:S(2)}, u32[]{:S(2)}) collective-permute-start(f32[2,64,128]{2,1,0:T(8,128)S(1)} %get-tuple-element.39.after), channel_id=1, source_target_pairs={{0,32},{4,36},{8,40},{12,44},{16,48},{20,52},{24,56},{28,60},{32,0... | collective-permute-start | bytes 196616 | tf_op jit(solution)/shard_map/ppermute | solution.py:439
  49.5 4.0 %collective-permute-start.14 = (f32[2,64,128]{2,1,0:T(8,128)S(1)}, f32[2,64,128]{2,1,0:T(8,128)S(1)}, u32[]{:S(2)}, u32[]{:S(2)}) collective-permute-start(f32[2,64,128]{2,1,0:T(8,128)S(1)} %get-tuple-element.40), channel_id=1, source_target_pairs={{0,224},{4,228},{8,232},{12,236},{16,240},{20,244},{24,248},{28,25... | collective-permute-start | bytes 196616 | tf_op jit(solution)/shard_map/ppermute | solution.py:439
  49.5 4.0 %collective-permute-start.19 = (f32[40,128]{1,0:T(8,128)S(1)}, f32[40,128]{1,0:T(8,128)S(1)}, u32[]{:S(2)}, u32[]{:S(2)}) collective-permute-start(f32[40,128]{1,0:T(8,128)S(1)} %pair.2.after.own), channel_id=1, source_target_pairs={{0,8},{4,12},{8,0},{12,4},{16,24},{20,28},{24,16},{28,20},{1,9},{5... | collective-permute-start | bytes 61448 | tf_op jit(solution)/shard_map/ppermute | solution.py:455
  53.5 6.1 %collective-permute-start.20 = (f32[40,128]{1,0:T(8,128)S(1)}, f32[40,128]{1,0:T(8,128)S(1)}, u32[]{:S(2)}, u32[]{:S(2)}) collective-permute-start(f32[40,128]{1,0:T(8,128)S(1)} %pair.3.own), channel_id=1, source_target_pairs={{0,28},{4,24},{8,20},{12,16},{16,12},{20,8},{24,4},{28,0},{1,29},{... | collective-permute-start | bytes 61448 | tf_op jit(solution)/shard_map/ppermute | solution.py:455
  55.2 19.5 %collective-permute-start.16 = (f32[256,256]{1,0:T(8,128)S(1)}, f32[256,256]{1,0:T(8,128)S(1)}, u32[]{:S(2)}, u32[]{:S(2)}) collective-permute-start(f32[256,256]{1,0:T(8,128)S(1)} %finish.1.one.after), channel_id=1, source_target_pairs={{0,1},{1,2},{2,3},{3,0},{4,5},{5,6},{6,7},{7,4},{8,9},{9,10},{10,1... | collective-permute-start | bytes 786440 | tf_op jit(solution)/shard_map/ppermute | solution.py:452
  56.1 18.6 %collective-permute-start.17 = (f32[256,256]{1,0:T(8,128)S(1)}, f32[256,256]{1,0:T(8,128)S(1)}, u32[]{:S(2)}, u32[]{:S(2)}) collective-permute-start(f32[256,256]{1,0:T(8,128)S(1)} %finish.1.one.after), channel_id=1, source_target_pairs={{0,2},{1,3},{2,0},{3,1},{4,6},{5,7},{6,4},{7,5},{8,10},{9,11},{10,... | collective-permute-start | bytes 786440 | tf_op jit(solution)/shard_map/ppermute | solution.py:452
  58.5 16.2 %collective-permute-start.18 = (f32[256,256]{1,0:T(8,128)S(1)}, f32[256,256]{1,0:T(8,128)S(1)}, u32[]{:S(2)}, u32[]{:S(2)}) collective-permute-start(f32[256,256]{1,0:T(8,128)S(1)} %finish.1.one.after), channel_id=1, source_target_pairs={{0,3},{1,0},{2,1},{3,2},{4,7},{5,4},{6,5},{7,6},{8,11},{9,8},{10,9... | collective-permute-start | bytes 786440 | tf_op jit(solution)/shard_map/ppermute | solution.py:452
  71.0 4.8 %collective-permute-start.21 = (f32[512,128]{1,0:T(8,128)S(1)}, f32[512,128]{1,0:T(8,128)S(1)}, u32[]{:S(2)}, u32[]{:S(2)}) collective-permute-start(f32[512,128]{1,0:T(8,128)S(1)} %bitcast.13), channel_id=1, source_target_pairs={{0,32},{4,36},{8,40},{12,44},{16,48},{20,52},{24,56},{28,60},{32,0... | collective-permute-start | bytes 786440 | tf_op jit(solution)/shard_map/ppermute | solution.py:439
  (1 other events, 1.2 us)

commit v5 on v4

--- a/solution.py
+++ b/solution.py
@@ -66,13 +66,18 @@
     right[...] = jnp.where(short, swap(upper[:, W:]), lower[:, W:])
 
 
-def sides_body(tile, to_left, to_right):
+def right_body(tile, to_right):
+    wide = low_lanes(W)
+    for part in range(4):
+        first, second = tile[part, :W, W:], tile[part, W:, W:]
+        to_right[part] = jnp.where(wide, swap(first), second)
+
+
+def left_body(tile, after, to_left):
     wide = low_lanes(W)
     for part in range(4):
         first, second = tile[part, :W, :W], tile[part, W:, :W]
         to_left[part] = jnp.where(wide, first, swap(second))
-        first, second = tile[part, :W, W:], tile[part, W:, W:]
-        to_right[part] = jnp.where(wide, swap(first), second)
 
 
 def strips_body(tile, after, to_core, to_far, far_left, far_right):
@@ -95,7 +100,11 @@
         out[part] = jnp.where(low, right, left)
 
 
-def phase_body(phase, far, right, left, real, imag):
+def guard_body(far, right, left, mark):
+    mark[...] = jnp.zeros_like(mark)
+
+
+def phase_body(phase, real, imag):
     real[...] = jnp.cos(phase[...])
     imag[...] = jnp.sin(phase[...])
 
@@ -148,6 +157,7 @@
     far_right,
     far_left,
     corners,
+    mark,
     probe,
     kernel_real,
     kernel_imag,
@@ -414,7 +424,7 @@
         slots_body,
         [message] * 4 + [share] * 2,
         (*args, *tables()),
-        [SMEM] * 2 + [VMEM] * 16,
+        [SMEM] * 2 + [VMEM] * 8 + [ANY] + [VMEM] * 8,
         scratch=[
             pltpu.VMEM((4, 3, TILE + 2 * HALF, W), F32),
             pltpu.VMEM((4, 2, W, W), F32),
@@ -456,7 +466,8 @@
 
     tile = specimen.reshape(4, TILE, TILE)
     strip, corner, side = (4, HALF, TILE), (4, HALF // 2, W), (4, W, W)
-    left, right = call(sides_body, [side, side], (tile,), [VMEM], name="sides")
+    (right,) = call(right_body, [side], (tile,), [VMEM], name="right")
+    (left,) = call(left_body, [side], (tile, right), [VMEM, ANY], name="left", flops=LONG)
     near, far, corner_left, corner_right = call(
         strips_body,
         [strip, strip, corner, corner],
@@ -472,13 +483,16 @@
         corners_body, [(4, HALF, W)], (from_right, from_left), [VMEM] * 2, name="corners"
     )
     corners = to_core(corners)
+    (mark,) = call(
+        guard_body,
+        [(8, W)],
+        (from_far, corner_right, corner_left),
+        [ANY] * 3,
+        name="guard",
+        flops=LONG,
+    )
     kernel_real, kernel_imag = call(
-        phase_body,
-        [(W, W)] * 2,
-        (kernel_phase, from_far, corner_right, corner_left),
-        [VMEM] + [ANY] * 3,
-        name="phase",
-        flops=LONG,
+        phase_body, [(W, W)] * 2, (kernel_phase,), [VMEM], name="phase"
     )
     rows = jnp.clip(offsets[0, 0, :, 0] + HALF, 0, TILE)
     cols = jnp.clip(offsets[0, 0, :, 1], -HALF, TILE - HALF)
@@ -494,6 +508,7 @@
         corner_right,
         corner_left,
         corners,
+        mark,
         probe_modes.reshape(2 * MODES, W, W),
         kernel_real,
         kernel_imag,

time: 77.2 us -> 76.5 us (level)
  waiting for transfers between devices: 9.15 us -> 7.38 us
    ppermute x3, starting transfers between devices: 1.84 us -> 4.32 us  [to_pair(): return lax.ppermute(value, 'tx', [(t, t ^ mask) for t in range(ntx)])]
    ppermute x13, waiting for transfers between devices: 4.66 us -> 2.44 us  [over_grid(): return lambda value: lax.ppermute(value, ('x', 'core', 'tx'), pairs)]
    ppermute x13, starting transfers between devices: 27.2 us -> 25.4 us  [over_grid(): return lambda value: lax.ppermute(value, ('x', 'core', 'tx'), pairs)]
    pallas_call x13 -> x15, Pallas kernels: 9.12 us -> 9.28 us  [call(): pl.pallas_call(body, out_shape=[jax.ShapeDtypeStruct(shape, F32) for shap...]
  transfers between devices with their start and end apart: 23 -> 23, of which waited for: 6 -> 8; matrix products, arithmetic and copies ran while one was open for 0% -> 0% of each run, Pallas kernels for 4% -> 4%
where the time goes in v5:
time: 76.5 us; the launch traced here: 76.2 us
  starting transfers between devices  42.7 us (56%)
  blocking collectives  11.7 us (15%)
  Pallas kernels  11.1 us (15%)
  waiting for transfers between devices  7.38 us (10%)
  between operations  1.73 us (2%)
  local copies, waits for them, and re-layouts  1.45 us (2%)
    ppermute x13, starting transfers between devices, over_grid(): return lambda value: lax.ppermute(value, ('x', 'core', 'tx'), pairs)  25.4 us
    all_to_all x1, blocking collectives, per_device(): mine = lax.all_to_all(spread, ('x', 'scan'), 0, 0).reshape(MODES * W, W)  11.7 us
    ppermute x6, starting transfers between devices, to_scan(): lax.ppermute(value, 'scan', [(s, (s + step) % nsc) for s in range(nsc)])  9.44 us
    pallas_call x15, Pallas kernels, call(): pl.pallas_call(body, out_shape=[jax.ShapeDtypeStruct(shape, F32) for shap...  9.28 us
    ppermute x3, starting transfers between devices, to_pair(): return lax.ppermute(value, 'tx', [(t, t ^ mask) for t in range(ntx)])  4.32 us
    all_to_all x1, starting transfers between devices, per_device(): chunks = lax.all_to_all(chunks, ('x', 'scan'), 0, 0)  3.54 us
    all_to_all x1, waiting for transfers between devices, per_device(): chunks = lax.all_to_all(chunks, ('x', 'scan'), 0, 0)  3.53 us
    ppermute x13, waiting for transfers between devices, over_grid(): return lambda value: lax.ppermute(value, ('x', 'core', 'tx'), pairs)  2.44 us
  transfers between devices with their start and end apart: 23, of which 8 were waited for; matrix products, arithmetic and copies ran while one was open for 0% of the time, Pallas kernels for 4%

profile of v5, /device:TPU:1, one launch (start us, length us, event | category | flops | bytes accessed | tf_op | source)
XLA Modules:
  0.0 76.2 jit_solution(8234993531476178650)
XLA Ops:
  0.6 1.2 %copy-done = f32[2,2,256,256]{3,2,1,0:T(8,128)S(1)} copy-done((f32[2,2,256,256]{3,2,1,0:T(8,128)S(1)}, f32[2,2,256,256]{3,2,1,0:T(8,128)}, u32[]{:S(2)}) %copy-start) | copy-done | bytes 1048600
  2.0 2.5 %collective-permute-start.1 = (f32[4,128,128]{2,1,0:T(8,128)S(1)}, f32[4,128,128]{2,1,0:T(8,128)S(1)}, u32[]{:S(2)}, u32[]{:S(2)}) collective-permute-start(f32[4,128,128]{2,1,0:T(8,128)S(1)} %right.1.after), channel_id=1, source_target_pairs={{0,4},{4,8},{8,12},{12,16},{16,20},{20,24},{24,28},{28,0},{32,36},... | collective-permute-start | bytes 786440 | tf_op jit(solution)/shard_map/ppermute | solution.py:449
  4.7 4.0 %collective-permute-start = (f32[4,128,128]{2,1,0:T(8,128)S(1)}, f32[4,128,128]{2,1,0:T(8,128)S(1)}, u32[]{:S(2)}, u32[]{:S(2)}) collective-permute-start(f32[4,128,128]{2,1,0:T(8,128)S(1)} %left.1.after), channel_id=1, source_target_pairs={{0,28},{4,0},{8,4},{12,8},{16,12},{20,16},{24,20},{28,24},{32,60},... | collective-permute-start | bytes 786440 | tf_op jit(solution)/shard_map/ppermute | solution.py:449
  8.8 2.1 %collective-permute-start.3 = (f32[4,64,256]{2,1,0:T(8,128)S(1)}, f32[4,64,256]{2,1,0:T(8,128)S(1)}, u32[]{:S(2)}, u32[]{:S(2)}) collective-permute-start(f32[4,64,256]{2,1,0:T(8,128)S(1)} %get-tuple-element.21), channel_id=1, source_target_pairs={{0,224},{4,228},{8,232},{12,236},{16,240},{20,244},{24,248},{28,25... | collective-permute-start | bytes 786440 | tf_op jit(solution)/shard_map/ppermute | solution.py:449
  11.0 1.5 %collective-permute-start.4 = (f32[4,32,128]{2,1,0:T(8,128)S(1)}, f32[4,32,128]{2,1,0:T(8,128)S(1)}, u32[]{:S(2)}, u32[]{:S(2)}) collective-permute-start(f32[4,32,128]{2,1,0:T(8,128)S(1)} %get-tuple-element.22), channel_id=1, source_target_pairs={{0,252},{4,224},{8,228},{12,232},{16,236},{20,240},{24,244},{28,24... | collective-permute-start | bytes 196616 | tf_op jit(solution)/shard_map/ppermute | solution.py:449
  12.5 1.1 %collective-permute-start.5 = (f32[4,32,128]{2,1,0:T(8,128)S(1)}, f32[4,32,128]{2,1,0:T(8,128)S(1)}, u32[]{:S(2)}, u32[]{:S(2)}) collective-permute-start(f32[4,32,128]{2,1,0:T(8,128)S(1)} %get-tuple-element.23), channel_id=1, source_target_pairs={{0,228},{4,232},{8,236},{12,240},{16,244},{20,248},{24,252},{28,22... | collective-permute-start | bytes 196616 | tf_op jit(solution)/shard_map/ppermute | solution.py:449
  15.1 2.1 %collective-permute-start.2 = (f32[4,64,256]{2,1,0:T(8,128)S(1)}, f32[4,64,256]{2,1,0:T(8,128)S(1)}, u32[]{:S(2)}, u32[]{:S(2)}) collective-permute-start(f32[4,64,256]{2,1,0:T(8,128)S(1)} %get-tuple-element.20), channel_id=1, source_target_pairs={{0,32},{4,36},{8,40},{12,44},{16,48},{20,52},{24,56},{28,60},{32,0... | collective-permute-start | bytes 786440 | tf_op jit(solution)/shard_map/ppermute | solution.py:449
  17.6 0.7 collective-permute-done.5.left.far_left
  18.4 0.5 collective-permute-done.6.corners
  18.9 6.9 %slots.1 = (f32[264,128]{1,0:T(8,128)S(1)}, f32[264,128]{1,0:T(8,128)S(1)}, f32[264,128]{1,0:T(8,128)S(1)}, f32[264,128]{1,0:T(8,128)S(1)}, f32[520,128]{1,0:T(8,128)S(1)}, /*index=5*/f32[520,128]{1,0:T(8,128)S(1)}) custom-call(s32[4]{0:T(128)S(1)} %reshape.62.starts, s32[1,1,1]{2,1,0:T(1,128)S(6)} %copy.13.live_counts, f32[4,256,256]{2,1,0:T(8,128)S(1)} %bitcast.12, ...), custom_call_target="tpu_custom_call" | custom-call | tf_op jit(solution)/shard_map/slots/pallas_call | solution.py:27
  25.8 2.5 %collective-permute-start.12 = (f32[520,128]{1,0:T(8,128)S(1)}, f32[520,128]{1,0:T(8,128)S(1)}, u32[]{:S(2)}, u32[]{:S(2)}) collective-permute-start(f32[520,128]{1,0:T(8,128)S(1)} %get-tuple-element.34), channel_id=1, source_target_pairs={{0,32},{4,36},{8,40},{12,44},{16,48},{20,52},{24,56},{28,60},{32,0... | collective-permute-start | bytes 798728 | tf_op jit(solution)/shard_map/ppermute | solution.py:449
  28.3 1.3 %collective-permute-start.7 = (f32[264,128]{1,0:T(8,128)S(1)}, f32[264,128]{1,0:T(8,128)S(1)}, u32[]{:S(2)}, u32[]{:S(2)}) collective-permute-start(f32[264,128]{1,0:T(8,128)S(1)} %get-tuple-element.27), channel_id=1, source_target_pairs={{0,1},{1,2},{2,3},{3,0},{4,5},{5,6},{6,7},{7,4},{8,9},{9,10},{10,1... | collective-permute-start | bytes 405512 | tf_op jit(solution)/shard_map/ppermute | solution.py:462
  29.6 2.6 %collective-permute-start.8 = (f32[264,128]{1,0:T(8,128)S(1)}, f32[264,128]{1,0:T(8,128)S(1)}, u32[]{:S(2)}, u32[]{:S(2)}) collective-permute-start(f32[264,128]{1,0:T(8,128)S(1)} %get-tuple-element.28), channel_id=1, source_target_pairs={{0,2},{1,3},{2,0},{3,1},{4,6},{5,7},{6,4},{7,5},{8,10},{9,11},{10,... | collective-permute-start | bytes 405512 | tf_op jit(solution)/shard_map/ppermute | solution.py:462
  32.2 1.1 %collective-permute-start.9 = (f32[264,128]{1,0:T(8,128)S(1)}, f32[264,128]{1,0:T(8,128)S(1)}, u32[]{:S(2)}, u32[]{:S(2)}) collective-permute-start(f32[264,128]{1,0:T(8,128)S(1)} %get-tuple-element.29), channel_id=1, source_target_pairs={{0,3},{1,0},{2,1},{3,2},{4,7},{5,4},{6,5},{7,6},{8,11},{9,8},{10,9... | collective-permute-start | bytes 405512 | tf_op jit(solution)/shard_map/ppermute | solution.py:462
  33.3 0.8 %spread.1 = f32[16,40,128]{2,1,0:T(8,128)} custom-call(f32[520,128]{1,0:T(8,128)S(1)} %get-tuple-element.33.keep, f32[520,128]{1,0:T(8,128)S(1)} %collective-permute-done.12.got), custom_call_target="tpu_custom_call" | custom-call | flops 10000000000 | tf_op jit(solution)/shard_map/spread/pallas_call | solution.py:27
  34.1 3.5 %all-to-all-start = ((f32[16,40,128]{2,1,0:T(8,128)}), f32[16,40,128]{2,1,0:T(8,128)S(1)}, u32[]{:S(2)}, u32[]{:S(2)}) async-start(f32[16,40,128]{2,1,0:T(8,128)} %spread.1), calls=%async_computation | async-start | bytes 655360 | tf_op jit(solution)/shard_map/all_to_all | solution.py:530
  37.6 0.9 %collective-permute-done.8.three = f32[264,128]{1,0:T(8,128)S(1)} collective-permute-done((f32[264,128]{1,0:T(8,128)S(1)}, f32[264,128]{1,0:T(8,128)S(1)}, u32[]{:S(2)}, u32[]{:S(2)}) %collective-permute-start.8) | collective-permute-done | bytes 135200 | tf_op jit(solution)/shard_map/ppermute | solution.py:462
  38.6 0.5 place.1
  39.2 2.7 %collective-permute-start.11 = (f32[192,128]{1,0:T(8,128)S(1)}, f32[192,128]{1,0:T(8,128)S(1)}, u32[]{:S(2)}, u32[]{:S(2)}) collective-permute-start(f32[192,128]{1,0:T(8,128)S(1)} %get-tuple-element.31.after), channel_id=1, source_target_pairs={{0,28},{4,0},{8,4},{12,8},{16,12},{20,16},{24,20},{28,24},{32,60},... | collective-permute-start | bytes 294920 | tf_op jit(solution)/shard_map/ppermute | solution.py:449
  41.8 3.5 %all-to-all-done.chunks = f32[16,40,128]{2,1,0:T(8,128)S(1)} async-done(((f32[16,40,128]{2,1,0:T(8,128)}), f32[16,40,128]{2,1,0:T(8,128)S(1)}, u32[]{:S(2)}, u32[]{:S(2)}) %all-to-all-start) | async-done | bytes 327712 | tf_op jit(solution)/shard_map/all_to_all | solution.py:530
  45.6 2.4 %collective-permute-start.13 = (f32[2,64,128]{2,1,0:T(8,128)S(1)}, f32[2,64,128]{2,1,0:T(8,128)S(1)}, u32[]{:S(2)}, u32[]{:S(2)}) collective-permute-start(f32[2,64,128]{2,1,0:T(8,128)S(1)} %get-tuple-element.35.after), channel_id=1, source_target_pairs={{0,32},{4,36},{8,40},{12,44},{16,48},{20,52},{24,56},{28,60},{32,0... | collective-permute-start | bytes 196616 | tf_op jit(solution)/shard_map/ppermute | solution.py:449
  48.1 3.0 %collective-permute-start.19 = (f32[40,128]{1,0:T(8,128)S(1)}, f32[40,128]{1,0:T(8,128)S(1)}, u32[]{:S(2)}, u32[]{:S(2)}) collective-permute-start(f32[40,128]{1,0:T(8,128)S(1)} %pair.2.after.own), channel_id=1, source_target_pairs={{0,8},{4,12},{8,0},{12,4},{16,24},{20,28},{24,16},{28,20},{1,9},{5... | collective-permute-start | bytes 61448 | tf_op jit(solution)/shard_map/ppermute | solution.py:465
  51.1 1.0 %collective-permute-done.14.from_far = f32[2,64,128]{2,1,0:T(8,128)S(1)} collective-permute-done((f32[2,64,128]{2,1,0:T(8,128)S(1)}, f32[2,64,128]{2,1,0:T(8,128)S(1)}, u32[]{:S(2)}, u32[]{:S(2)}) %collective-permute-start.14) | collective-permute-done | bytes 65568 | tf_op jit(solution)/shard_map/ppermute | solution.py:449
  52.1 0.4 collective-permute-done.19.got
  52.6 1.2 %collective-permute-start.20 = (f32[40,128]{1,0:T(8,128)S(1)}, f32[40,128]{1,0:T(8,128)S(1)}, u32[]{:S(2)}, u32[]{:S(2)}) collective-permute-start(f32[40,128]{1,0:T(8,128)S(1)} %pair.3.own), channel_id=1, source_target_pairs={{0,28},{4,24},{8,20},{12,16},{16,12},{20,8},{24,4},{28,0},{1,29},{... | collective-permute-start | bytes 61448 | tf_op jit(solution)/shard_map/ppermute | solution.py:465
  53.8 0.9 %collective-permute-start.16 = (f32[256,256]{1,0:T(8,128)S(1)}, f32[256,256]{1,0:T(8,128)S(1)}, u32[]{:S(2)}, u32[]{:S(2)}) collective-permute-start(f32[256,256]{1,0:T(8,128)S(1)} %finish.1.one.after), channel_id=1, source_target_pairs={{0,1},{1,2},{2,3},{3,0},{4,5},{5,6},{6,7},{7,4},{8,9},{9,10},{10,1... | collective-permute-start | bytes 786440 | tf_op jit(solution)/shard_map/ppermute | solution.py:462
  54.7 2.4 %collective-permute-start.17 = (f32[256,256]{1,0:T(8,128)S(1)}, f32[256,256]{1,0:T(8,128)S(1)}, u32[]{:S(2)}, u32[]{:S(2)}) collective-permute-start(f32[256,256]{1,0:T(8,128)S(1)} %finish.1.one.after), channel_id=1, source_target_pairs={{0,2},{1,3},{2,0},{3,1},{4,6},{5,7},{6,4},{7,5},{8,10},{9,11},{10,... | collective-permute-start | bytes 786440 | tf_op jit(solution)/shard_map/ppermute | solution.py:462
  57.1 1.2 %collective-permute-start.18 = (f32[256,256]{1,0:T(8,128)S(1)}, f32[256,256]{1,0:T(8,128)S(1)}, u32[]{:S(2)}, u32[]{:S(2)}) collective-permute-start(f32[256,256]{1,0:T(8,128)S(1)} %finish.1.one.after), channel_id=1, source_target_pairs={{0,3},{1,0},{2,1},{3,2},{4,7},{5,4},{6,5},{7,6},{8,11},{9,8},{10,9... | collective-permute-start | bytes 786440 | tf_op jit(solution)/shard_map/ppermute | solution.py:462
  58.3 11.7 %all_to_all.10 = f32[16,32,128]{2,1,0:T(8,128)S(1)} all-to-all(f32[16,32,128]{2,1,0:T(8,128)S(1)} %mean.1), channel_id=1, replica_groups=mesh['x'=4,'core'=2,'tx'=8,'scan'=4] {'x','scan'}, dimensions={0} | all-to-all | bytes 524288 | tf_op jit(solution)/shard_map/all_to_all | solution.py:580
  70.0 4.1 %collective-permute-start.21 = (f32[512,128]{1,0:T(8,128)S(1)}, f32[512,128]{1,0:T(8,128)S(1)}, u32[]{:S(2)}, u32[]{:S(2)}) collective-permute-start(f32[512,128]{1,0:T(8,128)S(1)} %bitcast.14), channel_id=1, source_target_pairs={{0,32},{4,36},{8,40},{12,44},{16,48},{20,52},{24,56},{28,60},{32,0... | collective-permute-start | bytes 786440 | tf_op jit(solution)/shard_map/ppermute | solution.py:449
  74.1 1.0 %gather.1 = f32[4,256,256]{2,1,0:T(8,128)} custom-call(f32[256,256]{1,0:T(8,128)S(1)} %finish.1.one.after, f32[256,256]{1,0:T(8,128)S(1)} %collective-permute-done.16.two, f32[256,256]{1,0:T(8,128)S(1)} %collective-permute-done.17.three, f32[256,256]{1,0:T(8,128)S(1)} %collective-permute-done.18.four), custom_call_target="tpu_custom_call" | custom-call | flops 10000000000 | tf_op jit(solution)/shard_map/gather/pallas_call | solution.py:395
  75.3 0.8 %halves.1 = f32[2,512,128]{2,1,0:T(8,128)} custom-call(f32[512,128]{1,0:T(8,128)S(1)} %bitcast.15, f32[512,128]{1,0:T(8,128)S(1)} %collective-permute-done.21.other), custom_call_target="tpu_custom_call" | custom-call | flops 10000000000 | tf_op jit(solution)/shard_map/halves/pallas_call | solution.py:395
  (57 shorter events, 2.2 us)
Async XLA Ops:
  2.0 15.2 %collective-permute-start.1 = (f32[4,128,128]{2,1,0:T(8,128)S(1)}, f32[4,128,128]{2,1,0:T(8,128)S(1)}, u32[]{:S(2)}, u32[]{:S(2)}) collective-permute-start(f32[4,128,128]{2,1,0:T(8,128)S(1)} %right.1.after), channel_id=1, source_target_pairs={{0,4},{4,8},{8,12},{12,16},{16,20},{20,24},{24,28},{28,0},{32,36},... | collective-permute-start | bytes 786440 | tf_op jit(solution)/shard_map/ppermute | solution.py:449
  4.7 10.4 %collective-permute-start = (f32[4,128,128]{2,1,0:T(8,128)S(1)}, f32[4,128,128]{2,1,0:T(8,128)S(1)}, u32[]{:S(2)}, u32[]{:S(2)}) collective-permute-start(f32[4,128,128]{2,1,0:T(8,128)S(1)} %left.1.after), channel_id=1, source_target_pairs={{0,28},{4,0},{8,4},{12,8},{16,12},{20,16},{24,20},{28,24},{32,60},... | collective-permute-start | bytes 786440 | tf_op jit(solution)/shard_map/ppermute | solution.py:449
  8.7 6.0 %copy-start.8 = (f32[128,128]{1,0:T(8,128)S(1)}, f32[128,128]{1,0:T(8,128)}, u32[]{:S(2)}) copy-start(f32[128,128]{1,0:T(8,128)} %phase.3) | copy-start | bytes 196612
  8.8 9.5 %collective-permute-start.3 = (f32[4,64,256]{2,1,0:T(8,128)S(1)}, f32[4,64,256]{2,1,0:T(8,128)S(1)}, u32[]{:S(2)}, u32[]{:S(2)}) collective-permute-start(f32[4,64,256]{2,1,0:T(8,128)S(1)} %get-tuple-element.21), channel_id=1, source_target_pairs={{0,224},{4,228},{8,232},{12,236},{16,240},{20,244},{24,248},{28,25... | collective-permute-start | bytes 786440 | tf_op jit(solution)/shard_map/ppermute | solution.py:449
  11.0 2.6 %copy-start.9 = (s32[1,1,2,2]{3,2,1,0:T(2,128)S(1)}, s32[1,1,2,2]{3,2,1,0:T(2,128)}, u32[]{:S(2)}) copy-start(s32[1,1,2,2]{3,2,1,0:T(2,128)} %param.13) | copy-start | bytes 52
  11.0 6.6 %collective-permute-start.4 = (f32[4,32,128]{2,1,0:T(8,128)S(1)}, f32[4,32,128]{2,1,0:T(8,128)S(1)}, u32[]{:S(2)}, u32[]{:S(2)}) collective-permute-start(f32[4,32,128]{2,1,0:T(8,128)S(1)} %get-tuple-element.22), channel_id=1, source_target_pairs={{0,252},{4,224},{8,228},{12,232},{16,236},{20,240},{24,244},{28,24... | collective-permute-start | bytes 196616 | tf_op jit(solution)/shard_map/ppermute | solution.py:449
  12.5 5.8 %collective-permute-start.5 = (f32[4,32,128]{2,1,0:T(8,128)S(1)}, f32[4,32,128]{2,1,0:T(8,128)S(1)}, u32[]{:S(2)}, u32[]{:S(2)}) collective-permute-start(f32[4,32,128]{2,1,0:T(8,128)S(1)} %get-tuple-element.23), channel_id=1, source_target_pairs={{0,228},{4,232},{8,236},{12,240},{16,244},{20,248},{24,252},{28,22... | collective-permute-start | bytes 196616 | tf_op jit(solution)/shard_map/ppermute | solution.py:449
  15.1 3.3 %collective-permute-start.2 = (f32[4,64,256]{2,1,0:T(8,128)S(1)}, f32[4,64,256]{2,1,0:T(8,128)S(1)}, u32[]{:S(2)}, u32[]{:S(2)}) collective-permute-start(f32[4,64,256]{2,1,0:T(8,128)S(1)} %get-tuple-element.20), channel_id=1, source_target_pairs={{0,32},{4,36},{8,40},{12,44},{16,48},{20,52},{24,56},{28,60},{32,0... | collective-permute-start | bytes 786440 | tf_op jit(solution)/shard_map/ppermute | solution.py:449
  17.4 1.5 %copy-start.1 = (f32[2,2,256,256]{3,2,1,0:T(8,128)S(1)}, f32[2,2,256,256]{3,2,1,0:T(8,128)}, u32[]{:S(2)}) copy-start(f32[2,2,256,256]{3,2,1,0:T(8,128)} %param.10) | copy-start | bytes 3145732
  17.4 1.5 %copy-start.2 = (f32[4,2,128,128]{3,2,1,0:T(8,128)S(1)}, f32[4,2,128,128]{3,2,1,0:T(8,128)}, u32[]{:S(2)}) copy-start(f32[4,2,128,128]{3,2,1,0:T(8,128)} %param.11) | copy-start | bytes 1572868
  17.4 1.5 %copy-start.3 = (f32[1,1,2,128,128]{4,3,2,1,0:T(8,128)S(1)}, f32[1,1,2,128,128]{4,3,2,1,0:T(8,128)}, u32[]{:S(2)}) copy-start(f32[1,1,2,128,128]{4,3,2,1,0:T(8,128)} %param.15) | copy-start | bytes 393220
  17.4 1.5 %copy-start.4 = (bf16[256,256]{1,0:T(8,128)(2,1)S(1)}, bf16[256,256]{1,0:T(8,128)(2,1)}, u32[]{:S(2)}) copy-start(bf16[256,256]{1,0:T(8,128)(2,1)} %constant.9.clone.right_high) | copy-start | bytes 393220
  17.4 1.5 %copy-start.5 = (bf16[256,256]{1,0:T(8,128)(2,1)S(1)}, bf16[256,256]{1,0:T(8,128)(2,1)}, u32[]{:S(2)}) copy-start(bf16[256,256]{1,0:T(8,128)(2,1)} %constant.22.clone.right_low) | copy-start | bytes 393220
  17.4 1.5 %copy-start.6 = (bf16[256,256]{1,0:T(8,128)(2,1)S(1)}, bf16[256,256]{1,0:T(8,128)(2,1)}, u32[]{:S(2)}) copy-start(bf16[256,256]{1,0:T(8,128)(2,1)} %constant.23.clone.left_high) | copy-start | bytes 393220
  17.5 1.5 %copy-start.7 = (bf16[256,256]{1,0:T(8,128)(2,1)S(1)}, bf16[256,256]{1,0:T(8,128)(2,1)}, u32[]{:S(2)}) copy-start(bf16[256,256]{1,0:T(8,128)(2,1)} %constant.24.clone.left_low) | copy-start | bytes 393220
  17.5 1.4 %collective-permute-start.6 = (f32[4,64,128]{2,1,0:T(8,128)S(1)}, f32[4,64,128]{2,1,0:T(8,128)S(1)}, u32[]{:S(2)}, u32[]{:S(2)}) collective-permute-start(f32[4,64,128]{2,1,0:T(8,128)S(1)} %corners.1), channel_id=1, source_target_pairs={{0,32},{4,36},{8,40},{12,44},{16,48},{20,52},{24,56},{28,60},{32,0... | collective-permute-start | bytes 393224 | tf_op jit(solution)/shard_map/ppermute | solution.py:449
  25.8 7.5 %collective-permute-start.12 = (f32[520,128]{1,0:T(8,128)S(1)}, f32[520,128]{1,0:T(8,128)S(1)}, u32[]{:S(2)}, u32[]{:S(2)}) collective-permute-start(f32[520,128]{1,0:T(8,128)S(1)} %get-tuple-element.34), channel_id=1, source_target_pairs={{0,32},{4,36},{8,40},{12,44},{16,48},{20,52},{24,56},{28,60},{32,0... | collective-permute-start | bytes 798728 | tf_op jit(solution)/shard_map/ppermute | solution.py:449
  28.3 9.3 %collective-permute-start.7 = (f32[264,128]{1,0:T(8,128)S(1)}, f32[264,128]{1,0:T(8,128)S(1)}, u32[]{:S(2)}, u32[]{:S(2)}) collective-permute-start(f32[264,128]{1,0:T(8,128)S(1)} %get-tuple-element.27), channel_id=1, source_target_pairs={{0,1},{1,2},{2,3},{3,0},{4,5},{5,6},{6,7},{7,4},{8,9},{9,10},{10,1... | collective-permute-start | bytes 405512 | tf_op jit(solution)/shard_map/ppermute | solution.py:462
  29.6 8.9 %collective-permute-start.8 = (f32[264,128]{1,0:T(8,128)S(1)}, f32[264,128]{1,0:T(8,128)S(1)}, u32[]{:S(2)}, u32[]{:S(2)}) collective-permute-start(f32[264,128]{1,0:T(8,128)S(1)} %get-tuple-element.28), channel_id=1, source_target_pairs={{0,2},{1,3},{2,0},{3,1},{4,6},{5,7},{6,4},{7,5},{8,10},{9,11},{10,... | collective-permute-start | bytes 405512 | tf_op jit(solution)/shard_map/ppermute | solution.py:462
  32.2 6.3 %collective-permute-start.9 = (f32[264,128]{1,0:T(8,128)S(1)}, f32[264,128]{1,0:T(8,128)S(1)}, u32[]{:S(2)}, u32[]{:S(2)}) collective-permute-start(f32[264,128]{1,0:T(8,128)S(1)} %get-tuple-element.29), channel_id=1, source_target_pairs={{0,3},{1,0},{2,1},{3,2},{4,7},{5,4},{6,5},{7,6},{8,11},{9,8},{10,9... | collective-permute-start | bytes 405512 | tf_op jit(solution)/shard_map/ppermute | solution.py:462
  34.1 11.3 %all-to-all-start = ((f32[16,40,128]{2,1,0:T(8,128)}), f32[16,40,128]{2,1,0:T(8,128)S(1)}, u32[]{:S(2)}, u32[]{:S(2)}) async-start(f32[16,40,128]{2,1,0:T(8,128)} %spread.1), calls=%async_computation | async-start | bytes 655360 | tf_op jit(solution)/shard_map/all_to_all | solution.py:530
  39.1 6.4 %collective-permute-start.10 = (f32[192,128]{1,0:T(8,128)S(1)}, f32[192,128]{1,0:T(8,128)S(1)}, u32[]{:S(2)}, u32[]{:S(2)}) collective-permute-start(f32[192,128]{1,0:T(8,128)S(1)} %get-tuple-element.30), channel_id=1, source_target_pairs={{0,4},{4,8},{8,12},{12,16},{16,20},{20,24},{24,28},{28,0},{32,36},... | collective-permute-start | bytes 294920 | tf_op jit(solution)/shard_map/ppermute | solution.py:449
  39.2 6.3 %collective-permute-start.11 = (f32[192,128]{1,0:T(8,128)S(1)}, f32[192,128]{1,0:T(8,128)S(1)}, u32[]{:S(2)}, u32[]{:S(2)}) collective-permute-start(f32[192,128]{1,0:T(8,128)S(1)} %get-tuple-element.31.after), channel_id=1, source_target_pairs={{0,28},{4,0},{8,4},{12,8},{16,12},{20,16},{24,20},{28,24},{32,60},... | collective-permute-start | bytes 294920 | tf_op jit(solution)/shard_map/ppermute | solution.py:449
  45.4 2.7 %collective-permute-start.15 = (f32[40,128]{1,0:T(8,128)S(1)}, f32[40,128]{1,0:T(8,128)S(1)}, u32[]{:S(2)}, u32[]{:S(2)}) collective-permute-start(f32[40,128]{1,0:T(8,128)S(1)} %sum.1.after.own), channel_id=1, source_target_pairs={{0,4},{4,0},{8,12},{12,8},{16,20},{20,16},{24,28},{28,24},{1,5},{5... | collective-permute-start | bytes 61448 | tf_op jit(solution)/shard_map/ppermute | solution.py:465
  45.6 5.4 %collective-permute-start.13 = (f32[2,64,128]{2,1,0:T(8,128)S(1)}, f32[2,64,128]{2,1,0:T(8,128)S(1)}, u32[]{:S(2)}, u32[]{:S(2)}) collective-permute-start(f32[2,64,128]{2,1,0:T(8,128)S(1)} %get-tuple-element.35.after), channel_id=1, source_target_pairs={{0,32},{4,36},{8,40},{12,44},{16,48},{20,52},{24,56},{28,60},{32,0... | collective-permute-start | bytes 196616 | tf_op jit(solution)/shard_map/ppermute | solution.py:449
  48.1 4.0 %collective-permute-start.14 = (f32[2,64,128]{2,1,0:T(8,128)S(1)}, f32[2,64,128]{2,1,0:T(8,128)S(1)}, u32[]{:S(2)}, u32[]{:S(2)}) collective-permute-start(f32[2,64,128]{2,1,0:T(8,128)S(1)} %get-tuple-element.36), channel_id=1, source_target_pairs={{0,224},{4,228},{8,232},{12,236},{16,240},{20,244},{24,248},{28,25... | collective-permute-start | bytes 196616 | tf_op jit(solution)/shard_map/ppermute | solution.py:449
  48.1 4.5 %collective-permute-start.19 = (f32[40,128]{1,0:T(8,128)S(1)}, f32[40,128]{1,0:T(8,128)S(1)}, u32[]{:S(2)}, u32[]{:S(2)}) collective-permute-start(f32[40,128]{1,0:T(8,128)S(1)} %pair.2.after.own), channel_id=1, source_target_pairs={{0,8},{4,12},{8,0},{12,4},{16,24},{20,28},{24,16},{28,20},{1,9},{5... | collective-permute-start | bytes 61448 | tf_op jit(solution)/shard_map/ppermute | solution.py:465
  52.6 5.7 %collective-permute-start.20 = (f32[40,128]{1,0:T(8,128)S(1)}, f32[40,128]{1,0:T(8,128)S(1)}, u32[]{:S(2)}, u32[]{:S(2)}) collective-permute-start(f32[40,128]{1,0:T(8,128)S(1)} %pair.3.own), channel_id=1, source_target_pairs={{0,28},{4,24},{8,20},{12,16},{16,12},{20,8},{24,4},{28,0},{1,29},{... | collective-permute-start | bytes 61448 | tf_op jit(solution)/shard_map/ppermute | solution.py:465
  53.8 20.3 %collective-permute-start.16 = (f32[256,256]{1,0:T(8,128)S(1)}, f32[256,256]{1,0:T(8,128)S(1)}, u32[]{:S(2)}, u32[]{:S(2)}) collective-permute-start(f32[256,256]{1,0:T(8,128)S(1)} %finish.1.one.after), channel_id=1, source_target_pairs={{0,1},{1,2},{2,3},{3,0},{4,5},{5,6},{6,7},{7,4},{8,9},{9,10},{10,1... | collective-permute-start | bytes 786440 | tf_op jit(solution)/shard_map/ppermute | solution.py:462
  54.7 19.4 %collective-permute-start.17 = (f32[256,256]{1,0:T(8,128)S(1)}, f32[256,256]{1,0:T(8,128)S(1)}, u32[]{:S(2)}, u32[]{:S(2)}) collective-permute-start(f32[256,256]{1,0:T(8,128)S(1)} %finish.1.one.after), channel_id=1, source_target_pairs={{0,2},{1,3},{2,0},{3,1},{4,6},{5,7},{6,4},{7,5},{8,10},{9,11},{10,... | collective-permute-start | bytes 786440 | tf_op jit(solution)/shard_map/ppermute | solution.py:462
  57.1 17.0 %collective-permute-start.18 = (f32[256,256]{1,0:T(8,128)S(1)}, f32[256,256]{1,0:T(8,128)S(1)}, u32[]{:S(2)}, u32[]{:S(2)}) collective-permute-start(f32[256,256]{1,0:T(8,128)S(1)} %finish.1.one.after), channel_id=1, source_target_pairs={{0,3},{1,0},{2,1},{3,2},{4,7},{5,4},{6,5},{7,6},{8,11},{9,8},{10,9... | collective-permute-start | bytes 786440 | tf_op jit(solution)/shard_map/ppermute | solution.py:462
  70.0 5.3 %collective-permute-start.21 = (f32[512,128]{1,0:T(8,128)S(1)}, f32[512,128]{1,0:T(8,128)S(1)}, u32[]{:S(2)}, u32[]{:S(2)}) collective-permute-start(f32[512,128]{1,0:T(8,128)S(1)} %bitcast.14), channel_id=1, source_target_pairs={{0,32},{4,36},{8,40},{12,44},{16,48},{20,52},{24,56},{28,60},{32,0... | collective-permute-start | bytes 786440 | tf_op jit(solution)/shard_map/ppermute | solution.py:449
  (1 other events, 1.2 us)

commit v6 on v5

--- a/solution.py
+++ b/solution.py
@@ -16,6 +16,7 @@
 ANY = pl.BlockSpec(memory_space=pl.ANY)
 LONG = 10**10
 CODE = 512
+STEPS = (0, 2, 1, 3)
 PARAMS = pltpu.CompilerParams(vmem_limit_bytes=48 * 1024 * 1024)
 W = 128
 HALF = 64
@@ -380,26 +381,27 @@
         out[pl.ds(far_row, HALF), span] += from_far[k]
 
 
-def gather_body(one, two, three, four, out, sems):
-    scan = lax.axis_index("scan")
-    parts = enumerate((one, two, three, four))
-    copy_all([(part, out.at[lax.rem(scan + 4 - step, 4)]) for step, part in parts], sems)
-
-
-def halves_body(mine, other, out, sems):
-    core = lax.axis_index("core")
-    copy_all([(mine, out.at[core]), (other, out.at[1 - core])], sems)
-
-
-def place_parts(body, shape, parts, name):
+def gather_body(one, two, three, four, mine, object_grad, probe_grad, sems):
+    scan, core = lax.axis_index("scan"), lax.axis_index("core")
+    parts = zip(STEPS, (one, two, three, four))
+    pairs = [(part, object_grad.at[lax.rem(scan + 4 - step, 4)]) for step, part in parts]
+    copy_all(pairs + [(mine, probe_grad.at[core])], sems)
+
+
+def other_body(probe_grad, other, out, sems):
+    copy_all([(other, out.at[1 - lax.axis_index("core")])], sems)
+
+
+def place_parts(body, shapes, parts, name, aliases=None):
     return pl.pallas_call(
         body,
-        out_shape=jax.ShapeDtypeStruct(shape, F32),
+        out_shape=[jax.ShapeDtypeStruct(shape, F32) for shape in shapes],
         in_specs=[ANY] * len(parts),
-        out_specs=ANY,
+        out_specs=[ANY] * len(shapes),
         scratch_shapes=[pltpu.SemaphoreType.DMA((len(parts),))],
         compiler_params=PARAMS,
         cost_estimate=pl.CostEstimate(flops=LONG, bytes_accessed=0, transcendentals=0),
+        input_output_aliases=aliases or {},
         name=name,
     )(*parts)
 
@@ -564,7 +566,7 @@
         name="finish",
         flops=LONG,
     )
-    quarters = [quarter] + [to_scan(quarter, step) for step in range(1, nsc)]
+    quarters = [quarter] + [to_scan(quarter, step) for step in STEPS[1:]]
     (share,) = call(
         pair_body, [(rows + 8, W)], (share, got, quarter), [VMEM] * 2 + [ANY], name="pair", flops=LONG
     )
@@ -579,8 +581,11 @@
     )
     mine = lax.all_to_all(spread, ("x", "scan"), 0, 0).reshape(MODES * W, W)
     other = to_core(mine)
-    probe_grad = place_parts(halves_body, (2, MODES * W, W), (mine, other), "halves")
-    object_grad = place_parts(gather_body, (4, TILE, TILE), quarters, "gather")
+    both = (2, MODES * W, W)
+    object_grad, probe_grad = place_parts(
+        gather_body, [(4, TILE, TILE), both], (*quarters, mine), "gather"
+    )
+    (probe_grad,) = place_parts(other_body, [both], (probe_grad, other), "other", {0: 0})
     return object_grad.reshape(specimen.shape), probe_grad.reshape(probe_modes.shape)
 
 

time: 76.5 us -> 76.3 us (level)
    ppermute x13, starting transfers between devices: 25.4 us -> 24.6 us  [over_grid(): return lambda value: lax.ppermute(value, ('x', 'core', 'tx'), pairs)]
  transfers between devices with their start and end apart: 23 -> 23, of which waited for: 8 -> 7; matrix products, arithmetic and copies ran while one was open for 0% -> 0% of each run, Pallas kernels for 4% -> 4%
where the time goes in v6:
time: 76.3 us; the launch traced here: 76 us
  starting transfers between devices  42.5 us (56%)
  blocking collectives  11.7 us (15%)
  Pallas kernels  11.1 us (15%)
  waiting for transfers between devices  7.28 us (10%)
  between operations  1.73 us (2%)
  local copies, waits for them, and re-layouts  1.45 us (2%)
    ppermute x13, starting transfers between devices, over_grid(): return lambda value: lax.ppermute(value, ('x', 'core', 'tx'), pairs)  24.6 us
    all_to_all x1, blocking collectives, per_device(): mine = lax.all_to_all(spread, ('x', 'scan'), 0, 0).reshape(MODES * W, W)  11.7 us
    ppermute x6, starting transfers between devices, to_scan(): lax.ppermute(value, 'scan', [(s, (s + step) % nsc) for s in range(nsc)])  10.1 us
    pallas_call x15, Pallas kernels, call(): pl.pallas_call(body, out_shape=[jax.ShapeDtypeStruct(shape, F32) for shap...  9.27 us
    ppermute x3, starting transfers between devices, to_pair(): return lax.ppermute(value, 'tx', [(t, t ^ mask) for t in range(ntx)])  4.31 us
    all_to_all x1, starting transfers between devices, per_device(): chunks = lax.all_to_all(chunks, ('x', 'scan'), 0, 0)  3.54 us
    all_to_all x1, waiting for transfers between devices, per_device(): chunks = lax.all_to_all(chunks, ('x', 'scan'), 0, 0)  3.52 us
    ppermute x13, waiting for transfers between devices, over_grid(): return lambda value: lax.ppermute(value, ('x', 'core', 'tx'), pairs)  2.35 us
  transfers between devices with their start and end apart: 23, of which 7 were waited for; matrix products, arithmetic and copies ran while one was open for 0% of the time, Pallas kernels for 4%

profile of v6, /device:TPU:1, one launch (start us, length us, event | category | flops | bytes accessed | tf_op | source)
XLA Modules:
  0.0 76.0 jit_solution(3544783441189590176)
XLA Ops:
  0.6 1.2 %copy-done = f32[2,2,256,256]{3,2,1,0:T(8,128)S(1)} copy-done((f32[2,2,256,256]{3,2,1,0:T(8,128)S(1)}, f32[2,2,256,256]{3,2,1,0:T(8,128)}, u32[]{:S(2)}) %copy-start) | copy-done | bytes 1048600
  2.0 2.5 %collective-permute-start.1 = (f32[4,128,128]{2,1,0:T(8,128)S(1)}, f32[4,128,128]{2,1,0:T(8,128)S(1)}, u32[]{:S(2)}, u32[]{:S(2)}) collective-permute-start(f32[4,128,128]{2,1,0:T(8,128)S(1)} %right.1.after), channel_id=1, source_target_pairs={{0,4},{4,8},{8,12},{12,16},{16,20},{20,24},{24,28},{28,0},{32,36},... | collective-permute-start | bytes 786440 | tf_op jit(solution)/shard_map/ppermute | solution.py:451
  4.7 4.0 %collective-permute-start = (f32[4,128,128]{2,1,0:T(8,128)S(1)}, f32[4,128,128]{2,1,0:T(8,128)S(1)}, u32[]{:S(2)}, u32[]{:S(2)}) collective-permute-start(f32[4,128,128]{2,1,0:T(8,128)S(1)} %left.1.after), channel_id=1, source_target_pairs={{0,28},{4,0},{8,4},{12,8},{16,12},{20,16},{24,20},{28,24},{32,60},... | collective-permute-start | bytes 786440 | tf_op jit(solution)/shard_map/ppermute | solution.py:451
  8.8 2.1 %collective-permute-start.3 = (f32[4,64,256]{2,1,0:T(8,128)S(1)}, f32[4,64,256]{2,1,0:T(8,128)S(1)}, u32[]{:S(2)}, u32[]{:S(2)}) collective-permute-start(f32[4,64,256]{2,1,0:T(8,128)S(1)} %get-tuple-element.23), channel_id=1, source_target_pairs={{0,224},{4,228},{8,232},{12,236},{16,240},{20,244},{24,248},{28,25... | collective-permute-start | bytes 786440 | tf_op jit(solution)/shard_map/ppermute | solution.py:451
  11.0 1.5 %collective-permute-start.4 = (f32[4,32,128]{2,1,0:T(8,128)S(1)}, f32[4,32,128]{2,1,0:T(8,128)S(1)}, u32[]{:S(2)}, u32[]{:S(2)}) collective-permute-start(f32[4,32,128]{2,1,0:T(8,128)S(1)} %get-tuple-element.24), channel_id=1, source_target_pairs={{0,252},{4,224},{8,228},{12,232},{16,236},{20,240},{24,244},{28,24... | collective-permute-start | bytes 196616 | tf_op jit(solution)/shard_map/ppermute | solution.py:451
  12.5 1.1 %collective-permute-start.5 = (f32[4,32,128]{2,1,0:T(8,128)S(1)}, f32[4,32,128]{2,1,0:T(8,128)S(1)}, u32[]{:S(2)}, u32[]{:S(2)}) collective-permute-start(f32[4,32,128]{2,1,0:T(8,128)S(1)} %get-tuple-element.25), channel_id=1, source_target_pairs={{0,228},{4,232},{8,236},{12,240},{16,244},{20,248},{24,252},{28,22... | collective-permute-start | bytes 196616 | tf_op jit(solution)/shard_map/ppermute | solution.py:451
  14.0 0.4 phase.2
  15.1 2.1 %collective-permute-start.2 = (f32[4,64,256]{2,1,0:T(8,128)S(1)}, f32[4,64,256]{2,1,0:T(8,128)S(1)}, u32[]{:S(2)}, u32[]{:S(2)}) collective-permute-start(f32[4,64,256]{2,1,0:T(8,128)S(1)} %get-tuple-element.22), channel_id=1, source_target_pairs={{0,32},{4,36},{8,40},{12,44},{16,48},{20,52},{24,56},{28,60},{32,0... | collective-permute-start | bytes 786440 | tf_op jit(solution)/shard_map/ppermute | solution.py:451
  17.6 0.7 collective-permute-done.5.left.far_left
  18.4 0.5 collective-permute-done.6.corners
  18.9 6.9 %slots.1 = (f32[264,128]{1,0:T(8,128)S(1)}, f32[264,128]{1,0:T(8,128)S(1)}, f32[264,128]{1,0:T(8,128)S(1)}, f32[264,128]{1,0:T(8,128)S(1)}, f32[520,128]{1,0:T(8,128)S(1)}, /*index=5*/f32[520,128]{1,0:T(8,128)S(1)}) custom-call(s32[4]{0:T(128)S(1)} %reshape.62.starts, s32[1,1,1]{2,1,0:T(1,128)S(6)} %copy.15.live_counts, f32[4,256,256]{2,1,0:T(8,128)S(1)} %bitcast.12, ...), custom_call_target="tpu_custom_call" | custom-call | tf_op jit(solution)/shard_map/slots/pallas_call | solution.py:28
  25.8 2.5 %collective-permute-start.12 = (f32[520,128]{1,0:T(8,128)S(1)}, f32[520,128]{1,0:T(8,128)S(1)}, u32[]{:S(2)}, u32[]{:S(2)}) collective-permute-start(f32[520,128]{1,0:T(8,128)S(1)} %get-tuple-element.36), channel_id=1, source_target_pairs={{0,32},{4,36},{8,40},{12,44},{16,48},{20,52},{24,56},{28,60},{32,0... | collective-permute-start | bytes 798728 | tf_op jit(solution)/shard_map/ppermute | solution.py:451
  28.3 1.3 %collective-permute-start.7 = (f32[264,128]{1,0:T(8,128)S(1)}, f32[264,128]{1,0:T(8,128)S(1)}, u32[]{:S(2)}, u32[]{:S(2)}) collective-permute-start(f32[264,128]{1,0:T(8,128)S(1)} %get-tuple-element.29), channel_id=1, source_target_pairs={{0,1},{1,2},{2,3},{3,0},{4,5},{5,6},{6,7},{7,4},{8,9},{9,10},{10,1... | collective-permute-start | bytes 405512 | tf_op jit(solution)/shard_map/ppermute | solution.py:464
  29.6 2.6 %collective-permute-start.8 = (f32[264,128]{1,0:T(8,128)S(1)}, f32[264,128]{1,0:T(8,128)S(1)}, u32[]{:S(2)}, u32[]{:S(2)}) collective-permute-start(f32[264,128]{1,0:T(8,128)S(1)} %get-tuple-element.30), channel_id=1, source_target_pairs={{0,2},{1,3},{2,0},{3,1},{4,6},{5,7},{6,4},{7,5},{8,10},{9,11},{10,... | collective-permute-start | bytes 405512 | tf_op jit(solution)/shard_map/ppermute | solution.py:464
  32.3 1.1 %collective-permute-start.9 = (f32[264,128]{1,0:T(8,128)S(1)}, f32[264,128]{1,0:T(8,128)S(1)}, u32[]{:S(2)}, u32[]{:S(2)}) collective-permute-start(f32[264,128]{1,0:T(8,128)S(1)} %get-tuple-element.31), channel_id=1, source_target_pairs={{0,3},{1,0},{2,1},{3,2},{4,7},{5,4},{6,5},{7,6},{8,11},{9,8},{10,9... | collective-permute-start | bytes 405512 | tf_op jit(solution)/shard_map/ppermute | solution.py:464
  33.3 0.8 %spread.1 = f32[16,40,128]{2,1,0:T(8,128)} custom-call(f32[520,128]{1,0:T(8,128)S(1)} %get-tuple-element.35.keep, f32[520,128]{1,0:T(8,128)S(1)} %collective-permute-done.12.got), custom_call_target="tpu_custom_call" | custom-call | flops 10000000000 | tf_op jit(solution)/shard_map/spread/pallas_call | solution.py:28
  34.1 3.5 %all-to-all-start = ((f32[16,40,128]{2,1,0:T(8,128)}), f32[16,40,128]{2,1,0:T(8,128)S(1)}, u32[]{:S(2)}, u32[]{:S(2)}) async-start(f32[16,40,128]{2,1,0:T(8,128)} %spread.1), calls=%async_computation | async-start | bytes 655360 | tf_op jit(solution)/shard_map/all_to_all | solution.py:532
  37.6 0.9 %collective-permute-done.8.three = f32[264,128]{1,0:T(8,128)S(1)} collective-permute-done((f32[264,128]{1,0:T(8,128)S(1)}, f32[264,128]{1,0:T(8,128)S(1)}, u32[]{:S(2)}, u32[]{:S(2)}) %collective-permute-start.8) | collective-permute-done | bytes 135200 | tf_op jit(solution)/shard_map/ppermute | solution.py:464
  38.6 0.5 place.1
  39.2 2.7 %collective-permute-start.11 = (f32[192,128]{1,0:T(8,128)S(1)}, f32[192,128]{1,0:T(8,128)S(1)}, u32[]{:S(2)}, u32[]{:S(2)}) collective-permute-start(f32[192,128]{1,0:T(8,128)S(1)} %get-tuple-element.33.after), channel_id=1, source_target_pairs={{0,28},{4,0},{8,4},{12,8},{16,12},{20,16},{24,20},{28,24},{32,60},... | collective-permute-start | bytes 294920 | tf_op jit(solution)/shard_map/ppermute | solution.py:451
  41.8 3.5 %all-to-all-done.chunks = f32[16,40,128]{2,1,0:T(8,128)S(1)} async-done(((f32[16,40,128]{2,1,0:T(8,128)}), f32[16,40,128]{2,1,0:T(8,128)S(1)}, u32[]{:S(2)}, u32[]{:S(2)}) %all-to-all-start) | async-done | bytes 327712 | tf_op jit(solution)/shard_map/all_to_all | solution.py:532
  45.6 2.4 %collective-permute-start.13 = (f32[2,64,128]{2,1,0:T(8,128)S(1)}, f32[2,64,128]{2,1,0:T(8,128)S(1)}, u32[]{:S(2)}, u32[]{:S(2)}) collective-permute-start(f32[2,64,128]{2,1,0:T(8,128)S(1)} %get-tuple-element.37.after), channel_id=1, source_target_pairs={{0,32},{4,36},{8,40},{12,44},{16,48},{20,52},{24,56},{28,60},{32,0... | collective-permute-start | bytes 196616 | tf_op jit(solution)/shard_map/ppermute | solution.py:451
  48.1 3.0 %collective-permute-start.19 = (f32[40,128]{1,0:T(8,128)S(1)}, f32[40,128]{1,0:T(8,128)S(1)}, u32[]{:S(2)}, u32[]{:S(2)}) collective-permute-start(f32[40,128]{1,0:T(8,128)S(1)} %pair.2.after.own), channel_id=1, source_target_pairs={{0,8},{4,12},{8,0},{12,4},{16,24},{20,28},{24,16},{28,20},{1,9},{5... | collective-permute-start | bytes 61448 | tf_op jit(solution)/shard_map/ppermute | solution.py:467
  51.1 1.0 %collective-permute-done.14.from_far = f32[2,64,128]{2,1,0:T(8,128)S(1)} collective-permute-done((f32[2,64,128]{2,1,0:T(8,128)S(1)}, f32[2,64,128]{2,1,0:T(8,128)S(1)}, u32[]{:S(2)}, u32[]{:S(2)}) %collective-permute-start.14) | collective-permute-done | bytes 65568 | tf_op jit(solution)/shard_map/ppermute | solution.py:451
  52.1 0.4 collective-permute-done.19.got
  52.6 1.2 %collective-permute-start.20 = (f32[40,128]{1,0:T(8,128)S(1)}, f32[40,128]{1,0:T(8,128)S(1)}, u32[]{:S(2)}, u32[]{:S(2)}) collective-permute-start(f32[40,128]{1,0:T(8,128)S(1)} %pair.3.own), channel_id=1, source_target_pairs={{0,28},{4,24},{8,20},{12,16},{16,12},{20,8},{24,4},{28,0},{1,29},{... | collective-permute-start | bytes 61448 | tf_op jit(solution)/shard_map/ppermute | solution.py:467
  53.8 2.4 %collective-permute-start.16 = (f32[256,256]{1,0:T(8,128)S(1)}, f32[256,256]{1,0:T(8,128)S(1)}, u32[]{:S(2)}, u32[]{:S(2)}) collective-permute-start(f32[256,256]{1,0:T(8,128)S(1)} %finish.1.after.one), channel_id=1, source_target_pairs={{0,2},{1,3},{2,0},{3,1},{4,6},{5,7},{6,4},{7,5},{8,10},{9,11},{10,... | collective-permute-start | bytes 786440 | tf_op jit(solution)/shard_map/ppermute | solution.py:464
  56.5 2.4 %collective-permute-start.18 = (f32[256,256]{1,0:T(8,128)S(1)}, f32[256,256]{1,0:T(8,128)S(1)}, u32[]{:S(2)}, u32[]{:S(2)}) collective-permute-start(f32[256,256]{1,0:T(8,128)S(1)} %finish.1.after.one), channel_id=1, source_target_pairs={{0,3},{1,0},{2,1},{3,2},{4,7},{5,4},{6,5},{7,6},{8,11},{9,8},{10,9... | collective-permute-start | bytes 786440 | tf_op jit(solution)/shard_map/ppermute | solution.py:464
  58.9 11.7 %all_to_all.10 = f32[16,32,128]{2,1,0:T(8,128)S(1)} all-to-all(f32[16,32,128]{2,1,0:T(8,128)S(1)} %mean.1), channel_id=1, replica_groups=mesh['x'=4,'core'=2,'tx'=8,'scan'=4] {'x','scan'}, dimensions={0} | all-to-all | bytes 524288 | tf_op jit(solution)/shard_map/all_to_all | solution.py:582
  70.6 3.3 %collective-permute-start.21 = (f32[512,128]{1,0:T(8,128)S(1)}, f32[512,128]{1,0:T(8,128)S(1)}, u32[]{:S(2)}, u32[]{:S(2)}) collective-permute-start(f32[512,128]{1,0:T(8,128)S(1)} %bitcast.14), channel_id=1, source_target_pairs={{0,32},{4,36},{8,40},{12,44},{16,48},{20,52},{24,56},{28,60},{32,0... | collective-permute-start | bytes 786440 | tf_op jit(solution)/shard_map/ppermute | solution.py:451
  74.0 1.1 %gather.1 = (f32[4,256,256]{2,1,0:T(8,128)}, f32[2,512,128]{2,1,0:T(8,128)}) custom-call(f32[256,256]{1,0:T(8,128)S(1)} %finish.1.after.one, f32[256,256]{1,0:T(8,128)S(1)} %collective-permute-done.16.two, f32[256,256]{1,0:T(8,128)S(1)} %collective-permute-done.17.three, f32[256,256]{1,0:T(8,128)S(1)} %collective-permute-done.18.four, f32[512,128]{1,0:T(8,128)S(1)} %bitcast.15), custom_call_target="tpu_custom_call" | custom-call | flops 10000000000 | tf_op jit(solution)/shard_map/gather/pallas_call | solution.py:396
  75.1 0.7 other.1
  (57 shorter events, 1.9 us)
Async XLA Ops:
  2.0 15.2 %collective-permute-start.1 = (f32[4,128,128]{2,1,0:T(8,128)S(1)}, f32[4,128,128]{2,1,0:T(8,128)S(1)}, u32[]{:S(2)}, u32[]{:S(2)}) collective-permute-start(f32[4,128,128]{2,1,0:T(8,128)S(1)} %right.1.after), channel_id=1, source_target_pairs={{0,4},{4,8},{8,12},{12,16},{16,20},{20,24},{24,28},{28,0},{32,36},... | collective-permute-start | bytes 786440 | tf_op jit(solution)/shard_map/ppermute | solution.py:451
  4.7 10.4 %collective-permute-start = (f32[4,128,128]{2,1,0:T(8,128)S(1)}, f32[4,128,128]{2,1,0:T(8,128)S(1)}, u32[]{:S(2)}, u32[]{:S(2)}) collective-permute-start(f32[4,128,128]{2,1,0:T(8,128)S(1)} %left.1.after), channel_id=1, source_target_pairs={{0,28},{4,0},{8,4},{12,8},{16,12},{20,16},{24,20},{28,24},{32,60},... | collective-permute-start | bytes 786440 | tf_op jit(solution)/shard_map/ppermute | solution.py:451
  8.7 5.3 %copy-start.8 = (f32[128,128]{1,0:T(8,128)S(1)}, f32[128,128]{1,0:T(8,128)}, u32[]{:S(2)}) copy-start(f32[128,128]{1,0:T(8,128)} %phase.3) | copy-start | bytes 196612
  8.8 9.5 %collective-permute-start.3 = (f32[4,64,256]{2,1,0:T(8,128)S(1)}, f32[4,64,256]{2,1,0:T(8,128)S(1)}, u32[]{:S(2)}, u32[]{:S(2)}) collective-permute-start(f32[4,64,256]{2,1,0:T(8,128)S(1)} %get-tuple-element.23), channel_id=1, source_target_pairs={{0,224},{4,228},{8,232},{12,236},{16,240},{20,244},{24,248},{28,25... | collective-permute-start | bytes 786440 | tf_op jit(solution)/shard_map/ppermute | solution.py:451
  11.0 2.6 %copy-start.9 = (s32[1,1,2,2]{3,2,1,0:T(2,128)S(1)}, s32[1,1,2,2]{3,2,1,0:T(2,128)}, u32[]{:S(2)}) copy-start(s32[1,1,2,2]{3,2,1,0:T(2,128)} %param.13) | copy-start | bytes 52
  11.0 6.6 %collective-permute-start.4 = (f32[4,32,128]{2,1,0:T(8,128)S(1)}, f32[4,32,128]{2,1,0:T(8,128)S(1)}, u32[]{:S(2)}, u32[]{:S(2)}) collective-permute-start(f32[4,32,128]{2,1,0:T(8,128)S(1)} %get-tuple-element.24), channel_id=1, source_target_pairs={{0,252},{4,224},{8,228},{12,232},{16,236},{20,240},{24,244},{28,24... | collective-permute-start | bytes 196616 | tf_op jit(solution)/shard_map/ppermute | solution.py:451
  12.5 5.8 %collective-permute-start.5 = (f32[4,32,128]{2,1,0:T(8,128)S(1)}, f32[4,32,128]{2,1,0:T(8,128)S(1)}, u32[]{:S(2)}, u32[]{:S(2)}) collective-permute-start(f32[4,32,128]{2,1,0:T(8,128)S(1)} %get-tuple-element.25), channel_id=1, source_target_pairs={{0,228},{4,232},{8,236},{12,240},{16,244},{20,248},{24,252},{28,22... | collective-permute-start | bytes 196616 | tf_op jit(solution)/shard_map/ppermute | solution.py:451
  15.1 3.3 %collective-permute-start.2 = (f32[4,64,256]{2,1,0:T(8,128)S(1)}, f32[4,64,256]{2,1,0:T(8,128)S(1)}, u32[]{:S(2)}, u32[]{:S(2)}) collective-permute-start(f32[4,64,256]{2,1,0:T(8,128)S(1)} %get-tuple-element.22), channel_id=1, source_target_pairs={{0,32},{4,36},{8,40},{12,44},{16,48},{20,52},{24,56},{28,60},{32,0... | collective-permute-start | bytes 786440 | tf_op jit(solution)/shard_map/ppermute | solution.py:451
  17.4 1.5 %copy-start.1 = (f32[2,2,256,256]{3,2,1,0:T(8,128)S(1)}, f32[2,2,256,256]{3,2,1,0:T(8,128)}, u32[]{:S(2)}) copy-start(f32[2,2,256,256]{3,2,1,0:T(8,128)} %param.10) | copy-start | bytes 3145732
  17.4 1.5 %copy-start.2 = (f32[4,2,128,128]{3,2,1,0:T(8,128)S(1)}, f32[4,2,128,128]{3,2,1,0:T(8,128)}, u32[]{:S(2)}) copy-start(f32[4,2,128,128]{3,2,1,0:T(8,128)} %param.11) | copy-start | bytes 1572868
  17.4 1.5 %copy-start.3 = (f32[1,1,2,128,128]{4,3,2,1,0:T(8,128)S(1)}, f32[1,1,2,128,128]{4,3,2,1,0:T(8,128)}, u32[]{:S(2)}) copy-start(f32[1,1,2,128,128]{4,3,2,1,0:T(8,128)} %param.15) | copy-start | bytes 393220
  17.4 1.5 %copy-start.4 = (bf16[256,256]{1,0:T(8,128)(2,1)S(1)}, bf16[256,256]{1,0:T(8,128)(2,1)}, u32[]{:S(2)}) copy-start(bf16[256,256]{1,0:T(8,128)(2,1)} %constant.22.clone.right_low) | copy-start | bytes 393220
  17.4 1.5 %copy-start.5 = (bf16[256,256]{1,0:T(8,128)(2,1)S(1)}, bf16[256,256]{1,0:T(8,128)(2,1)}, u32[]{:S(2)}) copy-start(bf16[256,256]{1,0:T(8,128)(2,1)} %constant.23.clone.left_high) | copy-start | bytes 393220
  17.4 1.5 %copy-start.6 = (bf16[256,256]{1,0:T(8,128)(2,1)S(1)}, bf16[256,256]{1,0:T(8,128)(2,1)}, u32[]{:S(2)}) copy-start(bf16[256,256]{1,0:T(8,128)(2,1)} %constant.24.clone.left_low) | copy-start | bytes 393220
  17.4 1.5 %copy-start.7 = (bf16[256,256]{1,0:T(8,128)(2,1)S(1)}, bf16[256,256]{1,0:T(8,128)(2,1)}, u32[]{:S(2)}) copy-start(bf16[256,256]{1,0:T(8,128)(2,1)} %constant.9.clone.right_high) | copy-start | bytes 393220
  17.5 1.4 %collective-permute-start.6 = (f32[4,64,128]{2,1,0:T(8,128)S(1)}, f32[4,64,128]{2,1,0:T(8,128)S(1)}, u32[]{:S(2)}, u32[]{:S(2)}) collective-permute-start(f32[4,64,128]{2,1,0:T(8,128)S(1)} %corners.1), channel_id=1, source_target_pairs={{0,32},{4,36},{8,40},{12,44},{16,48},{20,52},{24,56},{28,60},{32,0... | collective-permute-start | bytes 393224 | tf_op jit(solution)/shard_map/ppermute | solution.py:451
  25.8 7.5 %collective-permute-start.12 = (f32[520,128]{1,0:T(8,128)S(1)}, f32[520,128]{1,0:T(8,128)S(1)}, u32[]{:S(2)}, u32[]{:S(2)}) collective-permute-start(f32[520,128]{1,0:T(8,128)S(1)} %get-tuple-element.36), channel_id=1, source_target_pairs={{0,32},{4,36},{8,40},{12,44},{16,48},{20,52},{24,56},{28,60},{32,0... | collective-permute-start | bytes 798728 | tf_op jit(solution)/shard_map/ppermute | solution.py:451
  28.3 9.3 %collective-permute-start.7 = (f32[264,128]{1,0:T(8,128)S(1)}, f32[264,128]{1,0:T(8,128)S(1)}, u32[]{:S(2)}, u32[]{:S(2)}) collective-permute-start(f32[264,128]{1,0:T(8,128)S(1)} %get-tuple-element.29), channel_id=1, source_target_pairs={{0,1},{1,2},{2,3},{3,0},{4,5},{5,6},{6,7},{7,4},{8,9},{9,10},{10,1... | collective-permute-start | bytes 405512 | tf_op jit(solution)/shard_map/ppermute | solution.py:464
  29.6 9.0 %collective-permute-start.8 = (f32[264,128]{1,0:T(8,128)S(1)}, f32[264,128]{1,0:T(8,128)S(1)}, u32[]{:S(2)}, u32[]{:S(2)}) collective-permute-start(f32[264,128]{1,0:T(8,128)S(1)} %get-tuple-element.30), channel_id=1, source_target_pairs={{0,2},{1,3},{2,0},{3,1},{4,6},{5,7},{6,4},{7,5},{8,10},{9,11},{10,... | collective-permute-start | bytes 405512 | tf_op jit(solution)/shard_map/ppermute | solution.py:464
  32.3 6.3 %collective-permute-start.9 = (f32[264,128]{1,0:T(8,128)S(1)}, f32[264,128]{1,0:T(8,128)S(1)}, u32[]{:S(2)}, u32[]{:S(2)}) collective-permute-start(f32[264,128]{1,0:T(8,128)S(1)} %get-tuple-element.31), channel_id=1, source_target_pairs={{0,3},{1,0},{2,1},{3,2},{4,7},{5,4},{6,5},{7,6},{8,11},{9,8},{10,9... | collective-permute-start | bytes 405512 | tf_op jit(solution)/shard_map/ppermute | solution.py:464
  34.1 11.3 %all-to-all-start = ((f32[16,40,128]{2,1,0:T(8,128)}), f32[16,40,128]{2,1,0:T(8,128)S(1)}, u32[]{:S(2)}, u32[]{:S(2)}) async-start(f32[16,40,128]{2,1,0:T(8,128)} %spread.1), calls=%async_computation | async-start | bytes 655360 | tf_op jit(solution)/shard_map/all_to_all | solution.py:532
  39.1 6.4 %collective-permute-start.10 = (f32[192,128]{1,0:T(8,128)S(1)}, f32[192,128]{1,0:T(8,128)S(1)}, u32[]{:S(2)}, u32[]{:S(2)}) collective-permute-start(f32[192,128]{1,0:T(8,128)S(1)} %get-tuple-element.32), channel_id=1, source_target_pairs={{0,4},{4,8},{8,12},{12,16},{16,20},{20,24},{24,28},{28,0},{32,36},... | collective-permute-start | bytes 294920 | tf_op jit(solution)/shard_map/ppermute | solution.py:451
  39.2 6.3 %collective-permute-start.11 = (f32[192,128]{1,0:T(8,128)S(1)}, f32[192,128]{1,0:T(8,128)S(1)}, u32[]{:S(2)}, u32[]{:S(2)}) collective-permute-start(f32[192,128]{1,0:T(8,128)S(1)} %get-tuple-element.33.after), channel_id=1, source_target_pairs={{0,28},{4,0},{8,4},{12,8},{16,12},{20,16},{24,20},{28,24},{32,60},... | collective-permute-start | bytes 294920 | tf_op jit(solution)/shard_map/ppermute | solution.py:451
  45.4 2.7 %collective-permute-start.15 = (f32[40,128]{1,0:T(8,128)S(1)}, f32[40,128]{1,0:T(8,128)S(1)}, u32[]{:S(2)}, u32[]{:S(2)}) collective-permute-start(f32[40,128]{1,0:T(8,128)S(1)} %sum.1.after.own), channel_id=1, source_target_pairs={{0,4},{4,0},{8,12},{12,8},{16,20},{20,16},{24,28},{28,24},{1,5},{5... | collective-permute-start | bytes 61448 | tf_op jit(solution)/shard_map/ppermute | solution.py:467
  45.6 5.4 %collective-permute-start.13 = (f32[2,64,128]{2,1,0:T(8,128)S(1)}, f32[2,64,128]{2,1,0:T(8,128)S(1)}, u32[]{:S(2)}, u32[]{:S(2)}) collective-permute-start(f32[2,64,128]{2,1,0:T(8,128)S(1)} %get-tuple-element.37.after), channel_id=1, source_target_pairs={{0,32},{4,36},{8,40},{12,44},{16,48},{20,52},{24,56},{28,60},{32,0... | collective-permute-start | bytes 196616 | tf_op jit(solution)/shard_map/ppermute | solution.py:451
  48.1 4.0 %collective-permute-start.14 = (f32[2,64,128]{2,1,0:T(8,128)S(1)}, f32[2,64,128]{2,1,0:T(8,128)S(1)}, u32[]{:S(2)}, u32[]{:S(2)}) collective-permute-start(f32[2,64,128]{2,1,0:T(8,128)S(1)} %get-tuple-element.38), channel_id=1, source_target_pairs={{0,224},{4,228},{8,232},{12,236},{16,240},{20,244},{24,248},{28,25... | collective-permute-start | bytes 196616 | tf_op jit(solution)/shard_map/ppermute | solution.py:451
  48.1 4.4 %collective-permute-start.19 = (f32[40,128]{1,0:T(8,128)S(1)}, f32[40,128]{1,0:T(8,128)S(1)}, u32[]{:S(2)}, u32[]{:S(2)}) collective-permute-start(f32[40,128]{1,0:T(8,128)S(1)} %pair.2.after.own), channel_id=1, source_target_pairs={{0,8},{4,12},{8,0},{12,4},{16,24},{20,28},{24,16},{28,20},{1,9},{5... | collective-permute-start | bytes 61448 | tf_op jit(solution)/shard_map/ppermute | solution.py:467
  52.6 6.3 %collective-permute-start.20 = (f32[40,128]{1,0:T(8,128)S(1)}, f32[40,128]{1,0:T(8,128)S(1)}, u32[]{:S(2)}, u32[]{:S(2)}) collective-permute-start(f32[40,128]{1,0:T(8,128)S(1)} %pair.3.own), channel_id=1, source_target_pairs={{0,28},{4,24},{8,20},{12,16},{16,12},{20,8},{24,4},{28,0},{1,29},{... | collective-permute-start | bytes 61448 | tf_op jit(solution)/shard_map/ppermute | solution.py:467
  53.8 20.1 %collective-permute-start.16 = (f32[256,256]{1,0:T(8,128)S(1)}, f32[256,256]{1,0:T(8,128)S(1)}, u32[]{:S(2)}, u32[]{:S(2)}) collective-permute-start(f32[256,256]{1,0:T(8,128)S(1)} %finish.1.after.one), channel_id=1, source_target_pairs={{0,2},{1,3},{2,0},{3,1},{4,6},{5,7},{6,4},{7,5},{8,10},{9,11},{10,... | collective-permute-start | bytes 786440 | tf_op jit(solution)/shard_map/ppermute | solution.py:464
  56.2 17.7 %collective-permute-start.17 = (f32[256,256]{1,0:T(8,128)S(1)}, f32[256,256]{1,0:T(8,128)S(1)}, u32[]{:S(2)}, u32[]{:S(2)}) collective-permute-start(f32[256,256]{1,0:T(8,128)S(1)} %finish.1.after.one), channel_id=1, source_target_pairs={{0,1},{1,2},{2,3},{3,0},{4,5},{5,6},{6,7},{7,4},{8,9},{9,10},{10,1... | collective-permute-start | bytes 786440 | tf_op jit(solution)/shard_map/ppermute | solution.py:464
  56.5 17.5 %collective-permute-start.18 = (f32[256,256]{1,0:T(8,128)S(1)}, f32[256,256]{1,0:T(8,128)S(1)}, u32[]{:S(2)}, u32[]{:S(2)}) collective-permute-start(f32[256,256]{1,0:T(8,128)S(1)} %finish.1.after.one), channel_id=1, source_target_pairs={{0,3},{1,0},{2,1},{3,2},{4,7},{5,4},{6,5},{7,6},{8,11},{9,8},{10,9... | collective-permute-start | bytes 786440 | tf_op jit(solution)/shard_map/ppermute | solution.py:464
  70.6 4.5 %collective-permute-start.21 = (f32[512,128]{1,0:T(8,128)S(1)}, f32[512,128]{1,0:T(8,128)S(1)}, u32[]{:S(2)}, u32[]{:S(2)}) collective-permute-start(f32[512,128]{1,0:T(8,128)S(1)} %bitcast.14), channel_id=1, source_target_pairs={{0,32},{4,36},{8,40},{12,44},{16,48},{20,52},{24,56},{28,60},{32,0... | collective-permute-start | bytes 786440 | tf_op jit(solution)/shard_map/ppermute | solution.py:451
  (1 other events, 1.2 us)

commit v7 on v6

--- a/solution.py
+++ b/solution.py
@@ -543,7 +543,7 @@
         sum_body, [(rows + 8, W)], (chunks, left), [VMEM, ANY], name="sum", flops=LONG
     )
     left, right = to_left(left), to_right(right)
-    got = to_pair(share, 1)
+    got = to_pair(share, 2)
     near, far, held = call(
         rows_body,
         [(2, HALF, W)] * 2 + [(2, TILE, W)],
@@ -556,7 +556,7 @@
     (share,) = call(
         pair_body, [(rows + 8, W)], (share, got, near), [VMEM] * 2 + [ANY], name="pair", flops=LONG
     )
-    got = to_pair(share, 2)
+    got = to_pair(share, 1)
     near, far = to_core(near), to_far(far)
     (quarter,) = call(
         finish_body,

time: 76.3 us -> 75.8 us (level)
  starting transfers between devices: 42.5 us -> 41.2 us
  waiting for transfers between devices: 7.28 us -> 8.15 us
    ppermute x6, starting transfers between devices: 10.1 us -> 8.96 us  [to_scan(): lax.ppermute(value, 'scan', [(s, (s + step) % nsc) for s in range(nsc)])]
  transfers between devices with their start and end apart: 23 -> 23, of which waited for: 7 -> 8; matrix products, arithmetic and copies ran while one was open for 0% -> 0% of each run, Pallas kernels for 4% -> 4%
where the time goes in v7:
time: 75.8 us; the launch traced here: 75.5 us
  starting transfers between devices  41.2 us (54%)
  blocking collectives  11.7 us (15%)
  Pallas kernels  11.1 us (15%)
  waiting for transfers between devices  8.15 us (11%)
  between operations  1.71 us (2%)
  local copies, waits for them, and re-layouts  1.45 us (2%)
    ppermute x13, starting transfers between devices, over_grid(): return lambda value: lax.ppermute(value, ('x', 'core', 'tx'), pairs)  24.9 us
    all_to_all x1, blocking collectives, per_device(): mine = lax.all_to_all(spread, ('x', 'scan'), 0, 0).reshape(MODES * W, W)  11.7 us
    pallas_call x15, Pallas kernels, call(): pl.pallas_call(body, out_shape=[jax.ShapeDtypeStruct(shape, F32) for shap...  9.29 us
    ppermute x6, starting transfers between devices, to_scan(): lax.ppermute(value, 'scan', [(s, (s + step) % nsc) for s in range(nsc)])  8.96 us
    ppermute x3, starting transfers between devices, to_pair(): return lax.ppermute(value, 'tx', [(t, t ^ mask) for t in range(ntx)])  3.79 us
    all_to_all x1, starting transfers between devices, per_device(): chunks = lax.all_to_all(chunks, ('x', 'scan'), 0, 0)  3.54 us
    all_to_all x1, waiting for transfers between devices, per_device(): chunks = lax.all_to_all(chunks, ('x', 'scan'), 0, 0)  3.53 us
    ppermute x13, waiting for transfers between devices, over_grid(): return lambda value: lax.ppermute(value, ('x', 'core', 'tx'), pairs)  2.59 us
  transfers between devices with their start and end apart: 23, of which 8 were waited for; matrix products, arithmetic and copies ran while one was open for 0% of the time, Pallas kernels for 4%

profile of v7, /device:TPU:1, one launch (start us, length us, event | category | flops | bytes accessed | tf_op | source)
XLA Modules:
  0.0 75.5 jit_solution(15108966782318760937)
XLA Ops:
  0.6 1.2 %copy-done = f32[2,2,256,256]{3,2,1,0:T(8,128)S(1)} copy-done((f32[2,2,256,256]{3,2,1,0:T(8,128)S(1)}, f32[2,2,256,256]{3,2,1,0:T(8,128)}, u32[]{:S(2)}) %copy-start) | copy-done | bytes 1048600
  2.0 2.5 %collective-permute-start.1 = (f32[4,128,128]{2,1,0:T(8,128)S(1)}, f32[4,128,128]{2,1,0:T(8,128)S(1)}, u32[]{:S(2)}, u32[]{:S(2)}) collective-permute-start(f32[4,128,128]{2,1,0:T(8,128)S(1)} %right.1.after), channel_id=1, source_target_pairs={{0,4},{4,8},{8,12},{12,16},{16,20},{20,24},{24,28},{28,0},{32,36},... | collective-permute-start | bytes 786440 | tf_op jit(solution)/shard_map/ppermute | solution.py:451
  4.7 4.0 %collective-permute-start = (f32[4,128,128]{2,1,0:T(8,128)S(1)}, f32[4,128,128]{2,1,0:T(8,128)S(1)}, u32[]{:S(2)}, u32[]{:S(2)}) collective-permute-start(f32[4,128,128]{2,1,0:T(8,128)S(1)} %left.1.after), channel_id=1, source_target_pairs={{0,28},{4,0},{8,4},{12,8},{16,12},{20,16},{24,20},{28,24},{32,60},... | collective-permute-start | bytes 786440 | tf_op jit(solution)/shard_map/ppermute | solution.py:451
  8.8 2.1 %collective-permute-start.3 = (f32[4,64,256]{2,1,0:T(8,128)S(1)}, f32[4,64,256]{2,1,0:T(8,128)S(1)}, u32[]{:S(2)}, u32[]{:S(2)}) collective-permute-start(f32[4,64,256]{2,1,0:T(8,128)S(1)} %get-tuple-element.23), channel_id=1, source_target_pairs={{0,224},{4,228},{8,232},{12,236},{16,240},{20,244},{24,248},{28,25... | collective-permute-start | bytes 786440 | tf_op jit(solution)/shard_map/ppermute | solution.py:451
  11.0 1.5 %collective-permute-start.4 = (f32[4,32,128]{2,1,0:T(8,128)S(1)}, f32[4,32,128]{2,1,0:T(8,128)S(1)}, u32[]{:S(2)}, u32[]{:S(2)}) collective-permute-start(f32[4,32,128]{2,1,0:T(8,128)S(1)} %get-tuple-element.24), channel_id=1, source_target_pairs={{0,252},{4,224},{8,228},{12,232},{16,236},{20,240},{24,244},{28,24... | collective-permute-start | bytes 196616 | tf_op jit(solution)/shard_map/ppermute | solution.py:451
  12.5 1.1 %collective-permute-start.5 = (f32[4,32,128]{2,1,0:T(8,128)S(1)}, f32[4,32,128]{2,1,0:T(8,128)S(1)}, u32[]{:S(2)}, u32[]{:S(2)}) collective-permute-start(f32[4,32,128]{2,1,0:T(8,128)S(1)} %get-tuple-element.25), channel_id=1, source_target_pairs={{0,228},{4,232},{8,236},{12,240},{16,244},{20,248},{24,252},{28,22... | collective-permute-start | bytes 196616 | tf_op jit(solution)/shard_map/ppermute | solution.py:451
  14.0 0.4 phase.2
  15.1 2.1 %collective-permute-start.2 = (f32[4,64,256]{2,1,0:T(8,128)S(1)}, f32[4,64,256]{2,1,0:T(8,128)S(1)}, u32[]{:S(2)}, u32[]{:S(2)}) collective-permute-start(f32[4,64,256]{2,1,0:T(8,128)S(1)} %get-tuple-element.22), channel_id=1, source_target_pairs={{0,32},{4,36},{8,40},{12,44},{16,48},{20,52},{24,56},{28,60},{32,0... | collective-permute-start | bytes 786440 | tf_op jit(solution)/shard_map/ppermute | solution.py:451
  17.6 0.7 collective-permute-done.5.left.far_left
  18.4 0.5 collective-permute-done.6.corners
  18.9 6.9 %slots.1 = (f32[264,128]{1,0:T(8,128)S(1)}, f32[264,128]{1,0:T(8,128)S(1)}, f32[264,128]{1,0:T(8,128)S(1)}, f32[264,128]{1,0:T(8,128)S(1)}, f32[520,128]{1,0:T(8,128)S(1)}, /*index=5*/f32[520,128]{1,0:T(8,128)S(1)}) custom-call(s32[4]{0:T(128)S(1)} %reshape.62.starts, s32[1,1,1]{2,1,0:T(1,128)S(6)} %copy.15.live_counts, f32[4,256,256]{2,1,0:T(8,128)S(1)} %bitcast.12, ...), custom_call_target="tpu_custom_call" | custom-call | tf_op jit(solution)/shard_map/slots/pallas_call | solution.py:28
  25.8 2.5 %collective-permute-start.12 = (f32[520,128]{1,0:T(8,128)S(1)}, f32[520,128]{1,0:T(8,128)S(1)}, u32[]{:S(2)}, u32[]{:S(2)}) collective-permute-start(f32[520,128]{1,0:T(8,128)S(1)} %get-tuple-element.36), channel_id=1, source_target_pairs={{0,32},{4,36},{8,40},{12,44},{16,48},{20,52},{24,56},{28,60},{32,0... | collective-permute-start | bytes 798728 | tf_op jit(solution)/shard_map/ppermute | solution.py:451
  28.3 1.3 %collective-permute-start.7 = (f32[264,128]{1,0:T(8,128)S(1)}, f32[264,128]{1,0:T(8,128)S(1)}, u32[]{:S(2)}, u32[]{:S(2)}) collective-permute-start(f32[264,128]{1,0:T(8,128)S(1)} %get-tuple-element.29), channel_id=1, source_target_pairs={{0,1},{1,2},{2,3},{3,0},{4,5},{5,6},{6,7},{7,4},{8,9},{9,10},{10,1... | collective-permute-start | bytes 405512 | tf_op jit(solution)/shard_map/ppermute | solution.py:464
  29.6 2.6 %collective-permute-start.8 = (f32[264,128]{1,0:T(8,128)S(1)}, f32[264,128]{1,0:T(8,128)S(1)}, u32[]{:S(2)}, u32[]{:S(2)}) collective-permute-start(f32[264,128]{1,0:T(8,128)S(1)} %get-tuple-element.30), channel_id=1, source_target_pairs={{0,2},{1,3},{2,0},{3,1},{4,6},{5,7},{6,4},{7,5},{8,10},{9,11},{10,... | collective-permute-start | bytes 405512 | tf_op jit(solution)/shard_map/ppermute | solution.py:464
  32.2 1.1 %collective-permute-start.9 = (f32[264,128]{1,0:T(8,128)S(1)}, f32[264,128]{1,0:T(8,128)S(1)}, u32[]{:S(2)}, u32[]{:S(2)}) collective-permute-start(f32[264,128]{1,0:T(8,128)S(1)} %get-tuple-element.31), channel_id=1, source_target_pairs={{0,3},{1,0},{2,1},{3,2},{4,7},{5,4},{6,5},{7,6},{8,11},{9,8},{10,9... | collective-permute-start | bytes 405512 | tf_op jit(solution)/shard_map/ppermute | solution.py:464
  33.3 0.8 %spread.1 = f32[16,40,128]{2,1,0:T(8,128)} custom-call(f32[520,128]{1,0:T(8,128)S(1)} %get-tuple-element.35.keep, f32[520,128]{1,0:T(8,128)S(1)} %collective-permute-done.12.got), custom_call_target="tpu_custom_call" | custom-call | flops 10000000000 | tf_op jit(solution)/shard_map/spread/pallas_call | solution.py:28
  34.1 3.5 %all-to-all-start = ((f32[16,40,128]{2,1,0:T(8,128)}), f32[16,40,128]{2,1,0:T(8,128)S(1)}, u32[]{:S(2)}, u32[]{:S(2)}) async-start(f32[16,40,128]{2,1,0:T(8,128)} %spread.1), calls=%async_computation | async-start | bytes 655360 | tf_op jit(solution)/shard_map/all_to_all | solution.py:532
  37.6 0.9 %collective-permute-done.8.three = f32[264,128]{1,0:T(8,128)S(1)} collective-permute-done((f32[264,128]{1,0:T(8,128)S(1)}, f32[264,128]{1,0:T(8,128)S(1)}, u32[]{:S(2)}, u32[]{:S(2)}) %collective-permute-start.8) | collective-permute-done | bytes 135200 | tf_op jit(solution)/shard_map/ppermute | solution.py:464
  38.6 0.5 place.1
  39.2 2.7 %collective-permute-start.11 = (f32[192,128]{1,0:T(8,128)S(1)}, f32[192,128]{1,0:T(8,128)S(1)}, u32[]{:S(2)}, u32[]{:S(2)}) collective-permute-start(f32[192,128]{1,0:T(8,128)S(1)} %get-tuple-element.33.after), channel_id=1, source_target_pairs={{0,28},{4,0},{8,4},{12,8},{16,12},{20,16},{24,20},{28,24},{32,60},... | collective-permute-start | bytes 294920 | tf_op jit(solution)/shard_map/ppermute | solution.py:451
  41.8 3.5 %all-to-all-done.chunks = f32[16,40,128]{2,1,0:T(8,128)S(1)} async-done(((f32[16,40,128]{2,1,0:T(8,128)}), f32[16,40,128]{2,1,0:T(8,128)S(1)}, u32[]{:S(2)}, u32[]{:S(2)}) %all-to-all-start) | async-done | bytes 327712 | tf_op jit(solution)/shard_map/all_to_all | solution.py:532
  45.6 2.7 %collective-permute-start.13 = (f32[2,64,128]{2,1,0:T(8,128)S(1)}, f32[2,64,128]{2,1,0:T(8,128)S(1)}, u32[]{:S(2)}, u32[]{:S(2)}) collective-permute-start(f32[2,64,128]{2,1,0:T(8,128)S(1)} %get-tuple-element.37.after), channel_id=1, source_target_pairs={{0,32},{4,36},{8,40},{12,44},{16,48},{20,52},{24,56},{28,60},{32,0... | collective-permute-start | bytes 196616 | tf_op jit(solution)/shard_map/ppermute | solution.py:451
  48.3 0.9 %collective-permute-done.15.got = f32[40,128]{1,0:T(8,128)S(1)} collective-permute-done((f32[40,128]{1,0:T(8,128)S(1)}, f32[40,128]{1,0:T(8,128)S(1)}, u32[]{:S(2)}, u32[]{:S(2)}) %collective-permute-start.15) | collective-permute-done | bytes 20512 | tf_op jit(solution)/shard_map/ppermute | solution.py:467
  49.2 1.9 %collective-permute-start.19 = (f32[40,128]{1,0:T(8,128)S(1)}, f32[40,128]{1,0:T(8,128)S(1)}, u32[]{:S(2)}, u32[]{:S(2)}) collective-permute-start(f32[40,128]{1,0:T(8,128)S(1)} %pair.2.after.own), channel_id=1, source_target_pairs={{0,4},{4,0},{8,12},{12,8},{16,20},{20,16},{24,28},{28,24},{1,5},{5... | collective-permute-start | bytes 61448 | tf_op jit(solution)/shard_map/ppermute | solution.py:467
  51.1 1.2 %collective-permute-done.14.from_far = f32[2,64,128]{2,1,0:T(8,128)S(1)} collective-permute-done((f32[2,64,128]{2,1,0:T(8,128)S(1)}, f32[2,64,128]{2,1,0:T(8,128)S(1)}, u32[]{:S(2)}, u32[]{:S(2)}) %collective-permute-start.14) | collective-permute-done | bytes 65568 | tf_op jit(solution)/shard_map/ppermute | solution.py:451
  52.6 1.8 %collective-permute-start.20 = (f32[40,128]{1,0:T(8,128)S(1)}, f32[40,128]{1,0:T(8,128)S(1)}, u32[]{:S(2)}, u32[]{:S(2)}) collective-permute-start(f32[40,128]{1,0:T(8,128)S(1)} %pair.3.own), channel_id=1, source_target_pairs={{0,28},{4,24},{8,20},{12,16},{16,12},{20,8},{24,4},{28,0},{1,29},{... | collective-permute-start | bytes 61448 | tf_op jit(solution)/shard_map/ppermute | solution.py:467
  54.4 1.3 %collective-permute-start.16 = (f32[256,256]{1,0:T(8,128)S(1)}, f32[256,256]{1,0:T(8,128)S(1)}, u32[]{:S(2)}, u32[]{:S(2)}) collective-permute-start(f32[256,256]{1,0:T(8,128)S(1)} %finish.1.after.one), channel_id=1, source_target_pairs={{0,2},{1,3},{2,0},{3,1},{4,6},{5,7},{6,4},{7,5},{8,10},{9,11},{10,... | collective-permute-start | bytes 786440 | tf_op jit(solution)/shard_map/ppermute | solution.py:464
  55.9 2.5 %collective-permute-start.18 = (f32[256,256]{1,0:T(8,128)S(1)}, f32[256,256]{1,0:T(8,128)S(1)}, u32[]{:S(2)}, u32[]{:S(2)}) collective-permute-start(f32[256,256]{1,0:T(8,128)S(1)} %finish.1.after.one), channel_id=1, source_target_pairs={{0,3},{1,0},{2,1},{3,2},{4,7},{5,4},{6,5},{7,6},{8,11},{9,8},{10,9... | collective-permute-start | bytes 786440 | tf_op jit(solution)/shard_map/ppermute | solution.py:464
  58.4 11.7 %all_to_all.10 = f32[16,32,128]{2,1,0:T(8,128)S(1)} all-to-all(f32[16,32,128]{2,1,0:T(8,128)S(1)} %mean.1), channel_id=1, replica_groups=mesh['x'=4,'core'=2,'tx'=8,'scan'=4] {'x','scan'}, dimensions={0} | all-to-all | bytes 524288 | tf_op jit(solution)/shard_map/all_to_all | solution.py:582
  70.1 3.3 %collective-permute-start.21 = (f32[512,128]{1,0:T(8,128)S(1)}, f32[512,128]{1,0:T(8,128)S(1)}, u32[]{:S(2)}, u32[]{:S(2)}) collective-permute-start(f32[512,128]{1,0:T(8,128)S(1)} %bitcast.14), channel_id=1, source_target_pairs={{0,32},{4,36},{8,40},{12,44},{16,48},{20,52},{24,56},{28,60},{32,0... | collective-permute-start | bytes 786440 | tf_op jit(solution)/shard_map/ppermute | solution.py:451
  73.5 1.1 %gather.1 = (f32[4,256,256]{2,1,0:T(8,128)}, f32[2,512,128]{2,1,0:T(8,128)}) custom-call(f32[256,256]{1,0:T(8,128)S(1)} %finish.1.after.one, f32[256,256]{1,0:T(8,128)S(1)} %collective-permute-done.16.two, f32[256,256]{1,0:T(8,128)S(1)} %collective-permute-done.17.three, f32[256,256]{1,0:T(8,128)S(1)} %collective-permute-done.18.four, f32[512,128]{1,0:T(8,128)S(1)} %bitcast.15), custom_call_target="tpu_custom_call" | custom-call | flops 10000000000 | tf_op jit(solution)/shard_map/gather/pallas_call | solution.py:396
  74.6 0.7 other.1
  (57 shorter events, 2.0 us)
Async XLA Ops:
  2.0 15.2 %collective-permute-start.1 = (f32[4,128,128]{2,1,0:T(8,128)S(1)}, f32[4,128,128]{2,1,0:T(8,128)S(1)}, u32[]{:S(2)}, u32[]{:S(2)}) collective-permute-start(f32[4,128,128]{2,1,0:T(8,128)S(1)} %right.1.after), channel_id=1, source_target_pairs={{0,4},{4,8},{8,12},{12,16},{16,20},{20,24},{24,28},{28,0},{32,36},... | collective-permute-start | bytes 786440 | tf_op jit(solution)/shard_map/ppermute | solution.py:451
  4.7 10.4 %collective-permute-start = (f32[4,128,128]{2,1,0:T(8,128)S(1)}, f32[4,128,128]{2,1,0:T(8,128)S(1)}, u32[]{:S(2)}, u32[]{:S(2)}) collective-permute-start(f32[4,128,128]{2,1,0:T(8,128)S(1)} %left.1.after), channel_id=1, source_target_pairs={{0,28},{4,0},{8,4},{12,8},{16,12},{20,16},{24,20},{28,24},{32,60},... | collective-permute-start | bytes 786440 | tf_op jit(solution)/shard_map/ppermute | solution.py:451
  8.7 5.3 %copy-start.8 = (f32[128,128]{1,0:T(8,128)S(1)}, f32[128,128]{1,0:T(8,128)}, u32[]{:S(2)}) copy-start(f32[128,128]{1,0:T(8,128)} %phase.3) | copy-start | bytes 196612
  8.8 9.5 %collective-permute-start.3 = (f32[4,64,256]{2,1,0:T(8,128)S(1)}, f32[4,64,256]{2,1,0:T(8,128)S(1)}, u32[]{:S(2)}, u32[]{:S(2)}) collective-permute-start(f32[4,64,256]{2,1,0:T(8,128)S(1)} %get-tuple-element.23), channel_id=1, source_target_pairs={{0,224},{4,228},{8,232},{12,236},{16,240},{20,244},{24,248},{28,25... | collective-permute-start | bytes 786440 | tf_op jit(solution)/shard_map/ppermute | solution.py:451
  11.0 2.6 %copy-start.9 = (s32[1,1,2,2]{3,2,1,0:T(2,128)S(1)}, s32[1,1,2,2]{3,2,1,0:T(2,128)}, u32[]{:S(2)}) copy-start(s32[1,1,2,2]{3,2,1,0:T(2,128)} %param.13) | copy-start | bytes 52
  11.0 6.6 %collective-permute-start.4 = (f32[4,32,128]{2,1,0:T(8,128)S(1)}, f32[4,32,128]{2,1,0:T(8,128)S(1)}, u32[]{:S(2)}, u32[]{:S(2)}) collective-permute-start(f32[4,32,128]{2,1,0:T(8,128)S(1)} %get-tuple-element.24), channel_id=1, source_target_pairs={{0,252},{4,224},{8,228},{12,232},{16,236},{20,240},{24,244},{28,24... | collective-permute-start | bytes 196616 | tf_op jit(solution)/shard_map/ppermute | solution.py:451
  12.5 5.8 %collective-permute-start.5 = (f32[4,32,128]{2,1,0:T(8,128)S(1)}, f32[4,32,128]{2,1,0:T(8,128)S(1)}, u32[]{:S(2)}, u32[]{:S(2)}) collective-permute-start(f32[4,32,128]{2,1,0:T(8,128)S(1)} %get-tuple-element.25), channel_id=1, source_target_pairs={{0,228},{4,232},{8,236},{12,240},{16,244},{20,248},{24,252},{28,22... | collective-permute-start | bytes 196616 | tf_op jit(solution)/shard_map/ppermute | solution.py:451
  15.1 3.3 %collective-permute-start.2 = (f32[4,64,256]{2,1,0:T(8,128)S(1)}, f32[4,64,256]{2,1,0:T(8,128)S(1)}, u32[]{:S(2)}, u32[]{:S(2)}) collective-permute-start(f32[4,64,256]{2,1,0:T(8,128)S(1)} %get-tuple-element.22), channel_id=1, source_target_pairs={{0,32},{4,36},{8,40},{12,44},{16,48},{20,52},{24,56},{28,60},{32,0... | collective-permute-start | bytes 786440 | tf_op jit(solution)/shard_map/ppermute | solution.py:451
  17.4 1.5 %copy-start.1 = (f32[2,2,256,256]{3,2,1,0:T(8,128)S(1)}, f32[2,2,256,256]{3,2,1,0:T(8,128)}, u32[]{:S(2)}) copy-start(f32[2,2,256,256]{3,2,1,0:T(8,128)} %param.10) | copy-start | bytes 3145732
  17.4 1.5 %copy-start.2 = (f32[4,2,128,128]{3,2,1,0:T(8,128)S(1)}, f32[4,2,128,128]{3,2,1,0:T(8,128)}, u32[]{:S(2)}) copy-start(f32[4,2,128,128]{3,2,1,0:T(8,128)} %param.11) | copy-start | bytes 1572868
  17.4 1.5 %copy-start.3 = (f32[1,1,2,128,128]{4,3,2,1,0:T(8,128)S(1)}, f32[1,1,2,128,128]{4,3,2,1,0:T(8,128)}, u32[]{:S(2)}) copy-start(f32[1,1,2,128,128]{4,3,2,1,0:T(8,128)} %param.15) | copy-start | bytes 393220
  17.4 1.5 %copy-start.4 = (bf16[256,256]{1,0:T(8,128)(2,1)S(1)}, bf16[256,256]{1,0:T(8,128)(2,1)}, u32[]{:S(2)}) copy-start(bf16[256,256]{1,0:T(8,128)(2,1)} %constant.22.clone.right_low) | copy-start | bytes 393220
  17.4 1.5 %copy-start.5 = (bf16[256,256]{1,0:T(8,128)(2,1)S(1)}, bf16[256,256]{1,0:T(8,128)(2,1)}, u32[]{:S(2)}) copy-start(bf16[256,256]{1,0:T(8,128)(2,1)} %constant.23.clone.left_high) | copy-start | bytes 393220
  17.4 1.5 %copy-start.6 = (bf16[256,256]{1,0:T(8,128)(2,1)S(1)}, bf16[256,256]{1,0:T(8,128)(2,1)}, u32[]{:S(2)}) copy-start(bf16[256,256]{1,0:T(8,128)(2,1)} %constant.24.clone.left_low) | copy-start | bytes 393220
  17.4 1.5 %copy-start.7 = (bf16[256,256]{1,0:T(8,128)(2,1)S(1)}, bf16[256,256]{1,0:T(8,128)(2,1)}, u32[]{:S(2)}) copy-start(bf16[256,256]{1,0:T(8,128)(2,1)} %constant.9.clone.right_high) | copy-start | bytes 393220
  17.5 1.4 %collective-permute-start.6 = (f32[4,64,128]{2,1,0:T(8,128)S(1)}, f32[4,64,128]{2,1,0:T(8,128)S(1)}, u32[]{:S(2)}, u32[]{:S(2)}) collective-permute-start(f32[4,64,128]{2,1,0:T(8,128)S(1)} %corners.1), channel_id=1, source_target_pairs={{0,32},{4,36},{8,40},{12,44},{16,48},{20,52},{24,56},{28,60},{32,0... | collective-permute-start | bytes 393224 | tf_op jit(solution)/shard_map/ppermute | solution.py:451
  25.8 7.5 %collective-permute-start.12 = (f32[520,128]{1,0:T(8,128)S(1)}, f32[520,128]{1,0:T(8,128)S(1)}, u32[]{:S(2)}, u32[]{:S(2)}) collective-permute-start(f32[520,128]{1,0:T(8,128)S(1)} %get-tuple-element.36), channel_id=1, source_target_pairs={{0,32},{4,36},{8,40},{12,44},{16,48},{20,52},{24,56},{28,60},{32,0... | collective-permute-start | bytes 798728 | tf_op jit(solution)/shard_map/ppermute | solution.py:451
  28.3 9.3 %collective-permute-start.7 = (f32[264,128]{1,0:T(8,128)S(1)}, f32[264,128]{1,0:T(8,128)S(1)}, u32[]{:S(2)}, u32[]{:S(2)}) collective-permute-start(f32[264,128]{1,0:T(8,128)S(1)} %get-tuple-element.29), channel_id=1, source_target_pairs={{0,1},{1,2},{2,3},{3,0},{4,5},{5,6},{6,7},{7,4},{8,9},{9,10},{10,1... | collective-permute-start | bytes 405512 | tf_op jit(solution)/shard_map/ppermute | solution.py:464
  29.6 8.9 %collective-permute-start.8 = (f32[264,128]{1,0:T(8,128)S(1)}, f32[264,128]{1,0:T(8,128)S(1)}, u32[]{:S(2)}, u32[]{:S(2)}) collective-permute-start(f32[264,128]{1,0:T(8,128)S(1)} %get-tuple-element.30), channel_id=1, source_target_pairs={{0,2},{1,3},{2,0},{3,1},{4,6},{5,7},{6,4},{7,5},{8,10},{9,11},{10,... | collective-permute-start | bytes 405512 | tf_op jit(solution)/shard_map/ppermute | solution.py:464
  32.2 6.3 %collective-permute-start.9 = (f32[264,128]{1,0:T(8,128)S(1)}, f32[264,128]{1,0:T(8,128)S(1)}, u32[]{:S(2)}, u32[]{:S(2)}) collective-permute-start(f32[264,128]{1,0:T(8,128)S(1)} %get-tuple-element.31), channel_id=1, source_target_pairs={{0,3},{1,0},{2,1},{3,2},{4,7},{5,4},{6,5},{7,6},{8,11},{9,8},{10,9... | collective-permute-start | bytes 405512 | tf_op jit(solution)/shard_map/ppermute | solution.py:464
  34.1 11.3 %all-to-all-start = ((f32[16,40,128]{2,1,0:T(8,128)}), f32[16,40,128]{2,1,0:T(8,128)S(1)}, u32[]{:S(2)}, u32[]{:S(2)}) async-start(f32[16,40,128]{2,1,0:T(8,128)} %spread.1), calls=%async_computation | async-start | bytes 655360 | tf_op jit(solution)/shard_map/all_to_all | solution.py:532
  39.1 6.4 %collective-permute-start.10 = (f32[192,128]{1,0:T(8,128)S(1)}, f32[192,128]{1,0:T(8,128)S(1)}, u32[]{:S(2)}, u32[]{:S(2)}) collective-permute-start(f32[192,128]{1,0:T(8,128)S(1)} %get-tuple-element.32), channel_id=1, source_target_pairs={{0,4},{4,8},{8,12},{12,16},{16,20},{20,24},{24,28},{28,0},{32,36},... | collective-permute-start | bytes 294920 | tf_op jit(solution)/shard_map/ppermute | solution.py:451
  39.2 6.3 %collective-permute-start.11 = (f32[192,128]{1,0:T(8,128)S(1)}, f32[192,128]{1,0:T(8,128)S(1)}, u32[]{:S(2)}, u32[]{:S(2)}) collective-permute-start(f32[192,128]{1,0:T(8,128)S(1)} %get-tuple-element.33.after), channel_id=1, source_target_pairs={{0,28},{4,0},{8,4},{12,8},{16,12},{20,16},{24,20},{28,24},{32,60},... | collective-permute-start | bytes 294920 | tf_op jit(solution)/shard_map/ppermute | solution.py:451
  45.4 3.8 %collective-permute-start.15 = (f32[40,128]{1,0:T(8,128)S(1)}, f32[40,128]{1,0:T(8,128)S(1)}, u32[]{:S(2)}, u32[]{:S(2)}) collective-permute-start(f32[40,128]{1,0:T(8,128)S(1)} %sum.1.after.own), channel_id=1, source_target_pairs={{0,8},{4,12},{8,0},{12,4},{16,24},{20,28},{24,16},{28,20},{1,9},{5... | collective-permute-start | bytes 61448 | tf_op jit(solution)/shard_map/ppermute | solution.py:467
  45.6 5.4 %collective-permute-start.13 = (f32[2,64,128]{2,1,0:T(8,128)S(1)}, f32[2,64,128]{2,1,0:T(8,128)S(1)}, u32[]{:S(2)}, u32[]{:S(2)}) collective-permute-start(f32[2,64,128]{2,1,0:T(8,128)S(1)} %get-tuple-element.37.after), channel_id=1, source_target_pairs={{0,32},{4,36},{8,40},{12,44},{16,48},{20,52},{24,56},{28,60},{32,0... | collective-permute-start | bytes 196616 | tf_op jit(solution)/shard_map/ppermute | solution.py:451
  48.3 4.0 %collective-permute-start.14 = (f32[2,64,128]{2,1,0:T(8,128)S(1)}, f32[2,64,128]{2,1,0:T(8,128)S(1)}, u32[]{:S(2)}, u32[]{:S(2)}) collective-permute-start(f32[2,64,128]{2,1,0:T(8,128)S(1)} %get-tuple-element.38), channel_id=1, source_target_pairs={{0,224},{4,228},{8,232},{12,236},{16,240},{20,244},{24,248},{28,25... | collective-permute-start | bytes 196616 | tf_op jit(solution)/shard_map/ppermute | solution.py:451
  49.2 3.3 %collective-permute-start.19 = (f32[40,128]{1,0:T(8,128)S(1)}, f32[40,128]{1,0:T(8,128)S(1)}, u32[]{:S(2)}, u32[]{:S(2)}) collective-permute-start(f32[40,128]{1,0:T(8,128)S(1)} %pair.2.after.own), channel_id=1, source_target_pairs={{0,4},{4,0},{8,12},{12,8},{16,20},{20,16},{24,28},{28,24},{1,5},{5... | collective-permute-start | bytes 61448 | tf_op jit(solution)/shard_map/ppermute | solution.py:467
  52.6 5.8 %collective-permute-start.20 = (f32[40,128]{1,0:T(8,128)S(1)}, f32[40,128]{1,0:T(8,128)S(1)}, u32[]{:S(2)}, u32[]{:S(2)}) collective-permute-start(f32[40,128]{1,0:T(8,128)S(1)} %pair.3.own), channel_id=1, source_target_pairs={{0,28},{4,24},{8,20},{12,16},{16,12},{20,8},{24,4},{28,0},{1,29},{... | collective-permute-start | bytes 61448 | tf_op jit(solution)/shard_map/ppermute | solution.py:467
  54.4 19.1 %collective-permute-start.16 = (f32[256,256]{1,0:T(8,128)S(1)}, f32[256,256]{1,0:T(8,128)S(1)}, u32[]{:S(2)}, u32[]{:S(2)}) collective-permute-start(f32[256,256]{1,0:T(8,128)S(1)} %finish.1.after.one), channel_id=1, source_target_pairs={{0,2},{1,3},{2,0},{3,1},{4,6},{5,7},{6,4},{7,5},{8,10},{9,11},{10,... | collective-permute-start | bytes 786440 | tf_op jit(solution)/shard_map/ppermute | solution.py:464
  55.7 17.8 %collective-permute-start.17 = (f32[256,256]{1,0:T(8,128)S(1)}, f32[256,256]{1,0:T(8,128)S(1)}, u32[]{:S(2)}, u32[]{:S(2)}) collective-permute-start(f32[256,256]{1,0:T(8,128)S(1)} %finish.1.after.one), channel_id=1, source_target_pairs={{0,1},{1,2},{2,3},{3,0},{4,5},{5,6},{6,7},{7,4},{8,9},{9,10},{10,1... | collective-permute-start | bytes 786440 | tf_op jit(solution)/shard_map/ppermute | solution.py:464
  55.9 17.6 %collective-permute-start.18 = (f32[256,256]{1,0:T(8,128)S(1)}, f32[256,256]{1,0:T(8,128)S(1)}, u32[]{:S(2)}, u32[]{:S(2)}) collective-permute-start(f32[256,256]{1,0:T(8,128)S(1)} %finish.1.after.one), channel_id=1, source_target_pairs={{0,3},{1,0},{2,1},{3,2},{4,7},{5,4},{6,5},{7,6},{8,11},{9,8},{10,9... | collective-permute-start | bytes 786440 | tf_op jit(solution)/shard_map/ppermute | solution.py:464
  70.1 4.5 %collective-permute-start.21 = (f32[512,128]{1,0:T(8,128)S(1)}, f32[512,128]{1,0:T(8,128)S(1)}, u32[]{:S(2)}, u32[]{:S(2)}) collective-permute-start(f32[512,128]{1,0:T(8,128)S(1)} %bitcast.14), channel_id=1, source_target_pairs={{0,32},{4,36},{8,40},{12,44},{16,48},{20,52},{24,56},{28,60},{32,0... | collective-permute-start | bytes 786440 | tf_op jit(solution)/shard_map/ppermute | solution.py:451
  (1 other events, 1.2 us)

commit v8 on v6

--- a/solution.py
+++ b/solution.py
@@ -330,7 +330,12 @@
         spread[k] = mean
 
 
-def place_body(one, two, three, four, to_left, to_right, wide):
+def by_parity(right, left):
+    even = lax.rem(lax.axis_index("tx"), 2) == 0
+    return jnp.where(even, right, left), jnp.where(even, left, right)
+
+
+def place_body(one, two, three, four, first, second, wide):
     messages = (one, two, three, four)
     spots = []
     for message in messages:
@@ -353,14 +358,15 @@
     half = (TILE + 2 * HALF) // 2
     low = low_lanes(half)
     upper, lower = wide[2, :half], wide[2, half:]
-    to_right[...] = jnp.where(low, upper, swap(lower))
-    to_left[...] = jnp.where(low, swap(upper), lower)
-
-
-def rows_body(from_left, from_right, held, after, to_core, to_far, keep, wide):
+    right = jnp.where(low, upper, swap(lower))
+    left = jnp.where(low, swap(upper), lower)
+    first[...], second[...] = by_parity(right, left)
+
+
+def rows_body(first, second, held, after, to_core, to_far, keep, wide):
     half = (TILE + 2 * HALF) // 2
     low = low_lanes(half)
-    left, right = from_left[...], from_right[...]
+    right, left = by_parity(first[...], second[...])
     wide[0, :half] = held[0, :half] + jnp.where(low, left, 0.0)
     wide[0, half:] = held[0, half:] + jnp.where(low, swap(left), 0.0)
     wide[1, :half] = held[1, :half] + jnp.where(low, 0.0, swap(right))
@@ -455,6 +461,8 @@
 
     to_left = over_grid(lambda x, c, t: (x, c, t - 1))
     to_right = over_grid(lambda x, c, t: (x, c, t + 1))
+    to_first = over_grid(lambda x, c, t: (x, c, t ^ 1))
+    to_second = over_grid(lambda x, c, t: (x, c, t + 1 if t % 2 else t - 1))
     to_core = over_grid(lambda x, c, t: (x, 1 - c, t))
     to_far = over_grid(lambda x, c, t: (*across(x, c), t))
     far_left = over_grid(lambda x, c, t: (*across(x, c), t - 1))
@@ -531,7 +539,7 @@
     )
     chunks = lax.all_to_all(chunks, ("x", "scan"), 0, 0)
     tall = TILE + 2 * HALF
-    left, right, held = call(
+    first, second, held = call(
         place_body,
         [(tall // 2, W)] * 2 + [(3, tall, W)],
         (own, *arrived),
@@ -540,14 +548,14 @@
         flops=LONG,
     )
     (share,) = call(
-        sum_body, [(rows + 8, W)], (chunks, left), [VMEM, ANY], name="sum", flops=LONG
-    )
-    left, right = to_left(left), to_right(right)
+        sum_body, [(rows + 8, W)], (chunks, first), [VMEM, ANY], name="sum", flops=LONG
+    )
+    first, second = to_first(first), to_second(second)
     got = to_pair(share, 1)
     near, far, held = call(
         rows_body,
         [(2, HALF, W)] * 2 + [(2, TILE, W)],
-        (right, left, held, share),
+        (first, second, held, share),
         [VMEM] * 3 + [ANY],
         scratch=[pltpu.VMEM((2, tall, W), F32)],
         name="rows",

time: 76.3 us -> 75.8 us (level)
  waiting for transfers between devices: 7.28 us -> 9.3 us
  starting transfers between devices: 42.5 us -> 40.9 us
  blocking collectives: 11.7 us -> 10.9 us
    all_to_all x1, waiting for transfers between devices: 3.52 us -> 5.55 us  [per_device(): chunks = lax.all_to_all(chunks, ('x', 'scan'), 0, 0)]
    ppermute x6, starting transfers between devices: 10.1 us -> 9.22 us  [to_scan(): lax.ppermute(value, 'scan', [(s, (s + step) % nsc) for s in range(nsc)])]
    all_to_all x1, blocking collectives: 11.7 us -> 10.9 us  [per_device(): mine = lax.all_to_all(spread, ('x', 'scan'), 0, 0).reshape(MODES * W, W)]
  transfers between devices with their start and end apart: 23 -> 23, of which waited for: 7 -> 7; matrix products, arithmetic and copies ran while one was open for 0% -> 0% of each run, Pallas kernels for 4% -> 5%
where the time goes in v8:
time: 75.8 us; the launch traced here: 75.5 us
  starting transfers between devices  40.9 us (54%)
  Pallas kernels  11.1 us (15%)
  blocking collectives  10.9 us (14%)
  waiting for transfers between devices  9.3 us (12%)
  between operations  1.73 us (2%)
  local copies, waits for them, and re-layouts  1.45 us (2%)
    ppermute x13, starting transfers between devices, over_grid(): return lambda value: lax.ppermute(value, ('x', 'core', 'tx'), pairs)  24.1 us
    all_to_all x1, blocking collectives, per_device(): mine = lax.all_to_all(spread, ('x', 'scan'), 0, 0).reshape(MODES * W, W)  10.9 us
    pallas_call x15, Pallas kernels, call(): pl.pallas_call(body, out_shape=[jax.ShapeDtypeStruct(shape, F32) for shap...  9.29 us
    ppermute x6, starting transfers between devices, to_scan(): lax.ppermute(value, 'scan', [(s, (s + step) % nsc) for s in range(nsc)])  9.22 us
    all_to_all x1, waiting for transfers between devices, per_device(): chunks = lax.all_to_all(chunks, ('x', 'scan'), 0, 0)  5.55 us
    ppermute x3, starting transfers between devices, to_pair(): return lax.ppermute(value, 'tx', [(t, t ^ mask) for t in range(ntx)])  4.01 us
    all_to_all x1, starting transfers between devices, per_device(): chunks = lax.all_to_all(chunks, ('x', 'scan'), 0, 0)  3.54 us
    ppermute x13, waiting for transfers between devices, over_grid(): return lambda value: lax.ppermute(value, ('x', 'core', 'tx'), pairs)  2.34 us
  transfers between devices with their start and end apart: 23, of which 7 were waited for; matrix products, arithmetic and copies ran while one was open for 0% of the time, Pallas kernels for 5%

profile of v8, /device:TPU:1, one launch (start us, length us, event | category | flops | bytes accessed | tf_op | source)
XLA Modules:
  0.0 75.5 jit_solution(15601619901192224558)
XLA Ops:
  0.6 1.2 %copy-done = f32[2,2,256,256]{3,2,1,0:T(8,128)S(1)} copy-done((f32[2,2,256,256]{3,2,1,0:T(8,128)S(1)}, f32[2,2,256,256]{3,2,1,0:T(8,128)}, u32[]{:S(2)}) %copy-start) | copy-done | bytes 1048600
  2.0 2.5 %collective-permute-start.1 = (f32[4,128,128]{2,1,0:T(8,128)S(1)}, f32[4,128,128]{2,1,0:T(8,128)S(1)}, u32[]{:S(2)}, u32[]{:S(2)}) collective-permute-start(f32[4,128,128]{2,1,0:T(8,128)S(1)} %right.1.after), channel_id=1, source_target_pairs={{0,4},{4,8},{8,12},{12,16},{16,20},{20,24},{24,28},{28,0},{32,36},... | collective-permute-start | bytes 786440 | tf_op jit(solution)/shard_map/ppermute | solution.py:457
  4.7 4.0 %collective-permute-start = (f32[4,128,128]{2,1,0:T(8,128)S(1)}, f32[4,128,128]{2,1,0:T(8,128)S(1)}, u32[]{:S(2)}, u32[]{:S(2)}) collective-permute-start(f32[4,128,128]{2,1,0:T(8,128)S(1)} %left.1.after), channel_id=1, source_target_pairs={{0,28},{4,0},{8,4},{12,8},{16,12},{20,16},{24,20},{28,24},{32,60},... | collective-permute-start | bytes 786440 | tf_op jit(solution)/shard_map/ppermute | solution.py:457
  8.8 2.1 %collective-permute-start.3 = (f32[4,64,256]{2,1,0:T(8,128)S(1)}, f32[4,64,256]{2,1,0:T(8,128)S(1)}, u32[]{:S(2)}, u32[]{:S(2)}) collective-permute-start(f32[4,64,256]{2,1,0:T(8,128)S(1)} %get-tuple-element.23), channel_id=1, source_target_pairs={{0,224},{4,228},{8,232},{12,236},{16,240},{20,244},{24,248},{28,25... | collective-permute-start | bytes 786440 | tf_op jit(solution)/shard_map/ppermute | solution.py:457
  11.0 1.5 %collective-permute-start.4 = (f32[4,32,128]{2,1,0:T(8,128)S(1)}, f32[4,32,128]{2,1,0:T(8,128)S(1)}, u32[]{:S(2)}, u32[]{:S(2)}) collective-permute-start(f32[4,32,128]{2,1,0:T(8,128)S(1)} %get-tuple-element.24), channel_id=1, source_target_pairs={{0,252},{4,224},{8,228},{12,232},{16,236},{20,240},{24,244},{28,24... | collective-permute-start | bytes 196616 | tf_op jit(solution)/shard_map/ppermute | solution.py:457
  12.5 1.1 %collective-permute-start.5 = (f32[4,32,128]{2,1,0:T(8,128)S(1)}, f32[4,32,128]{2,1,0:T(8,128)S(1)}, u32[]{:S(2)}, u32[]{:S(2)}) collective-permute-start(f32[4,32,128]{2,1,0:T(8,128)S(1)} %get-tuple-element.25), channel_id=1, source_target_pairs={{0,228},{4,232},{8,236},{12,240},{16,244},{20,248},{24,252},{28,22... | collective-permute-start | bytes 196616 | tf_op jit(solution)/shard_map/ppermute | solution.py:457
  14.0 0.4 phase.2
  15.1 2.1 %collective-permute-start.2 = (f32[4,64,256]{2,1,0:T(8,128)S(1)}, f32[4,64,256]{2,1,0:T(8,128)S(1)}, u32[]{:S(2)}, u32[]{:S(2)}) collective-permute-start(f32[4,64,256]{2,1,0:T(8,128)S(1)} %get-tuple-element.22), channel_id=1, source_target_pairs={{0,32},{4,36},{8,40},{12,44},{16,48},{20,52},{24,56},{28,60},{32,0... | collective-permute-start | bytes 786440 | tf_op jit(solution)/shard_map/ppermute | solution.py:457
  17.6 0.7 collective-permute-done.5.left.far_left
  18.4 0.5 collective-permute-done.6.corners
  18.9 6.9 %slots.1 = (f32[264,128]{1,0:T(8,128)S(1)}, f32[264,128]{1,0:T(8,128)S(1)}, f32[264,128]{1,0:T(8,128)S(1)}, f32[264,128]{1,0:T(8,128)S(1)}, f32[520,128]{1,0:T(8,128)S(1)}, /*index=5*/f32[520,128]{1,0:T(8,128)S(1)}) custom-call(s32[4]{0:T(128)S(1)} %reshape.62.starts, s32[1,1,1]{2,1,0:T(1,128)S(6)} %copy.15.live_counts, f32[4,256,256]{2,1,0:T(8,128)S(1)} %bitcast.12, ...), custom_call_target="tpu_custom_call" | custom-call | tf_op jit(solution)/shard_map/slots/pallas_call | solution.py:28
  25.8 2.5 %collective-permute-start.12 = (f32[520,128]{1,0:T(8,128)S(1)}, f32[520,128]{1,0:T(8,128)S(1)}, u32[]{:S(2)}, u32[]{:S(2)}) collective-permute-start(f32[520,128]{1,0:T(8,128)S(1)} %get-tuple-element.36), channel_id=1, source_target_pairs={{0,32},{4,36},{8,40},{12,44},{16,48},{20,52},{24,56},{28,60},{32,0... | collective-permute-start | bytes 798728 | tf_op jit(solution)/shard_map/ppermute | solution.py:457
  28.3 1.3 %collective-permute-start.7 = (f32[264,128]{1,0:T(8,128)S(1)}, f32[264,128]{1,0:T(8,128)S(1)}, u32[]{:S(2)}, u32[]{:S(2)}) collective-permute-start(f32[264,128]{1,0:T(8,128)S(1)} %get-tuple-element.29), channel_id=1, source_target_pairs={{0,1},{1,2},{2,3},{3,0},{4,5},{5,6},{6,7},{7,4},{8,9},{9,10},{10,1... | collective-permute-start | bytes 405512 | tf_op jit(solution)/shard_map/ppermute | solution.py:472
  29.6 2.6 %collective-permute-start.8 = (f32[264,128]{1,0:T(8,128)S(1)}, f32[264,128]{1,0:T(8,128)S(1)}, u32[]{:S(2)}, u32[]{:S(2)}) collective-permute-start(f32[264,128]{1,0:T(8,128)S(1)} %get-tuple-element.30), channel_id=1, source_target_pairs={{0,2},{1,3},{2,0},{3,1},{4,6},{5,7},{6,4},{7,5},{8,10},{9,11},{10,... | collective-permute-start | bytes 405512 | tf_op jit(solution)/shard_map/ppermute | solution.py:472
  32.2 1.1 %collective-permute-start.9 = (f32[264,128]{1,0:T(8,128)S(1)}, f32[264,128]{1,0:T(8,128)S(1)}, u32[]{:S(2)}, u32[]{:S(2)}) collective-permute-start(f32[264,128]{1,0:T(8,128)S(1)} %get-tuple-element.31), channel_id=1, source_target_pairs={{0,3},{1,0},{2,1},{3,2},{4,7},{5,4},{6,5},{7,6},{8,11},{9,8},{10,9... | collective-permute-start | bytes 405512 | tf_op jit(solution)/shard_map/ppermute | solution.py:472
  33.3 0.8 %spread.1 = f32[16,40,128]{2,1,0:T(8,128)} custom-call(f32[520,128]{1,0:T(8,128)S(1)} %get-tuple-element.35.keep, f32[520,128]{1,0:T(8,128)S(1)} %collective-permute-done.12.got), custom_call_target="tpu_custom_call" | custom-call | flops 10000000000 | tf_op jit(solution)/shard_map/spread/pallas_call | solution.py:28
  34.1 3.5 %all-to-all-start = ((f32[16,40,128]{2,1,0:T(8,128)}), f32[16,40,128]{2,1,0:T(8,128)S(1)}, u32[]{:S(2)}, u32[]{:S(2)}) async-start(f32[16,40,128]{2,1,0:T(8,128)} %spread.1), calls=%async_computation | async-start | bytes 655360 | tf_op jit(solution)/shard_map/all_to_all | solution.py:540
  37.6 0.9 %collective-permute-done.8.three = f32[264,128]{1,0:T(8,128)S(1)} collective-permute-done((f32[264,128]{1,0:T(8,128)S(1)}, f32[264,128]{1,0:T(8,128)S(1)}, u32[]{:S(2)}, u32[]{:S(2)}) %collective-permute-start.8) | collective-permute-done | bytes 135200 | tf_op jit(solution)/shard_map/ppermute | solution.py:472
  38.6 0.5 place.1
  39.2 0.6 collective-permute-start.11
  39.8 5.6 %all-to-all-done.chunks = f32[16,40,128]{2,1,0:T(8,128)S(1)} async-done(((f32[16,40,128]{2,1,0:T(8,128)}), f32[16,40,128]{2,1,0:T(8,128)S(1)}, u32[]{:S(2)}, u32[]{:S(2)}) %all-to-all-start) | async-done | bytes 327712 | tf_op jit(solution)/shard_map/all_to_all | solution.py:540
  45.7 2.4 %collective-permute-start.13 = (f32[2,64,128]{2,1,0:T(8,128)S(1)}, f32[2,64,128]{2,1,0:T(8,128)S(1)}, u32[]{:S(2)}, u32[]{:S(2)}) collective-permute-start(f32[2,64,128]{2,1,0:T(8,128)S(1)} %get-tuple-element.37.after), channel_id=1, source_target_pairs={{0,32},{4,36},{8,40},{12,44},{16,48},{20,52},{24,56},{28,60},{32,0... | collective-permute-start | bytes 196616 | tf_op jit(solution)/shard_map/ppermute | solution.py:457
  48.1 3.0 %collective-permute-start.19 = (f32[40,128]{1,0:T(8,128)S(1)}, f32[40,128]{1,0:T(8,128)S(1)}, u32[]{:S(2)}, u32[]{:S(2)}) collective-permute-start(f32[40,128]{1,0:T(8,128)S(1)} %pair.2.after.own), channel_id=1, source_target_pairs={{0,8},{4,12},{8,0},{12,4},{16,24},{20,28},{24,16},{28,20},{1,9},{5... | collective-permute-start | bytes 61448 | tf_op jit(solution)/shard_map/ppermute | solution.py:475
  51.1 1.0 %collective-permute-done.14.from_far = f32[2,64,128]{2,1,0:T(8,128)S(1)} collective-permute-done((f32[2,64,128]{2,1,0:T(8,128)S(1)}, f32[2,64,128]{2,1,0:T(8,128)S(1)}, u32[]{:S(2)}, u32[]{:S(2)}) %collective-permute-start.14) | collective-permute-done | bytes 65568 | tf_op jit(solution)/shard_map/ppermute | solution.py:457
  52.1 0.4 collective-permute-done.19.got
  52.6 0.9 %collective-permute-start.20 = (f32[40,128]{1,0:T(8,128)S(1)}, f32[40,128]{1,0:T(8,128)S(1)}, u32[]{:S(2)}, u32[]{:S(2)}) collective-permute-start(f32[40,128]{1,0:T(8,128)S(1)} %pair.3.own), channel_id=1, source_target_pairs={{0,28},{4,24},{8,20},{12,16},{16,12},{20,8},{24,4},{28,0},{1,29},{... | collective-permute-start | bytes 61448 | tf_op jit(solution)/shard_map/ppermute | solution.py:475
  53.5 1.6 %collective-permute-start.16 = (f32[256,256]{1,0:T(8,128)S(1)}, f32[256,256]{1,0:T(8,128)S(1)}, u32[]{:S(2)}, u32[]{:S(2)}) collective-permute-start(f32[256,256]{1,0:T(8,128)S(1)} %finish.1.after.one), channel_id=1, source_target_pairs={{0,2},{1,3},{2,0},{3,1},{4,6},{5,7},{6,4},{7,5},{8,10},{9,11},{10,... | collective-permute-start | bytes 786440 | tf_op jit(solution)/shard_map/ppermute | solution.py:472
  55.3 2.5 %collective-permute-start.18 = (f32[256,256]{1,0:T(8,128)S(1)}, f32[256,256]{1,0:T(8,128)S(1)}, u32[]{:S(2)}, u32[]{:S(2)}) collective-permute-start(f32[256,256]{1,0:T(8,128)S(1)} %finish.1.after.one), channel_id=1, source_target_pairs={{0,3},{1,0},{2,1},{3,2},{4,7},{5,4},{6,5},{7,6},{8,11},{9,8},{10,9... | collective-permute-start | bytes 786440 | tf_op jit(solution)/shard_map/ppermute | solution.py:472
  57.8 10.9 %all_to_all.10 = f32[16,32,128]{2,1,0:T(8,128)S(1)} all-to-all(f32[16,32,128]{2,1,0:T(8,128)S(1)} %mean.1), channel_id=1, replica_groups=mesh['x'=4,'core'=2,'tx'=8,'scan'=4] {'x','scan'}, dimensions={0} | all-to-all | bytes 524288 | tf_op jit(solution)/shard_map/all_to_all | solution.py:590
  68.7 4.8 %collective-permute-start.21 = (f32[512,128]{1,0:T(8,128)S(1)}, f32[512,128]{1,0:T(8,128)S(1)}, u32[]{:S(2)}, u32[]{:S(2)}) collective-permute-start(f32[512,128]{1,0:T(8,128)S(1)} %bitcast.14), channel_id=1, source_target_pairs={{0,32},{4,36},{8,40},{12,44},{16,48},{20,52},{24,56},{28,60},{32,0... | collective-permute-start | bytes 786440 | tf_op jit(solution)/shard_map/ppermute | solution.py:457
  73.5 1.1 %gather.1 = (f32[4,256,256]{2,1,0:T(8,128)}, f32[2,512,128]{2,1,0:T(8,128)}) custom-call(f32[256,256]{1,0:T(8,128)S(1)} %finish.1.after.one, f32[256,256]{1,0:T(8,128)S(1)} %collective-permute-done.16.two, f32[256,256]{1,0:T(8,128)S(1)} %collective-permute-done.17.three, f32[256,256]{1,0:T(8,128)S(1)} %collective-permute-done.18.four, f32[512,128]{1,0:T(8,128)S(1)} %bitcast.15), custom_call_target="tpu_custom_call" | custom-call | flops 10000000000 | tf_op jit(solution)/shard_map/gather/pallas_call | solution.py:402
  74.7 0.7 other.1
  (57 shorter events, 1.8 us)
Async XLA Ops:
  2.0 15.2 %collective-permute-start.1 = (f32[4,128,128]{2,1,0:T(8,128)S(1)}, f32[4,128,128]{2,1,0:T(8,128)S(1)}, u32[]{:S(2)}, u32[]{:S(2)}) collective-permute-start(f32[4,128,128]{2,1,0:T(8,128)S(1)} %right.1.after), channel_id=1, source_target_pairs={{0,4},{4,8},{8,12},{12,16},{16,20},{20,24},{24,28},{28,0},{32,36},... | collective-permute-start | bytes 786440 | tf_op jit(solution)/shard_map/ppermute | solution.py:457
  4.7 10.4 %collective-permute-start = (f32[4,128,128]{2,1,0:T(8,128)S(1)}, f32[4,128,128]{2,1,0:T(8,128)S(1)}, u32[]{:S(2)}, u32[]{:S(2)}) collective-permute-start(f32[4,128,128]{2,1,0:T(8,128)S(1)} %left.1.after), channel_id=1, source_target_pairs={{0,28},{4,0},{8,4},{12,8},{16,12},{20,16},{24,20},{28,24},{32,60},... | collective-permute-start | bytes 786440 | tf_op jit(solution)/shard_map/ppermute | solution.py:457
  8.7 5.3 %copy-start.8 = (f32[128,128]{1,0:T(8,128)S(1)}, f32[128,128]{1,0:T(8,128)}, u32[]{:S(2)}) copy-start(f32[128,128]{1,0:T(8,128)} %phase.3) | copy-start | bytes 196612
  8.8 9.5 %collective-permute-start.3 = (f32[4,64,256]{2,1,0:T(8,128)S(1)}, f32[4,64,256]{2,1,0:T(8,128)S(1)}, u32[]{:S(2)}, u32[]{:S(2)}) collective-permute-start(f32[4,64,256]{2,1,0:T(8,128)S(1)} %get-tuple-element.23), channel_id=1, source_target_pairs={{0,224},{4,228},{8,232},{12,236},{16,240},{20,244},{24,248},{28,25... | collective-permute-start | bytes 786440 | tf_op jit(solution)/shard_map/ppermute | solution.py:457
  11.0 2.6 %copy-start.9 = (s32[1,1,2,2]{3,2,1,0:T(2,128)S(1)}, s32[1,1,2,2]{3,2,1,0:T(2,128)}, u32[]{:S(2)}) copy-start(s32[1,1,2,2]{3,2,1,0:T(2,128)} %param.13) | copy-start | bytes 52
  11.0 6.6 %collective-permute-start.4 = (f32[4,32,128]{2,1,0:T(8,128)S(1)}, f32[4,32,128]{2,1,0:T(8,128)S(1)}, u32[]{:S(2)}, u32[]{:S(2)}) collective-permute-start(f32[4,32,128]{2,1,0:T(8,128)S(1)} %get-tuple-element.24), channel_id=1, source_target_pairs={{0,252},{4,224},{8,228},{12,232},{16,236},{20,240},{24,244},{28,24... | collective-permute-start | bytes 196616 | tf_op jit(solution)/shard_map/ppermute | solution.py:457
  12.5 5.8 %collective-permute-start.5 = (f32[4,32,128]{2,1,0:T(8,128)S(1)}, f32[4,32,128]{2,1,0:T(8,128)S(1)}, u32[]{:S(2)}, u32[]{:S(2)}) collective-permute-start(f32[4,32,128]{2,1,0:T(8,128)S(1)} %get-tuple-element.25), channel_id=1, source_target_pairs={{0,228},{4,232},{8,236},{12,240},{16,244},{20,248},{24,252},{28,22... | collective-permute-start | bytes 196616 | tf_op jit(solution)/shard_map/ppermute | solution.py:457
  15.1 3.3 %collective-permute-start.2 = (f32[4,64,256]{2,1,0:T(8,128)S(1)}, f32[4,64,256]{2,1,0:T(8,128)S(1)}, u32[]{:S(2)}, u32[]{:S(2)}) collective-permute-start(f32[4,64,256]{2,1,0:T(8,128)S(1)} %get-tuple-element.22), channel_id=1, source_target_pairs={{0,32},{4,36},{8,40},{12,44},{16,48},{20,52},{24,56},{28,60},{32,0... | collective-permute-start | bytes 786440 | tf_op jit(solution)/shard_map/ppermute | solution.py:457
  17.4 1.5 %copy-start.1 = (f32[2,2,256,256]{3,2,1,0:T(8,128)S(1)}, f32[2,2,256,256]{3,2,1,0:T(8,128)}, u32[]{:S(2)}) copy-start(f32[2,2,256,256]{3,2,1,0:T(8,128)} %param.10) | copy-start | bytes 3145732
  17.4 1.5 %copy-start.2 = (f32[4,2,128,128]{3,2,1,0:T(8,128)S(1)}, f32[4,2,128,128]{3,2,1,0:T(8,128)}, u32[]{:S(2)}) copy-start(f32[4,2,128,128]{3,2,1,0:T(8,128)} %param.11) | copy-start | bytes 1572868
  17.4 1.5 %copy-start.3 = (f32[1,1,2,128,128]{4,3,2,1,0:T(8,128)S(1)}, f32[1,1,2,128,128]{4,3,2,1,0:T(8,128)}, u32[]{:S(2)}) copy-start(f32[1,1,2,128,128]{4,3,2,1,0:T(8,128)} %param.15) | copy-start | bytes 393220
  17.4 1.5 %copy-start.4 = (bf16[256,256]{1,0:T(8,128)(2,1)S(1)}, bf16[256,256]{1,0:T(8,128)(2,1)}, u32[]{:S(2)}) copy-start(bf16[256,256]{1,0:T(8,128)(2,1)} %constant.22.clone.right_low) | copy-start | bytes 393220
  17.4 1.5 %copy-start.5 = (bf16[256,256]{1,0:T(8,128)(2,1)S(1)}, bf16[256,256]{1,0:T(8,128)(2,1)}, u32[]{:S(2)}) copy-start(bf16[256,256]{1,0:T(8,128)(2,1)} %constant.23.clone.left_high) | copy-start | bytes 393220
  17.4 1.5 %copy-start.6 = (bf16[256,256]{1,0:T(8,128)(2,1)S(1)}, bf16[256,256]{1,0:T(8,128)(2,1)}, u32[]{:S(2)}) copy-start(bf16[256,256]{1,0:T(8,128)(2,1)} %constant.24.clone.left_low) | copy-start | bytes 393220
  17.4 1.5 %copy-start.7 = (bf16[256,256]{1,0:T(8,128)(2,1)S(1)}, bf16[256,256]{1,0:T(8,128)(2,1)}, u32[]{:S(2)}) copy-start(bf16[256,256]{1,0:T(8,128)(2,1)} %constant.9.clone.right_high) | copy-start | bytes 393220
  17.5 1.4 %collective-permute-start.6 = (f32[4,64,128]{2,1,0:T(8,128)S(1)}, f32[4,64,128]{2,1,0:T(8,128)S(1)}, u32[]{:S(2)}, u32[]{:S(2)}) collective-permute-start(f32[4,64,128]{2,1,0:T(8,128)S(1)} %corners.1), channel_id=1, source_target_pairs={{0,32},{4,36},{8,40},{12,44},{16,48},{20,52},{24,56},{28,60},{32,0... | collective-permute-start | bytes 393224 | tf_op jit(solution)/shard_map/ppermute | solution.py:457
  25.8 7.5 %collective-permute-start.12 = (f32[520,128]{1,0:T(8,128)S(1)}, f32[520,128]{1,0:T(8,128)S(1)}, u32[]{:S(2)}, u32[]{:S(2)}) collective-permute-start(f32[520,128]{1,0:T(8,128)S(1)} %get-tuple-element.36), channel_id=1, source_target_pairs={{0,32},{4,36},{8,40},{12,44},{16,48},{20,52},{24,56},{28,60},{32,0... | collective-permute-start | bytes 798728 | tf_op jit(solution)/shard_map/ppermute | solution.py:457
  28.3 9.3 %collective-permute-start.7 = (f32[264,128]{1,0:T(8,128)S(1)}, f32[264,128]{1,0:T(8,128)S(1)}, u32[]{:S(2)}, u32[]{:S(2)}) collective-permute-start(f32[264,128]{1,0:T(8,128)S(1)} %get-tuple-element.29), channel_id=1, source_target_pairs={{0,1},{1,2},{2,3},{3,0},{4,5},{5,6},{6,7},{7,4},{8,9},{9,10},{10,1... | collective-permute-start | bytes 405512 | tf_op jit(solution)/shard_map/ppermute | solution.py:472
  29.6 9.0 %collective-permute-start.8 = (f32[264,128]{1,0:T(8,128)S(1)}, f32[264,128]{1,0:T(8,128)S(1)}, u32[]{:S(2)}, u32[]{:S(2)}) collective-permute-start(f32[264,128]{1,0:T(8,128)S(1)} %get-tuple-element.30), channel_id=1, source_target_pairs={{0,2},{1,3},{2,0},{3,1},{4,6},{5,7},{6,4},{7,5},{8,10},{9,11},{10,... | collective-permute-start | bytes 405512 | tf_op jit(solution)/shard_map/ppermute | solution.py:472
  32.2 6.3 %collective-permute-start.9 = (f32[264,128]{1,0:T(8,128)S(1)}, f32[264,128]{1,0:T(8,128)S(1)}, u32[]{:S(2)}, u32[]{:S(2)}) collective-permute-start(f32[264,128]{1,0:T(8,128)S(1)} %get-tuple-element.31), channel_id=1, source_target_pairs={{0,3},{1,0},{2,1},{3,2},{4,7},{5,4},{6,5},{7,6},{8,11},{9,8},{10,9... | collective-permute-start | bytes 405512 | tf_op jit(solution)/shard_map/ppermute | solution.py:472
  34.1 11.3 %all-to-all-start = ((f32[16,40,128]{2,1,0:T(8,128)}), f32[16,40,128]{2,1,0:T(8,128)S(1)}, u32[]{:S(2)}, u32[]{:S(2)}) async-start(f32[16,40,128]{2,1,0:T(8,128)} %spread.1), calls=%async_computation | async-start | bytes 655360 | tf_op jit(solution)/shard_map/all_to_all | solution.py:540
  39.1 6.4 %collective-permute-start.10 = (f32[192,128]{1,0:T(8,128)S(1)}, f32[192,128]{1,0:T(8,128)S(1)}, u32[]{:S(2)}, u32[]{:S(2)}) collective-permute-start(f32[192,128]{1,0:T(8,128)S(1)} %get-tuple-element.32.after), channel_id=1, source_target_pairs={{0,4},{4,0},{8,12},{12,8},{16,20},{20,16},{24,28},{28,24},{32,36},... | collective-permute-start | bytes 294920 | tf_op jit(solution)/shard_map/ppermute | solution.py:457
  39.2 6.3 %collective-permute-start.11 = (f32[192,128]{1,0:T(8,128)S(1)}, f32[192,128]{1,0:T(8,128)S(1)}, u32[]{:S(2)}, u32[]{:S(2)}) collective-permute-start(f32[192,128]{1,0:T(8,128)S(1)} %get-tuple-element.33), channel_id=1, source_target_pairs={{0,28},{4,8},{8,4},{12,16},{16,12},{20,24},{24,20},{28,0},{32,60},... | collective-permute-start | bytes 294920 | tf_op jit(solution)/shard_map/ppermute | solution.py:457
  45.4 2.7 %collective-permute-start.15 = (f32[40,128]{1,0:T(8,128)S(1)}, f32[40,128]{1,0:T(8,128)S(1)}, u32[]{:S(2)}, u32[]{:S(2)}) collective-permute-start(f32[40,128]{1,0:T(8,128)S(1)} %sum.1.after.own), channel_id=1, source_target_pairs={{0,4},{4,0},{8,12},{12,8},{16,20},{20,16},{24,28},{28,24},{1,5},{5... | collective-permute-start | bytes 61448 | tf_op jit(solution)/shard_map/ppermute | solution.py:475
  45.7 5.5 %collective-permute-start.13 = (f32[2,64,128]{2,1,0:T(8,128)S(1)}, f32[2,64,128]{2,1,0:T(8,128)S(1)}, u32[]{:S(2)}, u32[]{:S(2)}) collective-permute-start(f32[2,64,128]{2,1,0:T(8,128)S(1)} %get-tuple-element.37.after), channel_id=1, source_target_pairs={{0,32},{4,36},{8,40},{12,44},{16,48},{20,52},{24,56},{28,60},{32,0... | collective-permute-start | bytes 196616 | tf_op jit(solution)/shard_map/ppermute | solution.py:457
  48.1 4.0 %collective-permute-start.14 = (f32[2,64,128]{2,1,0:T(8,128)S(1)}, f32[2,64,128]{2,1,0:T(8,128)S(1)}, u32[]{:S(2)}, u32[]{:S(2)}) collective-permute-start(f32[2,64,128]{2,1,0:T(8,128)S(1)} %get-tuple-element.38), channel_id=1, source_target_pairs={{0,224},{4,228},{8,232},{12,236},{16,240},{20,244},{24,248},{28,25... | collective-permute-start | bytes 196616 | tf_op jit(solution)/shard_map/ppermute | solution.py:457
  48.1 4.5 %collective-permute-start.19 = (f32[40,128]{1,0:T(8,128)S(1)}, f32[40,128]{1,0:T(8,128)S(1)}, u32[]{:S(2)}, u32[]{:S(2)}) collective-permute-start(f32[40,128]{1,0:T(8,128)S(1)} %pair.2.after.own), channel_id=1, source_target_pairs={{0,8},{4,12},{8,0},{12,4},{16,24},{20,28},{24,16},{28,20},{1,9},{5... | collective-permute-start | bytes 61448 | tf_op jit(solution)/shard_map/ppermute | solution.py:475
  52.6 5.2 %collective-permute-start.20 = (f32[40,128]{1,0:T(8,128)S(1)}, f32[40,128]{1,0:T(8,128)S(1)}, u32[]{:S(2)}, u32[]{:S(2)}) collective-permute-start(f32[40,128]{1,0:T(8,128)S(1)} %pair.3.own), channel_id=1, source_target_pairs={{0,28},{4,24},{8,20},{12,16},{16,12},{20,8},{24,4},{28,0},{1,29},{... | collective-permute-start | bytes 61448 | tf_op jit(solution)/shard_map/ppermute | solution.py:475
  53.5 20.0 %collective-permute-start.16 = (f32[256,256]{1,0:T(8,128)S(1)}, f32[256,256]{1,0:T(8,128)S(1)}, u32[]{:S(2)}, u32[]{:S(2)}) collective-permute-start(f32[256,256]{1,0:T(8,128)S(1)} %finish.1.after.one), channel_id=1, source_target_pairs={{0,2},{1,3},{2,0},{3,1},{4,6},{5,7},{6,4},{7,5},{8,10},{9,11},{10,... | collective-permute-start | bytes 786440 | tf_op jit(solution)/shard_map/ppermute | solution.py:472
  55.1 18.4 %collective-permute-start.17 = (f32[256,256]{1,0:T(8,128)S(1)}, f32[256,256]{1,0:T(8,128)S(1)}, u32[]{:S(2)}, u32[]{:S(2)}) collective-permute-start(f32[256,256]{1,0:T(8,128)S(1)} %finish.1.after.one), channel_id=1, source_target_pairs={{0,1},{1,2},{2,3},{3,0},{4,5},{5,6},{6,7},{7,4},{8,9},{9,10},{10,1... | collective-permute-start | bytes 786440 | tf_op jit(solution)/shard_map/ppermute | solution.py:472
  55.3 18.2 %collective-permute-start.18 = (f32[256,256]{1,0:T(8,128)S(1)}, f32[256,256]{1,0:T(8,128)S(1)}, u32[]{:S(2)}, u32[]{:S(2)}) collective-permute-start(f32[256,256]{1,0:T(8,128)S(1)} %finish.1.after.one), channel_id=1, source_target_pairs={{0,3},{1,0},{2,1},{3,2},{4,7},{5,4},{6,5},{7,6},{8,11},{9,8},{10,9... | collective-permute-start | bytes 786440 | tf_op jit(solution)/shard_map/ppermute | solution.py:472
  68.7 6.0 %collective-permute-start.21 = (f32[512,128]{1,0:T(8,128)S(1)}, f32[512,128]{1,0:T(8,128)S(1)}, u32[]{:S(2)}, u32[]{:S(2)}) collective-permute-start(f32[512,128]{1,0:T(8,128)S(1)} %bitcast.14), channel_id=1, source_target_pairs={{0,32},{4,36},{8,40},{12,44},{16,48},{20,52},{24,56},{28,60},{32,0... | collective-permute-start | bytes 786440 | tf_op jit(solution)/shard_map/ppermute | solution.py:457
  (1 other events, 1.2 us)
